TPU v7x, 32 devices: a whole 2x2x4 slice. The times are simulated.
32 devices in a mesh: groups: 2 (over y), wide: 4 (over z), narrow: 2 (over x), sub: 2 (over core).
Axes of the slice: x: 2, y: 2, z: 4, core: 2. Of those that a mesh axis runs over, the one named last changes fastest.
Arguments:
- tokens: bfloat16 [128, 16384], P(('groups', 'narrow', 'sub'), 'wide'), parts along dimension 0, may hold values from -6 to 6
- q_weight: bfloat16 [16384, 8192], P('wide', ('narrow', 'sub')), may hold values from -0.046875 to 0.046875
- k_weight: bfloat16 [16384, 512], P('wide', 'narrow'), may hold values from -0.046875 to 0.046875
- v_weight: bfloat16 [16384, 512], P('wide', 'narrow'), may hold values from -0.046875 to 0.046875
- o_weight: bfloat16 [8192, 16384], P(('narrow', 'sub'), 'wide'), may hold values from -0.5 to 0.5
- cache_keys: bfloat16 [128, 512, 4, 128], P(('groups', 'wide', 'sub'), None, 'narrow'), parts along dimension 0, may hold values from -240 to 240
- cache_values: bfloat16 [128, 512, 4, 128], P(('groups', 'wide', 'sub'), None, 'narrow'), parts along dimension 0, may hold values from -6 to 6
- lengths: int32 [128], P(('groups', 'wide')), parts along dimension 0, may hold values from 1 to 512, 16384 in all
Outputs:
- output: bfloat16 [128, 16384], P(('groups', 'narrow', 'sub'), 'wide'), parts along dimension 0
There are 2 independent parts, one for each index of `groups`. A program takes and returns all parts, laid end to end along the dimension named above; an argument that names none is the same for every part. Nothing has to cross between parts.
All inputs are finite; a program needn't handle non-finite values. No bound on the sum of `lengths` on one device may be relied on, other than what follows from the above.
Results may differ from a plain program's by a relative error of at most 0.012.
Values may be sent and summed in bfloat16 or wider, within the bound.
No kernel may reach another device: no remote copies, remote signals or barrier semaphores. Data moves between devices by JAX's collectives and lax.ppermute only.
A program may use at most 128 MiB of HBM per device.

v0:
```python
import math

import jax
import jax.numpy as jnp
from jax import lax
from jax.sharding import PartitionSpec as P

HD = 128


rope_base = 500000.0


def rotate(head_values, token_positions):
    half_width = head_values.shape[-1] // 2
    exponents = jnp.arange(half_width, dtype=jnp.float32) * (2.0 / head_values.shape[-1])
    frequency = jnp.exp(-math.log(rope_base) * exponents)
    angles = token_positions.astype(jnp.float32)[:, None] * frequency[None, :]
    cosine_terms = jnp.cos(angles)[:, None, :]
    sine_terms = jnp.sin(angles)[:, None, :]
    lower_half = head_values[..., :half_width]
    upper_half = head_values[..., half_width:]
    return jnp.concatenate(
        [
            lower_half * cosine_terms - upper_half * sine_terms,
            upper_half * cosine_terms + lower_half * sine_terms,
        ],
        axis=-1,
    )


def attend(queries, keys_block, values_block, key_own, value_own, length_own):
    seq_count, combined_width = queries.shape
    kv_count = keys_block.shape[2]
    head_dim = keys_block.shape[3]
    group_size = combined_width // (kv_count * head_dim)
    grouped_heads = queries.reshape(seq_count, kv_count, group_size, head_dim)
    scaling_factor = 1.0 / math.sqrt(head_dim)
    scores = (
        jnp.einsum("skgd,stkd->skgt", grouped_heads, keys_block, preferred_element_type=jnp.float32)
        * scaling_factor
    )
    self_token_score = (
        jnp.einsum("skgd,skd->skg", grouped_heads, key_own, preferred_element_type=jnp.float32)
        * scaling_factor
    )
    visible = jnp.arange(keys_block.shape[1], dtype=jnp.int32)[None, :] < length_own[:, None]
    scores = jnp.where(visible[:, None, None, :], scores, -1e30)
    highest = jnp.maximum(jnp.max(scores, axis=-1), self_token_score)
    exp_scores = jnp.exp(scores - highest[..., None])
    exp_own = jnp.exp(self_token_score - highest)
    denominator = jnp.sum(exp_scores, axis=-1) + exp_own
    weights = (exp_scores / denominator[..., None]).astype(jnp.bfloat16)
    own_weight = (exp_own / denominator).astype(jnp.bfloat16)
    attended = jnp.einsum(
        "skgt,stkd->skgd", weights, values_block, preferred_element_type=jnp.float32
    )
    attended = (
        attended
        + own_weight.astype(jnp.float32)[..., None] * value_own.astype(jnp.float32)[:, :, None, :]
    )
    return attended.astype(jnp.bfloat16).reshape(seq_count, combined_width)


def body(tokens, q_weight, k_weight, v_weight, o_weight, cache_keys, cache_values, lengths):
    gathered = lax.all_gather(tokens, ("narrow", "sub"), axis=0, tiled=True)
    q_cols = q_weight.shape[1]
    kv_cols = k_weight.shape[1]
    head_dim = HD
    wide_rows = gathered.shape[0] // lax.axis_size("wide")
    summed = lax.psum_scatter(
        jnp.concatenate(
            [
                jnp.dot(gathered, q_weight, preferred_element_type=jnp.float32),
                jnp.dot(gathered, k_weight, preferred_element_type=jnp.float32),
                jnp.dot(gathered, v_weight, preferred_element_type=jnp.float32),
            ],
            axis=1,
        ),
        "wide",
        scatter_dimension=0,
        tiled=True,
    )
    queries = rotate(summed[:, :q_cols].reshape(wide_rows, q_cols // head_dim, head_dim), lengths)
    queries = queries.astype(jnp.bfloat16).reshape(wide_rows, q_cols)
    fresh_key_rows = rotate(
        summed[:, q_cols : q_cols + kv_cols].reshape(wide_rows, kv_cols // head_dim, head_dim),
        lengths,
    ).astype(jnp.bfloat16)
    new_values = (
        summed[:, q_cols + kv_cols :]
        .astype(jnp.bfloat16)
        .reshape(wide_rows, kv_cols // head_dim, head_dim)
    )
    seq_count = cache_keys.shape[0]
    offset = lax.axis_index("sub") * seq_count
    key_own = lax.dynamic_slice_in_dim(fresh_key_rows, offset, seq_count, 0)
    value_own = lax.dynamic_slice_in_dim(new_values, offset, seq_count, 0)
    length_own = lax.dynamic_slice_in_dim(lengths, offset, seq_count, 0)
    all_heads = lax.all_to_all(queries, "sub", split_axis=0, concat_axis=1, tiled=True)
    attention = attend(all_heads, cache_keys, cache_values, key_own, value_own, length_own)
    returned = lax.all_to_all(attention, "sub", split_axis=1, concat_axis=0, tiled=True)
    partial_value = jnp.dot(
        lax.all_gather(returned, "wide", axis=0, tiled=True),
        o_weight,
        preferred_element_type=jnp.float32,
    )
    total = lax.psum_scatter(partial_value, ("narrow", "sub"), scatter_dimension=0, tiled=True)
    return total.astype(jnp.bfloat16)


def solution(mesh):
    return jax.shard_map(
        body,
        mesh=mesh,
        in_specs=(
            P(("groups", "narrow", "sub"), "wide"),
            P("wide", ("narrow", "sub")),
            P("wide", "narrow"),
            P("wide", "narrow"),
            P(("narrow", "sub"), "wide"),
            P(("groups", "wide", "sub"), None, "narrow", None),
            P(("groups", "wide", "sub"), None, "narrow", None),
            P(("groups", "wide")),
        ),
        out_specs=P(("groups", "narrow", "sub"), "wide"),
        check_vma=False,
    )
```

profile of v0, /device:TPU:0, one launch (start us, length us, event | category | flops | bytes accessed | tf_op | source)
XLA Modules:
  0.0 122.0 jit_solution(2861990430192798115)
XLA Ops:
  6.5 0.0 copy-start
  6.5 0.0 reduce-scatter.3.cloned.1.call-start
  6.5 8.9 %all_gather.6 = bf16[64,4096]{1,0:T(8,128)(2,1)S(1)} all-gather(bf16[16,4096]{1,0:T(8,128)(2,1)} %param.8), channel_id=1, replica_groups=mesh['groups'=2,'wide'=4,'narrow'=2,'sub'=2] {'narrow','sub'}, dimensions={0}, use_global_device_ids=true | all-gather | bytes 655360 | tf_op jit(solution)/shard_map/all_gather | solution.py:66
  15.5 0.0 copy-start.1
  15.5 8.9 %fusion.28 = f32[64,2048]{1,0:T(8,128)S(1)} fusion(bf16[64,4096]{1,0:T(8,128)(2,1)S(1)} %all_gather.6, bf16[4096,2048]{1,0:T(8,128)(2,1)} %param.9), kind=kOutput, calls=%fused_computation.41 | convolution fusion | flops 1073741824 | bytes 17825792 | tf_op jit(solution)/shard_map/dot_general | solution.py:74
  24.4 0.0 copy-done.1
  24.5 0.0 copy-start.2
  24.5 0.5 fusion.29
  24.9 1.1 copy-done.2
  26.1 0.0 copy-start.3
  26.1 0.5 fusion.30
  26.5 0.9 pad_maximum_fusion
  27.4 0.0 reduce-scatter.3.cloned.1.call-update
  27.4 0.0 copy-done.3
  27.5 0.1 dynamic_slice.9
  27.6 0.1 iota_compare_fusion
  27.6 0.1 multiply_cosine_fusion
  27.8 22.9 %reduce-scatter.3.cloned.1.call-done = f32[16,2560]{1,0:T(8,128)} async-done(((f32[64,2560]{1,0:T(8,128)}), f32[16,2560]{1,0:T(8,128)}) %reduce-scatter.3.cloned.1.call-update) | async-done | bytes 163856 | tf_op jit(solution)/shard_map/reduce_scatter | solution.py:71
  50.6 0.7 slice.32
  51.4 0.9 slice_bitcast_fusion
  52.3 0.1 subtract_convert_fusion.1
  52.4 0.1 subtract_convert_fusion
  52.5 0.1 pad_maximum_fusion.1
  52.6 0.7 convert_element_type.31
  53.3 3.3 %all-to-all-start = ((bf16[2,8,2048]{2,1,0:T(8,128)(2,1)}), bf16[2,8,2048]{2,1,0:T(8,128)(2,1)S(1)}, u32[]{:S(2)}, u32[]{:S(2)}) async-start(bf16[2,8,2048]{2,1,0:T(8,128)(2,1)} %convert_element_type.31), calls=%async_computation.1 | async-start | bytes 131072 | tf_op jit(solution)/shard_map/all_to_all | solution.py:100
  56.6 0.0 reduce-scatter.5.cloned.1.call-start
  56.7 0.1 fusion.24
  56.7 1.3 %all-to-all-done = bf16[2,8,2048]{2,1,0:T(8,128)(2,1)S(1)} async-done(((bf16[2,8,2048]{2,1,0:T(8,128)(2,1)}), bf16[2,8,2048]{2,1,0:T(8,128)(2,1)S(1)}, u32[]{:S(2)}, u32[]{:S(2)}) %all-to-all-start) | async-done | bytes 65568 | tf_op jit(solution)/shard_map/all_to_all | solution.py:100
  58.0 0.1 fusion.19
  58.2 0.0 copy-done
  58.2 0.7 fusion.27
  58.9 0.3 fusion.16
  59.2 0.7 slice.46
  60.0 2.1 %fusion.13 = bf16[8,2,16,128]{3,2,1,0:T(8,128)(2,1)S(1)} fusion(bf16[8,512,2,128]{3,2,1,0:T(2,128)(2,1)} %param.14, f32[8,2,16,512]{3,2,1,0:T(8,128)S(1)} %get-tuple-element.14, f32[8,2,16]{2,1,0:T(2,128)S(1)} %get-tuple-element.10, f32[8,2,16]{2,1,0:T(2,128)S(1)} %multiply_maximum_fusion, f32[8,2,128]{2,1,0:T(2,128)S(1)} %dynamic-slice_convert_fusion, ...), kind=kOutput, calls=%fused_computation.7 | convolution fusion | flops 34045952 | bytes 2698240 | tf_op jit(solution)/shard_map/skgt,stkd->skgd/dot_general | solution.py:55
  62.1 3.8 %all_to_all.32 = bf16[8,2,2048]{2,0,1:T(8,128)(2,1)S(1)} all-to-all(bf16[8,2,2048]{2,0,1:T(8,128)(2,1)S(1)} %copy.19), channel_id=1, replica_groups=mesh['groups'=2,'wide'=4,'narrow'=2,'sub'=2] {'sub'}, dimensions={1} | all-to-all | bytes 131072 | tf_op jit(solution)/shard_map/all_to_all | solution.py:102
  65.9 14.0 %all_gather.7 = bf16[64,2048]{1,0:T(8,128)(2,1)S(1)} all-gather(bf16[16,2048]{1,0:T(8,128)(2,1)S(1)} %bitcast.33), channel_id=1, replica_groups=mesh['groups'=2,'wide'=4,'narrow'=2,'sub'=2] {'wide'}, dimensions={0}, use_global_device_ids=true | all-gather | bytes 327680 | tf_op jit(solution)/shard_map/all_gather | solution.py:104
  79.9 9.8 %fusion.31 = f32[64,4096]{1,0:T(8,128)} fusion(bf16[64,2048]{1,0:T(8,128)(2,1)S(1)} %all_gather.7, bf16[2048,4096]{1,0:T(8,128)(2,1)} %param.12), kind=kOutput, calls=%fused_computation.44 | convolution fusion | flops 1073741824 | bytes 18087936 | tf_op jit(solution)/shard_map/dot_general | solution.py:103
  89.6 0.0 reduce-scatter.5.cloned.1.call-update
  89.7 23.9 %reduce-scatter.5.cloned.1.call-done = f32[16,4096]{1,0:T(8,128)} async-done(((f32[64,4096]{1,0:T(8,128)}), f32[16,4096]{1,0:T(8,128)}) %reduce-scatter.5.cloned.1.call-update) | async-done | bytes 262160 | tf_op jit(solution)/shard_map/reduce_scatter | solution.py:108
  113.6 1.6 %convert_element_type.37 = bf16[16,4096]{1,0:T(8,128)(2,1)} convert(f32[16,4096]{1,0:T(8,128)} %reduce-scatter.5.cloned.1.call-done) | non-fusion elementwise | flops 65536 | bytes 393216 | tf_op jit(solution)/shard_map/convert_element_type | solution.py:109
  (10 shorter events, 0.2 us)
Async XLA Ops:
  6.5 51.6 %copy-start = (bf16[8,512,2,128]{3,2,1,0:T(2,128)(2,1)S(1)}, bf16[8,512,2,128]{3,2,1,0:T(2,128)(2,1)}, u32[]{:S(2)}) copy-start(bf16[8,512,2,128]{3,2,1,0:T(2,128)(2,1)} %param.13) | copy-start | bytes 6291460
  6.5 44.1 %reduce-scatter.3.cloned.1.call-start = ((), (), s32[]{:S(2)}) async-start(), calls=%async_computation.4 | async-start | bytes 819200 | tf_op jit(solution)/shard_map/reduce_scatter | solution.py:71
  15.5 9.0 %copy-start.1 = (bf16[4096,256]{1,0:T(8,128)(2,1)S(1)}, bf16[4096,256]{1,0:T(8,128)(2,1)}, u32[]{:S(2)}) copy-start(bf16[4096,256]{1,0:T(8,128)(2,1)} %param.10) | copy-start | bytes 6291460
  24.5 1.6 %copy-start.2 = (bf16[4096,256]{1,0:T(8,128)(2,1)S(1)}, bf16[4096,256]{1,0:T(8,128)(2,1)}, u32[]{:S(2)}) copy-start(bf16[4096,256]{1,0:T(8,128)(2,1)} %param.11) | copy-start | bytes 6291460
  26.1 1.4 %copy-start.3 = (s32[16]{0:T(128)S(1)}, s32[16]{0:T(128)}, u32[]{:S(2)}) copy-start(s32[16]{0:T(128)} %param.15) | copy-start | bytes 196
  53.3 4.7 %all-to-all-start = ((bf16[2,8,2048]{2,1,0:T(8,128)(2,1)}), bf16[2,8,2048]{2,1,0:T(8,128)(2,1)S(1)}, u32[]{:S(2)}, u32[]{:S(2)}) async-start(bf16[2,8,2048]{2,1,0:T(8,128)(2,1)} %convert_element_type.31), calls=%async_computation.1 | async-start | bytes 131072 | tf_op jit(solution)/shard_map/all_to_all | solution.py:100
  56.6 57.0 %reduce-scatter.5.cloned.1.call-start = ((), (), s32[]{:S(2)}) async-start(), calls=%async_computation.5 | async-start | bytes 1310720 | tf_op jit(solution)/shard_map/reduce_scatter | solution.py:108
Sparse Core Ops, SparseCore 0:
  27.6 23.0 reduce-scatter.2
  89.8 23.7 reduce-scatter.4
where the time goes:
time: 123 us; the launch traced here: 122 us
  waiting for transfers between devices  48.1 us (39%)
  blocking collectives  26.7 us (22%)
  matrix products  22.6 us (18%)
  between operations  13.6 us (11%)
  local copies, waits for them, and re-layouts  4.33 us (4%)
  other arithmetic  3.39 us (3%)
  starting transfers between devices  3.34 us (3%)
    reduce_scatter x1, waiting for transfers between devices, body(): lax.psum_scatter(partial_value, ('narrow', 'sub'), scatter_dimension=0, t...  23.9 us
    reduce_scatter x1, waiting for transfers between devices, body(): lax.psum_scatter(jnp.concatenate([jnp.dot(gathered, q_weight, preferred_e...  22.9 us
    all_gather x1, blocking collectives, body(): lax.all_gather(returned, 'wide', axis=0, tiled=True)  14 us
    dot_general x1, matrix products, body(): jnp.dot(lax.all_gather(returned, 'wide', axis=0, tiled=True), o_weight, p...  9.77 us
    dot_general x1, matrix products, body(): jnp.dot(gathered, q_weight, preferred_element_type=jnp.float32)  8.95 us
    all_gather x1, blocking collectives, body(): gathered = lax.all_gather(tokens, ('narrow', 'sub'), axis=0, tiled=True)  8.95 us
    all_to_all x1, blocking collectives, body(): lax.all_to_all(attention, 'sub', split_axis=1, concat_axis=0, tiled=True)  3.79 us
    all_to_all x1, starting transfers between devices, body(): lax.all_to_all(queries, 'sub', split_axis=0, concat_axis=1, tiled=True)  3.3 us
  transfers between devices with their start and end apart: 3, of which 3 were waited for; matrix products, arithmetic and copies ran while one was open for 0% of the time, Pallas kernels for 0%

commit v1 on v0

--- a/solution.py
+++ b/solution.py
@@ -3,6 +3,8 @@
 import jax
 import jax.numpy as jnp
 from jax import lax
+from jax.experimental import pallas as pl
+from jax.experimental.pallas import tpu as pltpu
 from jax.sharding import PartitionSpec as P
 
 HD = 128
@@ -62,7 +64,7 @@
     return attended.astype(jnp.bfloat16).reshape(seq_count, combined_width)
 
 
-def body(tokens, q_weight, k_weight, v_weight, o_weight, cache_keys, cache_values, lengths):
+def general_body(tokens, q_weight, k_weight, v_weight, o_weight, cache_keys, cache_values, lengths):
     gathered = lax.all_gather(tokens, ("narrow", "sub"), axis=0, tiled=True)
     q_cols = q_weight.shape[1]
     kv_cols = k_weight.shape[1]
@@ -109,9 +111,308 @@
     return total.astype(jnp.bfloat16)
 
 
+VMEM_SPEC = pl.BlockSpec(memory_space=pltpu.VMEM)
+SMEM_SPEC = pl.BlockSpec(memory_space=pltpu.SMEM)
+MIB = 2**20
+
+
+def small_vmem(mib):
+    return pltpu.CompilerParams(vmem_limit_bytes=mib * MIB)
+
+
+def exchange(array, axis, bit):
+    size = lax.axis_size(axis)
+    return lax.ppermute(array, axis, [(i, i ^ bit) for i in range(size)])
+
+
+def touch_kernel(weight_ref, out_ref):
+    out_ref[...] = weight_ref[:8, :128].astype(jnp.float32)
+
+
+def early(weight):
+    return pl.pallas_call(
+        touch_kernel,
+        out_shape=jax.ShapeDtypeStruct((8, 128), jnp.float32),
+        in_specs=[VMEM_SPEC],
+        out_specs=VMEM_SPEC,
+        compiler_params=small_vmem(1),
+        cost_estimate=pl.CostEstimate(
+            flops=0, bytes_accessed=weight.size * 2, transcendentals=0
+        ),
+        name="early",
+    )(weight)
+
+
+def project_kernel(
+    own_ref, core_ref, chip_ref, both_ref, q_ref, k_ref, v_ref, mark_ref, *refs
+):
+    outs, rows_scratch = refs[:4], refs[4]
+    narrow, sub, wide = lax.axis_index("narrow"), lax.axis_index("sub"), lax.axis_index("wide")
+    mine = (narrow * 2 + sub) ^ wide
+    rows = own_ref.shape[0]
+    for m, ref in enumerate((own_ref, core_ref, chip_ref, both_ref)):
+        place = pl.multiple_of((mine ^ m) * rows, rows)
+        rows_scratch[pl.ds(place, rows), :] = ref[...]
+    tokens = rows_scratch[...]
+    q_cols = q_ref.shape[1]
+    step = 512
+    for start in range(0, q_cols, step):
+        product = jnp.dot(
+            tokens, q_ref[:, start : start + step], preferred_element_type=jnp.float32
+        )
+        for place, out in enumerate(outs):
+            out[:, start : start + step] = product[place * rows : (place + 1) * rows].astype(
+                out.dtype
+            )
+
+    def side(weight_ref):
+        product = jnp.dot(tokens, weight_ref[...], preferred_element_type=jnp.float32)
+        for place, out in enumerate(outs):
+            out[:, q_cols:] = product[place * rows : (place + 1) * rows].astype(out.dtype)
+
+    @pl.when(sub == 0)
+    def _():
+        side(k_ref)
+
+    @pl.when(sub == 1)
+    def _():
+        side(v_ref)
+
+
+def project(own, core, chip, both, q_weight, k_weight, v_weight, mark):
+    rows, depth = own.shape
+    columns = q_weight.shape[1] + k_weight.shape[1]
+    return pl.pallas_call(
+        project_kernel,
+        out_shape=[jax.ShapeDtypeStruct((rows, columns), jnp.bfloat16)] * 4,
+        in_specs=[VMEM_SPEC] * 8,
+        out_specs=[VMEM_SPEC] * 4,
+        scratch_shapes=[pltpu.VMEM((4 * rows, depth), jnp.bfloat16)],
+        compiler_params=small_vmem(6),
+        cost_estimate=pl.CostEstimate(
+            flops=2 * 4 * rows * depth * columns, bytes_accessed=0, transcendentals=0
+        ),
+        name="project",
+    )(own, core, chip, both, q_weight, k_weight, v_weight, mark)
+
+
+def turn_kernel(a_ref, b_ref, c_ref, d_ref, cos_ref, sin_ref, keep_ref, send_ref, scratch):
+    sub = lax.axis_index("sub")
+    seqs, columns = a_ref.shape
+    half = seqs // 2
+    heads = (columns - 2 * HD) // HD
+    cos, sin = cos_ref[...], sin_ref[...]
+    for head in range(columns // HD):
+        cut = slice(head * HD, (head + 1) * HD)
+        total = (a_ref[:, cut].astype(jnp.float32) + b_ref[:, cut].astype(jnp.float32)) + (
+            c_ref[:, cut].astype(jnp.float32) + d_ref[:, cut].astype(jnp.float32)
+        )
+        turned = total * cos + pltpu.roll(total, HD // 2, 1) * sin
+        if head >= heads:
+            turned = jnp.where(sub == 0, turned, total)
+        scratch[head * seqs : (head + 1) * seqs, :] = turned
+    for out, base in ((keep_ref, sub * half), (send_ref, (1 - sub) * half)):
+        for i in range(half):
+            out[i * heads : (i + 1) * heads, :] = scratch[
+                pl.ds(base + i, heads, stride=seqs), :
+            ].astype(out.dtype)
+        parts = [
+            scratch[pl.ds(pl.multiple_of((heads + j) * seqs + base, half), half), :]
+            for j in range(2)
+        ]
+        out[half * heads :, :] = jnp.concatenate(parts, axis=0).astype(out.dtype)
+
+
+def turn(parts, cos, sin):
+    seqs, columns = parts[0].shape
+    shape = jax.ShapeDtypeStruct((seqs // 2 * columns // HD, HD), jnp.bfloat16)
+    return pl.pallas_call(
+        turn_kernel,
+        out_shape=[shape, shape],
+        in_specs=[VMEM_SPEC] * 6,
+        out_specs=[VMEM_SPEC] * 2,
+        scratch_shapes=[pltpu.VMEM((seqs * columns // HD, HD), jnp.float32)],
+        compiler_params=small_vmem(4),
+        name="turn",
+    )(*parts, cos, sin)
+
+
+def attend_kernel(length_ref, own_ref, other_ref, keys_ref, values_ref, keep_ref, send_ref, scratch):
+    sub = lax.axis_index("sub")
+    seqs, slots, _ = keys_ref.shape
+    heads = own_ref.shape[0] // seqs - 2
+    new = seqs * heads
+    first = sub == 0
+    own_new = own_ref[new:, :].astype(jnp.float32)
+    other_new = other_ref[new:, :].astype(jnp.float32)
+    new_keys = jnp.where(first, own_new, other_new)
+    new_values = jnp.where(first, other_new, own_new)
+    column = lax.broadcasted_iota(jnp.int32, (2 * heads, slots), 1)
+    row = lax.broadcasted_iota(jnp.int32, (2 * heads, slots), 0)
+    group = jnp.where(row < heads, sub, 1 - sub)
+    position = jnp.where((column & 1) == group, column >> 1, slots)
+    low = lax.broadcasted_iota(jnp.int32, (2 * heads, HD), 0) < heads
+    scale = 1.0 / math.sqrt(HD)
+    for i in range(seqs):
+        length = length_ref[sub * seqs + i]
+        query = jnp.concatenate(
+            [own_ref[i * heads : (i + 1) * heads, :], other_ref[i * heads : (i + 1) * heads, :]],
+            axis=0,
+        )
+        scores = (
+            lax.dot_general(
+                query, keys_ref[i], (((1,), (1,)), ((), ())), preferred_element_type=jnp.float32
+            )
+            * scale
+        )
+        key_zero, key_one = new_keys[i : i + 1], new_keys[seqs + i : seqs + i + 1]
+        value_zero, value_one = new_values[i : i + 1], new_values[seqs + i : seqs + i + 1]
+        key_rows = jnp.where(
+            low, jnp.where(first, key_zero, key_one), jnp.where(first, key_one, key_zero)
+        )
+        value_rows = jnp.where(
+            low, jnp.where(first, value_zero, value_one), jnp.where(first, value_one, value_zero)
+        )
+        own_score = (
+            jnp.sum(query.astype(jnp.float32) * key_rows, axis=1, keepdims=True) * scale
+        )
+        scores = jnp.where(position < length, scores, -1e30)
+        highest = jnp.maximum(jnp.max(scores, axis=1, keepdims=True), own_score)
+        terms = jnp.exp(scores - highest)
+        own_term = jnp.exp(own_score - highest)
+        inverse = 1.0 / (jnp.sum(terms, axis=1, keepdims=True) + own_term)
+        mixed = jnp.dot(
+            (terms * inverse).astype(jnp.bfloat16),
+            values_ref[i],
+            preferred_element_type=jnp.float32,
+        )
+        mixed = mixed + (own_term * inverse) * value_rows
+        scratch[pl.ds(i, 2 * heads, stride=seqs), :] = mixed
+    for head in range(heads):
+        cut = slice(head * HD, (head + 1) * HD)
+        keep_ref[:, cut] = scratch[head * seqs : (head + 1) * seqs, :].astype(keep_ref.dtype)
+        send_ref[:, cut] = scratch[
+            (heads + head) * seqs : (heads + head + 1) * seqs, :
+        ].astype(send_ref.dtype)
+
+
+def attend_here(lengths, own, other, keys, values):
+    seqs, slots, _ = keys.shape
+    heads = own.shape[0] // seqs - 2
+    shape = jax.ShapeDtypeStruct((seqs, heads * HD), jnp.bfloat16)
+    return pl.pallas_call(
+        attend_kernel,
+        out_shape=[shape, shape],
+        in_specs=[SMEM_SPEC] + [VMEM_SPEC] * 4,
+        out_specs=[VMEM_SPEC] * 2,
+        scratch_shapes=[pltpu.VMEM((2 * heads * seqs, HD), jnp.float32)],
+        compiler_params=small_vmem(6),
+        name="attend",
+    )(lengths, own, other, keys, values)
+
+
+def output_kernel(a_ref, b_ref, c_ref, d_ref, weight_ref, keep_ref, send_ref, rows_scratch):
+    narrow, sub, wide = lax.axis_index("narrow"), lax.axis_index("sub"), lax.axis_index("wide")
+    mine = (narrow * 2 + sub) ^ wide
+    rows = a_ref.shape[0]
+    for k, ref in enumerate((a_ref, b_ref, c_ref, d_ref)):
+        m = mine ^ k
+        place = pl.multiple_of(((m & 1) * 2 + (m >> 1)) * rows, rows)
+        rows_scratch[pl.ds(place, rows), :] = ref[...]
+    mixed = rows_scratch[...]
+    step = 512
+    for start in range(0, weight_ref.shape[1], step):
+        product = jnp.dot(
+            mixed, weight_ref[:, start : start + step], preferred_element_type=jnp.float32
+        )
+        keep_ref[:, start : start + step] = product[: 2 * rows]
+        send_ref[:, start : start + step] = product[2 * rows :].astype(send_ref.dtype)
+
+
+def output(blocks, weight):
+    rows, depth = blocks[0].shape
+    columns = weight.shape[1]
+    return pl.pallas_call(
+        output_kernel,
+        out_shape=[
+            jax.ShapeDtypeStruct((2 * rows, columns), jnp.float32),
+            jax.ShapeDtypeStruct((2 * rows, columns), jnp.bfloat16),
+        ],
+        in_specs=[VMEM_SPEC] * 5,
+        out_specs=[VMEM_SPEC] * 2,
+        scratch_shapes=[pltpu.VMEM((4 * rows, depth), jnp.bfloat16)],
+        compiler_params=small_vmem(6),
+        name="output",
+    )(*blocks, weight)
+
+
+def add_kernel(keep_ref, other_ref, mine_ref, send_ref):
+    rows = mine_ref.shape[0]
+    total = keep_ref[...] + other_ref[...].astype(jnp.float32)
+    mine_ref[...] = total[:rows]
+    send_ref[...] = total[rows:].astype(send_ref.dtype)
+
+
+def add_halves(keep, other):
+    rows, columns = keep.shape[0] // 2, keep.shape[1]
+    return pl.pallas_call(
+        add_kernel,
+        out_shape=[
+            jax.ShapeDtypeStruct((rows, columns), jnp.float32),
+            jax.ShapeDtypeStruct((rows, columns), jnp.bfloat16),
+        ],
+        in_specs=[VMEM_SPEC] * 2,
+        out_specs=[VMEM_SPEC] * 2,
+        compiler_params=small_vmem(4),
+        name="add_halves",
+    )(keep, other)
+
+
+def direct_body(
+    tokens, q_weight, k_weight, v_weight, o_weight, cache_keys, cache_values, lengths
+):
+    chip = exchange(tokens, "narrow", 1)
+    core = exchange(tokens, "sub", 1)
+    mark = early(q_weight)
+    both = exchange(chip, "sub", 1)
+    half = HD // 2
+    exponents = jnp.arange(half, dtype=jnp.float32) * (2.0 / HD)
+    frequency = jnp.exp(-math.log(rope_base) * exponents)
+    angles = lengths.astype(jnp.float32)[:, None] * frequency[None, :]
+    cosine, sine = jnp.cos(angles), jnp.sin(angles)
+    cosine = jnp.concatenate([cosine, cosine], axis=1)
+    sine = jnp.concatenate([-sine, sine], axis=1)
+    parts = project(tokens, core, chip, both, q_weight, k_weight, v_weight, mark)
+    parts = [parts[0]] + [exchange(parts[k], "wide", k) for k in (1, 2, 3)]
+    keep, send = turn(parts, cosine, sine)
+    other = exchange(send, "sub", 1)
+    seqs, slots, kv_heads, _ = cache_keys.shape
+    keep, send = attend_here(
+        lengths,
+        keep,
+        other,
+        cache_keys.reshape(seqs, slots * kv_heads, HD),
+        cache_values.reshape(seqs, slots * kv_heads, HD),
+    )
+    other = exchange(send, "sub", 1)
+    first = lax.axis_index("sub") == 0
+    mixed = jnp.concatenate(
+        [jnp.where(first, keep, other), jnp.where(first, other, keep)], axis=0
+    )
+    blocks = [mixed] + [exchange(mixed, "wide", k) for k in (1, 2, 3)]
+    keep, send = output(blocks, o_weight)
+    mine, send = add_halves(keep, exchange(send, "sub", 1))
+    return (mine + exchange(send, "narrow", 1).astype(jnp.float32)).astype(jnp.bfloat16)
+
+
+def body_for(mesh):
+    sizes = tuple(mesh.shape[name] for name in ("wide", "narrow", "sub"))
+    return direct_body if sizes == (4, 2, 2) else general_body
+
+
 def solution(mesh):
     return jax.shard_map(
-        body,
+        body_for(mesh),
         mesh=mesh,
         in_specs=(
             P(("groups", "narrow", "sub"), "wide"),

time: 123 us -> 66.6 us (0.54)
  waiting for transfers between devices: 48.1 us -> 20.8 us
  blocking collectives: 26.7 us -> 0 us
  matrix products: 22.6 us -> 0 us
  local copies, waits for them, and re-layouts: 4.33 us -> 19.8 us
  between operations: 13.6 us -> 0.11 us
  Pallas kernels: 0 us -> 10.7 us
  starting transfers between devices: 3.34 us -> 13.4 us
  other arithmetic: 3.39 us -> 1.56 us
    reduce_scatter x2 -> x0, waiting for transfers between devices: 46.8 us -> none  [the longest x1 23.9 us: body(): lax.psum_scatter(partial_value, ('narrow', 'sub'), scatter_dimension=0, t...]
    all_gather x2 -> x0, blocking collectives: 22.9 us -> none  [the longest x1 14 us: body(): lax.all_gather(returned, 'wide', axis=0, tiled=True)]
    dot_general x7 -> x0, matrix products: 22.6 us -> none  [the longest x1 9.77 us: body(): jnp.dot(lax.all_gather(returned, 'wide', axis=0, tiled=True), o_weight, p...]
    ppermute x0 -> x13, waiting for transfers between devices: none -> 20.8 us  [exchange(): return lax.ppermute(array, axis, [(i, i ^ bit) for i in range(size)])]
    unnamed x10 -> x18, local copies, waits for them, and re-layouts: 2.07 us -> 19.8 us
    ppermute x0 -> x13, starting transfers between devices: none -> 13.4 us  [exchange(): return lax.ppermute(array, axis, [(i, i ^ bit) for i in range(size)])]
    pallas_call x0 -> x6, Pallas kernels: none -> 10.7 us  [the longest x1 3.89 us: attend_here(): pl.pallas_call(attend_kernel, out_shape=[shape, shape], in_specs=[SMEM_SP...]
    all_to_all x1 -> x0, blocking collectives: 3.79 us -> none  [body(): lax.all_to_all(attention, 'sub', split_axis=1, concat_axis=0, tiled=True)]
  transfers between devices with their start and end apart: 3 -> 13, of which waited for: 3 -> 9; matrix products, arithmetic and copies ran while one was open for 0% -> 1% of each run, Pallas kernels for 0% -> 0%
where the time goes in v1:
time: 66.6 us; the launch traced here: 66.3 us
  waiting for transfers between devices  20.8 us (31%)
  local copies, waits for them, and re-layouts  19.8 us (30%)
  starting transfers between devices  13.4 us (20%)
  Pallas kernels  10.7 us (16%)
  other arithmetic  1.56 us (2%)
    ppermute x13, waiting for transfers between devices, exchange(): return lax.ppermute(array, axis, [(i, i ^ bit) for i in range(size)])  20.8 us
    unnamed x18, local copies, waits for them, and re-layouts  19.8 us
    ppermute x13, starting transfers between devices, exchange(): return lax.ppermute(array, axis, [(i, i ^ bit) for i in range(size)])  13.4 us
    pallas_call x1, Pallas kernels, attend_here(): pl.pallas_call(attend_kernel, out_shape=[shape, shape], in_specs=[SMEM_SP...  3.89 us
    pallas_call x1, Pallas kernels, project(): pl.pallas_call(project_kernel, out_shape=[jax.ShapeDtypeStruct((rows, col...  3.55 us
    pallas_call x1, Pallas kernels, output(): pl.pallas_call(output_kernel, out_shape=[jax.ShapeDtypeStruct((2 * rows,...  3.02 us
  transfers between devices with their start and end apart: 13, of which 9 were waited for; matrix products, arithmetic and copies ran while one was open for 1% of the time, Pallas kernels for 0%

profile of v1, /device:TPU:0, one launch (start us, length us, event | category | flops | bytes accessed | tf_op | source)
XLA Modules:
  0.0 66.3 jit_solution(18231824524768367425)
XLA Ops:
  0.0 2.9 %collective-permute-start.1 = (bf16[16,4096]{1,0:T(8,128)(2,1)}, bf16[16,4096]{1,0:T(8,128)(2,1)S(1)}, u32[]{:S(2)}, u32[]{:S(2)}) collective-permute-start(bf16[16,4096]{1,0:T(8,128)(2,1)} %own_ref.1), channel_id=1, source_target_pairs={{0,2},{2,0},{1,3},{3,1},{4,6},{6,4},{5,7},{7,5},{8,10},{10,8},{9,1... | collective-permute-start | bytes 393224 | tf_op jit(solution)/shard_map/ppermute | solution.py:125
  2.9 0.0 collective-permute-start
  2.9 0.7 convert_element_type.9
  3.6 0.0 copy-start
  3.6 5.8 %copy-done = bf16[4096,2048]{1,0:T(8,128)(2,1)S(1)} copy-done((bf16[4096,2048]{1,0:T(8,128)(2,1)S(1)}, bf16[4096,2048]{1,0:T(8,128)(2,1)}, u32[]{:S(2)}) %copy-start) | copy-done | bytes 16777240
  9.4 0.0 copy-start.1
  9.4 0.0 collective-permute-done.1.chip_ref
  9.4 0.6 collective-permute-start.2
  10.0 0.0 copy-start.8
  10.0 0.1 fusion
  10.1 0.0 collective-permute-done.core_ref
  10.1 0.9 %collective-permute-done.2.both_ref = bf16[16,4096]{1,0:T(8,128)(2,1)S(1)} collective-permute-done((bf16[16,4096]{1,0:T(8,128)(2,1)S(1)}, bf16[16,4096]{1,0:T(8,128)(2,1)S(1)}, u32[]{:S(2)}, u32[]{:S(2)}) %collective-permute-start.2) | collective-permute-done | bytes 131104 | tf_op jit(solution)/shard_map/ppermute | solution.py:125
  11.0 4.2 %copy-done.1 = bf16[4096,2048]{1,0:T(8,128)(2,1)S(1)} copy-done((bf16[4096,2048]{1,0:T(8,128)(2,1)S(1)}, bf16[4096,2048]{1,0:T(8,128)(2,1)}, u32[]{:S(2)}) %copy-start.1) | copy-done | bytes 16777240
  15.1 0.0 copy-start.3
  15.1 1.6 %copy-done.3 = bf16[4096,256]{1,0:T(8,128)(2,1)S(1)} copy-done((bf16[4096,256]{1,0:T(8,128)(2,1)S(1)}, bf16[4096,256]{1,0:T(8,128)(2,1)}, u32[]{:S(2)}) %copy-start.3) | copy-done | bytes 2097176
  16.7 0.0 copy-start.4
  16.7 1.6 %copy-done.4 = bf16[4096,256]{1,0:T(8,128)(2,1)S(1)} copy-done((bf16[4096,256]{1,0:T(8,128)(2,1)S(1)}, bf16[4096,256]{1,0:T(8,128)(2,1)}, u32[]{:S(2)}) %copy-start.4) | copy-done | bytes 2097176
  18.3 0.0 copy-start.7
  18.3 0.9 %copy-done.7 = bf16[16,4096]{1,0:T(8,128)(2,1)S(1)} copy-done((bf16[16,4096]{1,0:T(8,128)(2,1)S(1)}, bf16[16,4096]{1,0:T(8,128)(2,1)}, u32[]{:S(2)}) %copy-start.7) | copy-done | bytes 131096
  19.2 0.0 copy-start.5
  19.2 0.0 copy-start.6
  19.2 3.5 %project.1 = (bf16[16,2304]{1,0:T(8,128)(2,1)S(1)}, bf16[16,2304]{1,0:T(8,128)(2,1)S(1)}, bf16[16,2304]{1,0:T(8,128)(2,1)S(1)}, bf16[16,2304]{1,0:T(8,128)(2,1)S(1)}) custom-call(bf16[16,4096]{1,0:T(8,128)(2,1)S(1)} %copy-done.7, bf16[16,4096]{1,0:T(8,128)(2,1)S(1)} %collective-permute-done.core_ref, bf16[16,4096]{1,0:T(8,128)(2,1)S(1)} %collective-permute-done.1.chip_ref, ...), custom_call_target="tpu_custom_call" | custom-call | flops 1207959552 | tf_op jit(solution)/shard_map/project/pallas_call | solution.py:185
  22.8 1.6 %collective-permute-start.3 = (bf16[16,2304]{1,0:T(8,128)(2,1)S(1)}, bf16[16,2304]{1,0:T(8,128)(2,1)S(1)}, u32[]{:S(2)}, u32[]{:S(2)}) collective-permute-start(bf16[16,2304]{1,0:T(8,128)(2,1)S(1)} %get-tuple-element.18), channel_id=1, source_target_pairs={{0,4},{4,0},{8,12},{12,8},{1,5},{5,1},{9,13},{13,9},{2,6},{6,2},{1... | collective-permute-start | bytes 221192 | tf_op jit(solution)/shard_map/ppermute | solution.py:125
  24.4 2.6 %collective-permute-start.4 = (bf16[16,2304]{1,0:T(8,128)(2,1)S(1)}, bf16[16,2304]{1,0:T(8,128)(2,1)S(1)}, u32[]{:S(2)}, u32[]{:S(2)}) collective-permute-start(bf16[16,2304]{1,0:T(8,128)(2,1)S(1)} %get-tuple-element.19), channel_id=1, source_target_pairs={{0,8},{4,12},{8,0},{12,4},{1,9},{5,13},{9,1},{13,5},{2,10},{6,14},... | collective-permute-start | bytes 221192 | tf_op jit(solution)/shard_map/ppermute | solution.py:125
  27.0 0.2 collective-permute-start.5
  27.2 0.1 pad_maximum_fusion.1
  27.3 0.2 collective-permute-done.3.b_ref
  27.5 5.8 %collective-permute-done.4.c_ref = bf16[16,2304]{1,0:T(8,128)(2,1)S(1)} collective-permute-done((bf16[16,2304]{1,0:T(8,128)(2,1)S(1)}, bf16[16,2304]{1,0:T(8,128)(2,1)S(1)}, u32[]{:S(2)}, u32[]{:S(2)}) %collective-permute-start.4) | collective-permute-done | bytes 73760 | tf_op jit(solution)/shard_map/ppermute | solution.py:125
  33.4 0.0 collective-permute-done.5.d_ref
  33.4 0.2 turn.1
  33.5 0.1 collective-permute-start.6
  33.6 1.2 %collective-permute-done.6.other_ref = bf16[144,128]{1,0:T(8,128)(2,1)S(1)} collective-permute-done((bf16[144,128]{1,0:T(8,128)(2,1)S(1)}, bf16[144,128]{1,0:T(8,128)(2,1)S(1)}, u32[]{:S(2)}, u32[]{:S(2)}) %collective-permute-start.6) | collective-permute-done | bytes 36896 | tf_op jit(solution)/shard_map/ppermute | solution.py:125
  34.8 0.0 copy-done.8
  34.8 0.0 copy-done.5
  34.8 0.0 copy-done.6
  34.8 3.9 %attend.1 = (bf16[8,2048]{1,0:T(8,128)(2,1)S(1)}, bf16[8,2048]{1,0:T(8,128)(2,1)S(1)}) custom-call(s32[16]{0:T(128)S(1)} %copy-done.8, bf16[144,128]{1,0:T(8,128)(2,1)S(1)} %get-tuple-element.21.own_ref, bf16[144,128]{1,0:T(8,128)(2,1)S(1)} %collective-permute-done.6.other_ref, bf16[8,1024,128]{2,1,0:T(8,128)(2,1)S(1)} %bitcast.2, ...), custom_call_target="tpu_custom_call" | custom-call | tf_op jit(solution)/shard_map/attend/pallas_call | solution.py:303
  38.7 0.2 collective-permute-start.7
  39.0 1.1 %collective-permute-done.7 = bf16[8,2048]{1,0:T(8,128)(2,1)S(1)} collective-permute-done((bf16[8,2048]{1,0:T(8,128)(2,1)S(1)}, bf16[8,2048]{1,0:T(8,128)(2,1)S(1)}, u32[]{:S(2)}, u32[]{:S(2)}) %collective-permute-start.7) | collective-permute-done | bytes 32800 | tf_op jit(solution)/shard_map/ppermute | solution.py:125
  40.0 2.8 %collective-permute-start.10 = (bf16[16,2048]{1,0:T(8,128)(2,1)S(1)}, bf16[16,2048]{1,0:T(8,128)(2,1)S(1)}, u32[]{:S(2)}, u32[]{:S(2)}) collective-permute-start(bf16[16,2048]{1,0:T(8,128)(2,1)S(1)} %pad_maximum_fusion.a_ref), channel_id=1, source_target_pairs={{0,12},{4,8},{8,4},{12,0},{1,13},{5,9},{9,5},{13,1},{2,14},{6,10},... | collective-permute-start | bytes 196616 | tf_op jit(solution)/shard_map/ppermute | solution.py:125
  42.8 0.4 collective-permute-start.9
  43.2 1.3 %collective-permute-start.8 = (bf16[16,2048]{1,0:T(8,128)(2,1)S(1)}, bf16[16,2048]{1,0:T(8,128)(2,1)S(1)}, u32[]{:S(2)}, u32[]{:S(2)}) collective-permute-start(bf16[16,2048]{1,0:T(8,128)(2,1)S(1)} %pad_maximum_fusion.a_ref), channel_id=1, source_target_pairs={{0,4},{4,0},{8,12},{12,8},{1,5},{5,1},{9,13},{13,9},{2,6},{6,2},{1... | collective-permute-start | bytes 196616 | tf_op jit(solution)/shard_map/ppermute | solution.py:125
  44.5 1.8 %collective-permute-done.10.d_ref = bf16[16,2048]{1,0:T(8,128)(2,1)S(1)} collective-permute-done((bf16[16,2048]{1,0:T(8,128)(2,1)S(1)}, bf16[16,2048]{1,0:T(8,128)(2,1)S(1)}, u32[]{:S(2)}, u32[]{:S(2)}) %collective-permute-start.10) | collective-permute-done | bytes 65568 | tf_op jit(solution)/shard_map/ppermute | solution.py:125
  46.3 3.3 %collective-permute-done.9.c_ref = bf16[16,2048]{1,0:T(8,128)(2,1)S(1)} collective-permute-done((bf16[16,2048]{1,0:T(8,128)(2,1)S(1)}, bf16[16,2048]{1,0:T(8,128)(2,1)S(1)}, u32[]{:S(2)}, u32[]{:S(2)}) %collective-permute-start.9) | collective-permute-done | bytes 65568 | tf_op jit(solution)/shard_map/ppermute | solution.py:125
  49.6 0.0 collective-permute-done.8.b_ref
  49.6 0.0 copy-start.2
  49.6 5.8 %copy-done.2 = bf16[2048,4096]{1,0:T(8,128)(2,1)S(1)} copy-done((bf16[2048,4096]{1,0:T(8,128)(2,1)S(1)}, bf16[2048,4096]{1,0:T(8,128)(2,1)}, u32[]{:S(2)}) %copy-start.2) | copy-done | bytes 16777240
  55.4 3.0 %output.1 = (f32[32,4096]{1,0:T(8,128)S(1)}, bf16[32,4096]{1,0:T(8,128)(2,1)S(1)}) custom-call(bf16[16,2048]{1,0:T(8,128)(2,1)S(1)} %pad_maximum_fusion.a_ref, bf16[16,2048]{1,0:T(8,128)(2,1)S(1)} %collective-permute-done.8.b_ref, bf16[16,2048]{1,0:T(8,128)(2,1)S(1)} %collective-permute-done.9.c_ref, bf16[16,2048]{1,0:T(8,128)(2,1)S(1)} %collective-permute-done.10.d_ref, ...), custom_call_target="tpu_custom_call" | custom-call | tf_op jit(solution)/shard_map/output/pallas_call | solution.py:335
  58.4 0.1 collective-permute-start.11
  58.5 1.5 %collective-permute-done.11.other_ref = bf16[32,4096]{1,0:T(8,128)(2,1)S(1)} collective-permute-done((bf16[32,4096]{1,0:T(8,128)(2,1)S(1)}, bf16[32,4096]{1,0:T(8,128)(2,1)S(1)}, u32[]{:S(2)}, u32[]{:S(2)}) %collective-permute-start.11) | collective-permute-done | bytes 262176 | tf_op jit(solution)/shard_map/ppermute | solution.py:125
  60.0 0.6 collective-permute-start.12
  60.6 5.0 %collective-permute-done.12 = bf16[16,4096]{1,0:T(8,128)(2,1)S(1)} collective-permute-done((bf16[16,4096]{1,0:T(8,128)(2,1)S(1)}, bf16[16,4096]{1,0:T(8,128)(2,1)S(1)}, u32[]{:S(2)}, u32[]{:S(2)}) %collective-permute-start.12) | collective-permute-done | bytes 131104 | tf_op jit(solution)/shard_map/ppermute | solution.py:125
  65.6 0.7 %add_convert_fusion = bf16[16,4096]{1,0:T(8,128)(2,1)} fusion(f32[16,4096]{1,0:T(8,128)S(1)} %get-tuple-element.27, bf16[16,4096]{1,0:T(8,128)(2,1)S(1)} %collective-permute-done.12), kind=kLoop, calls=%fused_computation | loop fusion | flops 196608 | bytes 524288 | tf_op jit(solution)/shard_map/convert_element_type | solution.py:405
  (5 shorter events, 0.1 us)
Async XLA Ops:
  0.0 9.4 %collective-permute-start.1 = (bf16[16,4096]{1,0:T(8,128)(2,1)}, bf16[16,4096]{1,0:T(8,128)(2,1)S(1)}, u32[]{:S(2)}, u32[]{:S(2)}) collective-permute-start(bf16[16,4096]{1,0:T(8,128)(2,1)} %own_ref.1), channel_id=1, source_target_pairs={{0,2},{2,0},{1,3},{3,1},{4,6},{6,4},{5,7},{7,5},{8,10},{10,8},{9,1... | collective-permute-start | bytes 393224 | tf_op jit(solution)/shard_map/ppermute | solution.py:125
  2.9 7.2 %collective-permute-start = (bf16[16,4096]{1,0:T(8,128)(2,1)}, bf16[16,4096]{1,0:T(8,128)(2,1)S(1)}, u32[]{:S(2)}, u32[]{:S(2)}) collective-permute-start(bf16[16,4096]{1,0:T(8,128)(2,1)} %own_ref.1), channel_id=1, source_target_pairs={{0,1},{1,0},{2,3},{3,2},{4,5},{5,4},{6,7},{7,6},{8,9},{9,8},{10,11... | collective-permute-start | bytes 393224 | tf_op jit(solution)/shard_map/ppermute | solution.py:125
  3.6 5.8 %copy-start = (bf16[4096,2048]{1,0:T(8,128)(2,1)S(1)}, bf16[4096,2048]{1,0:T(8,128)(2,1)}, u32[]{:S(2)}) copy-start(bf16[4096,2048]{1,0:T(8,128)(2,1)} %q_ref.1) | copy-start | bytes 50331652
  9.4 5.8 %copy-start.1 = (bf16[4096,2048]{1,0:T(8,128)(2,1)S(1)}, bf16[4096,2048]{1,0:T(8,128)(2,1)}, u32[]{:S(2)}) copy-start(bf16[4096,2048]{1,0:T(8,128)(2,1)} %q_ref.1) | copy-start | bytes 50331652
  9.4 1.6 %collective-permute-start.2 = (bf16[16,4096]{1,0:T(8,128)(2,1)S(1)}, bf16[16,4096]{1,0:T(8,128)(2,1)S(1)}, u32[]{:S(2)}, u32[]{:S(2)}) collective-permute-start(bf16[16,4096]{1,0:T(8,128)(2,1)S(1)} %collective-permute-done.1.chip_ref), channel_id=1, source_target_pairs={{0,1},{1,0},{2,3},{3,2},{4,5},{5,4},{6,7},{7,6},{8,9},{9,8},{10,11... | collective-permute-start | bytes 393224 | tf_op jit(solution)/shard_map/ppermute | solution.py:125
  10.0 24.9 %copy-start.8 = (s32[16]{0:T(128)S(1)}, s32[16]{0:T(128)}, u32[]{:S(2)}) copy-start(s32[16]{0:T(128)} %length_ref.1) | copy-start | bytes 196
  15.1 1.6 %copy-start.3 = (bf16[4096,256]{1,0:T(8,128)(2,1)S(1)}, bf16[4096,256]{1,0:T(8,128)(2,1)}, u32[]{:S(2)}) copy-start(bf16[4096,256]{1,0:T(8,128)(2,1)} %k_ref.1) | copy-start | bytes 6291460
  16.7 1.6 %copy-start.4 = (bf16[4096,256]{1,0:T(8,128)(2,1)S(1)}, bf16[4096,256]{1,0:T(8,128)(2,1)}, u32[]{:S(2)}) copy-start(bf16[4096,256]{1,0:T(8,128)(2,1)} %v_ref.1) | copy-start | bytes 6291460
  18.3 0.9 %copy-start.7 = (bf16[16,4096]{1,0:T(8,128)(2,1)S(1)}, bf16[16,4096]{1,0:T(8,128)(2,1)}, u32[]{:S(2)}) copy-start(bf16[16,4096]{1,0:T(8,128)(2,1)} %own_ref.1) | copy-start | bytes 393220
  19.2 15.6 %copy-start.5 = (bf16[8,512,2,128]{3,2,1,0:T(2,128)(2,1)S(1)}, bf16[8,512,2,128]{3,2,1,0:T(2,128)(2,1)}, u32[]{:S(2)}) copy-start(bf16[8,512,2,128]{3,2,1,0:T(2,128)(2,1)} %param.13) | copy-start | bytes 6291460
  19.2 15.6 %copy-start.6 = (bf16[8,512,2,128]{3,2,1,0:T(2,128)(2,1)S(1)}, bf16[8,512,2,128]{3,2,1,0:T(2,128)(2,1)}, u32[]{:S(2)}) copy-start(bf16[8,512,2,128]{3,2,1,0:T(2,128)(2,1)} %param.14) | copy-start | bytes 6291460
  22.8 4.8 %collective-permute-start.3 = (bf16[16,2304]{1,0:T(8,128)(2,1)S(1)}, bf16[16,2304]{1,0:T(8,128)(2,1)S(1)}, u32[]{:S(2)}, u32[]{:S(2)}) collective-permute-start(bf16[16,2304]{1,0:T(8,128)(2,1)S(1)} %get-tuple-element.18), channel_id=1, source_target_pairs={{0,4},{4,0},{8,12},{12,8},{1,5},{5,1},{9,13},{13,9},{2,6},{6,2},{1... | collective-permute-start | bytes 221192 | tf_op jit(solution)/shard_map/ppermute | solution.py:125
  24.4 8.9 %collective-permute-start.4 = (bf16[16,2304]{1,0:T(8,128)(2,1)S(1)}, bf16[16,2304]{1,0:T(8,128)(2,1)S(1)}, u32[]{:S(2)}, u32[]{:S(2)}) collective-permute-start(bf16[16,2304]{1,0:T(8,128)(2,1)S(1)} %get-tuple-element.19), channel_id=1, source_target_pairs={{0,8},{4,12},{8,0},{12,4},{1,9},{5,13},{9,1},{13,5},{2,10},{6,14},... | collective-permute-start | bytes 221192 | tf_op jit(solution)/shard_map/ppermute | solution.py:125
  27.0 6.4 %collective-permute-start.5 = (bf16[16,2304]{1,0:T(8,128)(2,1)S(1)}, bf16[16,2304]{1,0:T(8,128)(2,1)S(1)}, u32[]{:S(2)}, u32[]{:S(2)}) collective-permute-start(bf16[16,2304]{1,0:T(8,128)(2,1)S(1)} %get-tuple-element.20), channel_id=1, source_target_pairs={{0,12},{4,8},{8,4},{12,0},{1,13},{5,9},{9,5},{13,1},{2,14},{6,10},... | collective-permute-start | bytes 221192 | tf_op jit(solution)/shard_map/ppermute | solution.py:125
  33.5 1.3 %collective-permute-start.6 = (bf16[144,128]{1,0:T(8,128)(2,1)S(1)}, bf16[144,128]{1,0:T(8,128)(2,1)S(1)}, u32[]{:S(2)}, u32[]{:S(2)}) collective-permute-start(bf16[144,128]{1,0:T(8,128)(2,1)S(1)} %get-tuple-element.22), channel_id=1, source_target_pairs={{0,1},{1,0},{2,3},{3,2},{4,5},{5,4},{6,7},{7,6},{8,9},{9,8},{10,11... | collective-permute-start | bytes 110600 | tf_op jit(solution)/shard_map/ppermute | solution.py:125
  38.7 1.3 %collective-permute-start.7 = (bf16[8,2048]{1,0:T(8,128)(2,1)S(1)}, bf16[8,2048]{1,0:T(8,128)(2,1)S(1)}, u32[]{:S(2)}, u32[]{:S(2)}) collective-permute-start(bf16[8,2048]{1,0:T(8,128)(2,1)S(1)} %get-tuple-element.24), channel_id=1, source_target_pairs={{0,1},{1,0},{2,3},{3,2},{4,5},{5,4},{6,7},{7,6},{8,9},{9,8},{10,11... | collective-permute-start | bytes 98312 | tf_op jit(solution)/shard_map/ppermute | solution.py:125
  40.0 6.2 %collective-permute-start.10 = (bf16[16,2048]{1,0:T(8,128)(2,1)S(1)}, bf16[16,2048]{1,0:T(8,128)(2,1)S(1)}, u32[]{:S(2)}, u32[]{:S(2)}) collective-permute-start(bf16[16,2048]{1,0:T(8,128)(2,1)S(1)} %pad_maximum_fusion.a_ref), channel_id=1, source_target_pairs={{0,12},{4,8},{8,4},{12,0},{1,13},{5,9},{9,5},{13,1},{2,14},{6,10},... | collective-permute-start | bytes 196616 | tf_op jit(solution)/shard_map/ppermute | solution.py:125
  42.8 6.8 %collective-permute-start.9 = (bf16[16,2048]{1,0:T(8,128)(2,1)S(1)}, bf16[16,2048]{1,0:T(8,128)(2,1)S(1)}, u32[]{:S(2)}, u32[]{:S(2)}) collective-permute-start(bf16[16,2048]{1,0:T(8,128)(2,1)S(1)} %pad_maximum_fusion.a_ref), channel_id=1, source_target_pairs={{0,8},{4,12},{8,0},{12,4},{1,9},{5,13},{9,1},{13,5},{2,10},{6,14},... | collective-permute-start | bytes 196616 | tf_op jit(solution)/shard_map/ppermute | solution.py:125
  43.2 6.3 %collective-permute-start.8 = (bf16[16,2048]{1,0:T(8,128)(2,1)S(1)}, bf16[16,2048]{1,0:T(8,128)(2,1)S(1)}, u32[]{:S(2)}, u32[]{:S(2)}) collective-permute-start(bf16[16,2048]{1,0:T(8,128)(2,1)S(1)} %pad_maximum_fusion.a_ref), channel_id=1, source_target_pairs={{0,4},{4,0},{8,12},{12,8},{1,5},{5,1},{9,13},{13,9},{2,6},{6,2},{1... | collective-permute-start | bytes 196616 | tf_op jit(solution)/shard_map/ppermute | solution.py:125
  49.6 5.8 %copy-start.2 = (bf16[2048,4096]{1,0:T(8,128)(2,1)S(1)}, bf16[2048,4096]{1,0:T(8,128)(2,1)}, u32[]{:S(2)}) copy-start(bf16[2048,4096]{1,0:T(8,128)(2,1)} %weight_ref.3) | copy-start | bytes 50331652
  58.4 1.6 %collective-permute-start.11 = (bf16[32,4096]{1,0:T(8,128)(2,1)S(1)}, bf16[32,4096]{1,0:T(8,128)(2,1)S(1)}, u32[]{:S(2)}, u32[]{:S(2)}) collective-permute-start(bf16[32,4096]{1,0:T(8,128)(2,1)S(1)} %get-tuple-element.26), channel_id=1, source_target_pairs={{0,1},{1,0},{2,3},{3,2},{4,5},{5,4},{6,7},{7,6},{8,9},{9,8},{10,11... | collective-permute-start | bytes 786440 | tf_op jit(solution)/shard_map/ppermute | solution.py:125
  60.0 5.6 %collective-permute-start.12 = (bf16[16,4096]{1,0:T(8,128)(2,1)S(1)}, bf16[16,4096]{1,0:T(8,128)(2,1)S(1)}, u32[]{:S(2)}, u32[]{:S(2)}) collective-permute-start(bf16[16,4096]{1,0:T(8,128)(2,1)S(1)} %get-tuple-element.28), channel_id=1, source_target_pairs={{0,2},{2,0},{1,3},{3,1},{4,6},{6,4},{5,7},{7,5},{8,10},{10,8},{9,1... | collective-permute-start | bytes 393224 | tf_op jit(solution)/shard_map/ppermute | solution.py:125

commit v2 on v1

--- a/solution.py
+++ b/solution.py
@@ -125,26 +125,30 @@
     return lax.ppermute(array, axis, [(i, i ^ bit) for i in range(size)])
 
 
-def touch_kernel(weight_ref, out_ref):
-    out_ref[...] = weight_ref[:8, :128].astype(jnp.float32)
-
-
-def early(weight):
-    return pl.pallas_call(
-        touch_kernel,
-        out_shape=jax.ShapeDtypeStruct((8, 128), jnp.float32),
-        in_specs=[VMEM_SPEC],
+def fetch_kernel(weight_ref, after_ref, out_ref, sem):
+    del after_ref
+    copy = pltpu.make_async_copy(weight_ref, out_ref, sem)
+    copy.start()
+    copy.wait()
+
+
+def fetch(weight, after, room):
+    return pl.pallas_call(
+        fetch_kernel,
+        out_shape=pltpu.VMEM(weight.shape, weight.dtype),
+        in_specs=[pl.BlockSpec(memory_space=pl.ANY)] * 2,
         out_specs=VMEM_SPEC,
-        compiler_params=small_vmem(1),
+        scratch_shapes=[pltpu.SemaphoreType.DMA],
+        compiler_params=small_vmem(room),
         cost_estimate=pl.CostEstimate(
             flops=0, bytes_accessed=weight.size * 2, transcendentals=0
         ),
-        name="early",
-    )(weight)
+        name="fetch",
+    )(weight, after)
 
 
 def project_kernel(
-    own_ref, core_ref, chip_ref, both_ref, q_ref, k_ref, v_ref, mark_ref, *refs
+    own_ref, core_ref, chip_ref, both_ref, q_ref, k_ref, v_ref, *refs
 ):
     outs, rows_scratch = refs[:4], refs[4]
     narrow, sub, wide = lax.axis_index("narrow"), lax.axis_index("sub"), lax.axis_index("wide")
@@ -179,21 +183,21 @@
         side(v_ref)
 
 
-def project(own, core, chip, both, q_weight, k_weight, v_weight, mark):
+def project(own, core, chip, both, q_weight, k_weight, v_weight):
     rows, depth = own.shape
     columns = q_weight.shape[1] + k_weight.shape[1]
     return pl.pallas_call(
         project_kernel,
         out_shape=[jax.ShapeDtypeStruct((rows, columns), jnp.bfloat16)] * 4,
-        in_specs=[VMEM_SPEC] * 8,
+        in_specs=[VMEM_SPEC] * 7,
         out_specs=[VMEM_SPEC] * 4,
         scratch_shapes=[pltpu.VMEM((4 * rows, depth), jnp.bfloat16)],
         compiler_params=small_vmem(6),
         cost_estimate=pl.CostEstimate(
-            flops=2 * 4 * rows * depth * columns, bytes_accessed=0, transcendentals=0
+            flops=4 * 2 * 4 * rows * depth * columns, bytes_accessed=0, transcendentals=0
         ),
         name="project",
-    )(own, core, chip, both, q_weight, k_weight, v_weight, mark)
+    )(own, core, chip, both, q_weight, k_weight, v_weight)
 
 
 def turn_kernel(a_ref, b_ref, c_ref, d_ref, cos_ref, sin_ref, keep_ref, send_ref, scratch):
@@ -307,6 +311,7 @@
         out_specs=[VMEM_SPEC] * 2,
         scratch_shapes=[pltpu.VMEM((2 * heads * seqs, HD), jnp.float32)],
         compiler_params=small_vmem(6),
+        cost_estimate=pl.CostEstimate(flops=4 * 10**9, bytes_accessed=0, transcendentals=0),
         name="attend",
     )(lengths, own, other, keys, values)
 
@@ -373,7 +378,7 @@
 ):
     chip = exchange(tokens, "narrow", 1)
     core = exchange(tokens, "sub", 1)
-    mark = early(q_weight)
+    q_weight = fetch(q_weight, tokens, 34)
     both = exchange(chip, "sub", 1)
     half = HD // 2
     exponents = jnp.arange(half, dtype=jnp.float32) * (2.0 / HD)
@@ -382,7 +387,8 @@
     cosine, sine = jnp.cos(angles), jnp.sin(angles)
     cosine = jnp.concatenate([cosine, cosine], axis=1)
     sine = jnp.concatenate([-sine, sine], axis=1)
-    parts = project(tokens, core, chip, both, q_weight, k_weight, v_weight, mark)
+    parts = project(tokens, core, chip, both, q_weight, k_weight, v_weight)
+    o_weight = fetch(o_weight, parts[0], 34)
     parts = [parts[0]] + [exchange(parts[k], "wide", k) for k in (1, 2, 3)]
     keep, send = turn(parts, cosine, sine)
     other = exchange(send, "sub", 1)

time: 66.6 us -> 54.3 us (0.82)
  local copies, waits for them, and re-layouts: 19.8 us -> 0.93 us
  Pallas kernels: 10.7 us -> 22.3 us
  waiting for transfers between devices: 20.8 us -> 15.7 us
    unnamed x18 -> x12, local copies, waits for them, and re-layouts: 19.8 us -> 0.93 us
    pallas_call x1 -> x2, Pallas kernels: 0.01 us -> 11.7 us  [fetch(): pl.pallas_call(fetch_kernel, out_shape=pltpu.VMEM(weight.shape, weight.dt...]
    ppermute x13, waiting for transfers between devices: 20.8 us -> 15.7 us  [exchange(): return lax.ppermute(array, axis, [(i, i ^ bit) for i in range(size)])]
  transfers between devices with their start and end apart: 13 -> 13, of which waited for: 9 -> 7; matrix products, arithmetic and copies ran while one was open for 1% -> 2% of each run, Pallas kernels for 0% -> 22%
where the time goes in v2:
time: 54.3 us; the launch traced here: 54.1 us
  Pallas kernels  22.3 us (41%)
  waiting for transfers between devices  15.7 us (29%)
  starting transfers between devices  13.4 us (25%)
  other arithmetic  1.56 us (3%)
  local copies, waits for them, and re-layouts  0.93 us (2%)
    ppermute x13, waiting for transfers between devices, exchange(): return lax.ppermute(array, axis, [(i, i ^ bit) for i in range(size)])  15.7 us
    ppermute x13, starting transfers between devices, exchange(): return lax.ppermute(array, axis, [(i, i ^ bit) for i in range(size)])  13.4 us
    pallas_call x2, Pallas kernels, fetch(): pl.pallas_call(fetch_kernel, out_shape=pltpu.VMEM(weight.shape, weight.dt...  11.7 us
    pallas_call x1, Pallas kernels, attend_here(): pl.pallas_call(attend_kernel, out_shape=[shape, shape], in_specs=[SMEM_SP...  3.88 us
    pallas_call x1, Pallas kernels, project(): pl.pallas_call(project_kernel, out_shape=[jax.ShapeDtypeStruct((rows, col...  3.51 us
    pallas_call x1, Pallas kernels, output(): pl.pallas_call(output_kernel, out_shape=[jax.ShapeDtypeStruct((2 * rows,...  3.04 us
  transfers between devices with their start and end apart: 13, of which 7 were waited for; matrix products, arithmetic and copies ran while one was open for 2% of the time, Pallas kernels for 22%

profile of v2, /device:TPU:0, one launch (start us, length us, event | category | flops | bytes accessed | tf_op | source)
XLA Modules:
  0.0 54.1 jit_solution(3481852122616192999)
XLA Ops:
  0.0 2.9 %collective-permute-start.1 = (bf16[16,4096]{1,0:T(8,128)(2,1)}, bf16[16,4096]{1,0:T(8,128)(2,1)S(1)}, u32[]{:S(2)}, u32[]{:S(2)}) collective-permute-start(bf16[16,4096]{1,0:T(8,128)(2,1)} %own_ref.1), channel_id=1, source_target_pairs={{0,2},{2,0},{1,3},{3,1},{4,6},{6,4},{5,7},{7,5},{8,10},{10,8},{9,1... | collective-permute-start | bytes 393224 | tf_op jit(solution)/shard_map/ppermute | solution.py:125
  2.9 0.0 collective-permute-start
  2.9 0.7 %convert_element_type.9 = f32[16]{0:T(128)S(1)} convert(s32[16]{0:T(128)} %length_ref.1) | non-fusion elementwise | flops 16 | bytes 128 | tf_op jit(solution)/shard_map/convert_element_type | solution.py:386
  3.6 0.0 copy-start.2
  3.6 0.9 %copy-done.2 = bf16[16,4096]{1,0:T(8,128)(2,1)S(1)} copy-done((bf16[16,4096]{1,0:T(8,128)(2,1)S(1)}, bf16[16,4096]{1,0:T(8,128)(2,1)}, u32[]{:S(2)}) %copy-start.2) | copy-done | bytes 131096
  4.5 0.0 copy-start
  4.5 0.0 copy-start.1
  4.5 5.9 %fetch.2.q_ref = bf16[4096,2048]{1,0:T(8,128)(2,1)S(1)} custom-call(bf16[4096,2048]{1,0:T(8,128)(2,1)} %weight_ref.2, bf16[16,4096]{1,0:T(8,128)(2,1)S(1)} %copy-done.2), custom_call_target="tpu_custom_call" | custom-call | bytes 16777216 | tf_op jit(solution)/shard_map/fetch/pallas_call | solution.py:136
  10.4 0.0 copy-start.3
  10.5 0.0 copy-start.4
  10.5 0.0 copy-start.5
  10.5 0.0 collective-permute-done.1.chip_ref
  10.5 0.6 %collective-permute-start.2 = (bf16[16,4096]{1,0:T(8,128)(2,1)S(1)}, bf16[16,4096]{1,0:T(8,128)(2,1)S(1)}, u32[]{:S(2)}, u32[]{:S(2)}) collective-permute-start(bf16[16,4096]{1,0:T(8,128)(2,1)S(1)} %collective-permute-done.1.chip_ref), channel_id=1, source_target_pairs={{0,1},{1,0},{2,3},{3,2},{4,5},{5,4},{6,7},{7,6},{8,9},{9,8},{10,11... | collective-permute-start | bytes 393224 | tf_op jit(solution)/shard_map/ppermute | solution.py:125
  11.1 0.1 fusion
  11.2 0.0 collective-permute-done.core_ref
  11.2 0.9 %collective-permute-done.2.both_ref = bf16[16,4096]{1,0:T(8,128)(2,1)S(1)} collective-permute-done((bf16[16,4096]{1,0:T(8,128)(2,1)S(1)}, bf16[16,4096]{1,0:T(8,128)(2,1)S(1)}, u32[]{:S(2)}, u32[]{:S(2)}) %collective-permute-start.2) | collective-permute-done | bytes 131104 | tf_op jit(solution)/shard_map/ppermute | solution.py:125
  12.1 0.0 copy-done
  12.1 0.0 copy-done.1
  12.1 3.5 %project.1 = (bf16[16,2304]{1,0:T(8,128)(2,1)S(1)}, bf16[16,2304]{1,0:T(8,128)(2,1)S(1)}, bf16[16,2304]{1,0:T(8,128)(2,1)S(1)}, bf16[16,2304]{1,0:T(8,128)(2,1)S(1)}) custom-call(bf16[16,4096]{1,0:T(8,128)(2,1)S(1)} %copy-done.2, bf16[16,4096]{1,0:T(8,128)(2,1)S(1)} %collective-permute-done.core_ref, bf16[16,4096]{1,0:T(8,128)(2,1)S(1)} %collective-permute-done.1.chip_ref, ...), custom_call_target="tpu_custom_call" | custom-call | flops 4831838208 | tf_op jit(solution)/shard_map/project/pallas_call | solution.py:189
  15.6 1.7 %collective-permute-start.3 = (bf16[16,2304]{1,0:T(8,128)(2,1)S(1)}, bf16[16,2304]{1,0:T(8,128)(2,1)S(1)}, u32[]{:S(2)}, u32[]{:S(2)}) collective-permute-start(bf16[16,2304]{1,0:T(8,128)(2,1)S(1)} %get-tuple-element.18), channel_id=1, source_target_pairs={{0,4},{4,0},{8,12},{12,8},{1,5},{5,1},{9,13},{13,9},{2,6},{6,2},{1... | collective-permute-start | bytes 221192 | tf_op jit(solution)/shard_map/ppermute | solution.py:125
  17.2 2.6 %collective-permute-start.4 = (bf16[16,2304]{1,0:T(8,128)(2,1)S(1)}, bf16[16,2304]{1,0:T(8,128)(2,1)S(1)}, u32[]{:S(2)}, u32[]{:S(2)}) collective-permute-start(bf16[16,2304]{1,0:T(8,128)(2,1)S(1)} %get-tuple-element.19), channel_id=1, source_target_pairs={{0,8},{4,12},{8,0},{12,4},{1,9},{5,13},{9,1},{13,5},{2,10},{6,14},... | collective-permute-start | bytes 221192 | tf_op jit(solution)/shard_map/ppermute | solution.py:125
  19.8 0.2 collective-permute-start.5
  20.1 0.1 pad_maximum_fusion.1
  20.1 0.1 collective-permute-done.3.b_ref
  20.2 6.0 %collective-permute-done.4.c_ref = bf16[16,2304]{1,0:T(8,128)(2,1)S(1)} collective-permute-done((bf16[16,2304]{1,0:T(8,128)(2,1)S(1)}, bf16[16,2304]{1,0:T(8,128)(2,1)S(1)}, u32[]{:S(2)}, u32[]{:S(2)}) %collective-permute-start.4) | collective-permute-done | bytes 73760 | tf_op jit(solution)/shard_map/ppermute | solution.py:125
  26.2 0.0 collective-permute-done.5.d_ref
  26.2 0.2 turn.1
  26.4 0.1 collective-permute-start.6
  26.5 1.2 %collective-permute-done.6.other_ref = bf16[144,128]{1,0:T(8,128)(2,1)S(1)} collective-permute-done((bf16[144,128]{1,0:T(8,128)(2,1)S(1)}, bf16[144,128]{1,0:T(8,128)(2,1)S(1)}, u32[]{:S(2)}, u32[]{:S(2)}) %collective-permute-start.6) | collective-permute-done | bytes 36896 | tf_op jit(solution)/shard_map/ppermute | solution.py:125
  27.7 0.0 copy-done.3
  27.7 0.0 copy-done.4
  27.7 0.0 copy-done.5
  27.7 3.9 %attend.1 = (bf16[8,2048]{1,0:T(8,128)(2,1)S(1)}, bf16[8,2048]{1,0:T(8,128)(2,1)S(1)}) custom-call(s32[16]{0:T(128)S(1)} %copy-done.5, bf16[144,128]{1,0:T(8,128)(2,1)S(1)} %get-tuple-element.21.own_ref, bf16[144,128]{1,0:T(8,128)(2,1)S(1)} %collective-permute-done.6.other_ref, bf16[8,1024,128]{2,1,0:T(8,128)(2,1)S(1)} %bitcast.2, ...), custom_call_target="tpu_custom_call" | custom-call | flops 4000000000 | tf_op jit(solution)/shard_map/attend/pallas_call | solution.py:307
  31.6 0.2 collective-permute-start.7
  31.8 1.0 %collective-permute-done.7 = bf16[8,2048]{1,0:T(8,128)(2,1)S(1)} collective-permute-done((bf16[8,2048]{1,0:T(8,128)(2,1)S(1)}, bf16[8,2048]{1,0:T(8,128)(2,1)S(1)}, u32[]{:S(2)}, u32[]{:S(2)}) %collective-permute-start.7) | collective-permute-done | bytes 32800 | tf_op jit(solution)/shard_map/ppermute | solution.py:125
  32.9 2.7 %collective-permute-start.10 = (bf16[16,2048]{1,0:T(8,128)(2,1)S(1)}, bf16[16,2048]{1,0:T(8,128)(2,1)S(1)}, u32[]{:S(2)}, u32[]{:S(2)}) collective-permute-start(bf16[16,2048]{1,0:T(8,128)(2,1)S(1)} %pad_maximum_fusion.a_ref), channel_id=1, source_target_pairs={{0,12},{4,8},{8,4},{12,0},{1,13},{5,9},{9,5},{13,1},{2,14},{6,10},... | collective-permute-start | bytes 196616 | tf_op jit(solution)/shard_map/ppermute | solution.py:125
  35.5 0.4 collective-permute-start.9
  36.0 1.4 %collective-permute-start.8 = (bf16[16,2048]{1,0:T(8,128)(2,1)S(1)}, bf16[16,2048]{1,0:T(8,128)(2,1)S(1)}, u32[]{:S(2)}, u32[]{:S(2)}) collective-permute-start(bf16[16,2048]{1,0:T(8,128)(2,1)S(1)} %pad_maximum_fusion.a_ref), channel_id=1, source_target_pairs={{0,4},{4,0},{8,12},{12,8},{1,5},{5,1},{9,13},{13,9},{2,6},{6,2},{1... | collective-permute-start | bytes 196616 | tf_op jit(solution)/shard_map/ppermute | solution.py:125
  37.3 5.8 %fetch.3.weight_ref = bf16[2048,4096]{1,0:T(8,128)(2,1)S(1)} custom-call(bf16[2048,4096]{1,0:T(8,128)(2,1)} %weight_ref.3, bf16[16,2304]{1,0:T(8,128)(2,1)S(1)} %get-tuple-element.17.a_ref.after_ref), custom_call_target="tpu_custom_call" | custom-call | bytes 16777216 | tf_op jit(solution)/shard_map/fetch/pallas_call | solution.py:136
  43.1 0.0 collective-permute-done.10.d_ref
  43.1 0.0 collective-permute-done.9.c_ref
  43.1 0.0 collective-permute-done.8.b_ref
  43.2 3.0 %output.1 = (f32[32,4096]{1,0:T(8,128)S(1)}, bf16[32,4096]{1,0:T(8,128)(2,1)S(1)}) custom-call(bf16[16,2048]{1,0:T(8,128)(2,1)S(1)} %pad_maximum_fusion.a_ref, bf16[16,2048]{1,0:T(8,128)(2,1)S(1)} %collective-permute-done.8.b_ref, bf16[16,2048]{1,0:T(8,128)(2,1)S(1)} %collective-permute-done.9.c_ref, bf16[16,2048]{1,0:T(8,128)(2,1)S(1)} %collective-permute-done.10.d_ref, ...), custom_call_target="tpu_custom_call" | custom-call | tf_op jit(solution)/shard_map/output/pallas_call | solution.py:340
  46.2 0.1 collective-permute-start.11
  46.3 1.5 %collective-permute-done.11.other_ref = bf16[32,4096]{1,0:T(8,128)(2,1)S(1)} collective-permute-done((bf16[32,4096]{1,0:T(8,128)(2,1)S(1)}, bf16[32,4096]{1,0:T(8,128)(2,1)S(1)}, u32[]{:S(2)}, u32[]{:S(2)}) %collective-permute-start.11) | collective-permute-done | bytes 262176 | tf_op jit(solution)/shard_map/ppermute | solution.py:125
  47.9 0.6 %collective-permute-start.12 = (bf16[16,4096]{1,0:T(8,128)(2,1)S(1)}, bf16[16,4096]{1,0:T(8,128)(2,1)S(1)}, u32[]{:S(2)}, u32[]{:S(2)}) collective-permute-start(bf16[16,4096]{1,0:T(8,128)(2,1)S(1)} %get-tuple-element.28), channel_id=1, source_target_pairs={{0,2},{2,0},{1,3},{3,1},{4,6},{6,4},{5,7},{7,5},{8,10},{10,8},{9,1... | collective-permute-start | bytes 393224 | tf_op jit(solution)/shard_map/ppermute | solution.py:125
  48.5 5.0 %collective-permute-done.12 = bf16[16,4096]{1,0:T(8,128)(2,1)S(1)} collective-permute-done((bf16[16,4096]{1,0:T(8,128)(2,1)S(1)}, bf16[16,4096]{1,0:T(8,128)(2,1)S(1)}, u32[]{:S(2)}, u32[]{:S(2)}) %collective-permute-start.12) | collective-permute-done | bytes 131104 | tf_op jit(solution)/shard_map/ppermute | solution.py:125
  53.5 0.7 %add_convert_fusion = bf16[16,4096]{1,0:T(8,128)(2,1)} fusion(f32[16,4096]{1,0:T(8,128)S(1)} %get-tuple-element.27, bf16[16,4096]{1,0:T(8,128)(2,1)S(1)} %collective-permute-done.12), kind=kLoop, calls=%fused_computation | loop fusion | flops 196608 | bytes 524288 | tf_op jit(solution)/shard_map/convert_element_type | solution.py:411
  (4 shorter events, 0.1 us)
Async XLA Ops:
  0.0 10.5 %collective-permute-start.1 = (bf16[16,4096]{1,0:T(8,128)(2,1)}, bf16[16,4096]{1,0:T(8,128)(2,1)S(1)}, u32[]{:S(2)}, u32[]{:S(2)}) collective-permute-start(bf16[16,4096]{1,0:T(8,128)(2,1)} %own_ref.1), channel_id=1, source_target_pairs={{0,2},{2,0},{1,3},{3,1},{4,6},{6,4},{5,7},{7,5},{8,10},{10,8},{9,1... | collective-permute-start | bytes 393224 | tf_op jit(solution)/shard_map/ppermute | solution.py:125
  2.9 8.3 %collective-permute-start = (bf16[16,4096]{1,0:T(8,128)(2,1)}, bf16[16,4096]{1,0:T(8,128)(2,1)S(1)}, u32[]{:S(2)}, u32[]{:S(2)}) collective-permute-start(bf16[16,4096]{1,0:T(8,128)(2,1)} %own_ref.1), channel_id=1, source_target_pairs={{0,1},{1,0},{2,3},{3,2},{4,5},{5,4},{6,7},{7,6},{8,9},{9,8},{10,11... | collective-permute-start | bytes 393224 | tf_op jit(solution)/shard_map/ppermute | solution.py:125
  3.6 0.9 %copy-start.2 = (bf16[16,4096]{1,0:T(8,128)(2,1)S(1)}, bf16[16,4096]{1,0:T(8,128)(2,1)}, u32[]{:S(2)}) copy-start(bf16[16,4096]{1,0:T(8,128)(2,1)} %own_ref.1) | copy-start | bytes 393220
  4.5 7.6 %copy-start = (bf16[4096,256]{1,0:T(8,128)(2,1)S(1)}, bf16[4096,256]{1,0:T(8,128)(2,1)}, u32[]{:S(2)}) copy-start(bf16[4096,256]{1,0:T(8,128)(2,1)} %k_ref.1) | copy-start | bytes 6291460
  4.5 7.6 %copy-start.1 = (bf16[4096,256]{1,0:T(8,128)(2,1)S(1)}, bf16[4096,256]{1,0:T(8,128)(2,1)}, u32[]{:S(2)}) copy-start(bf16[4096,256]{1,0:T(8,128)(2,1)} %v_ref.1) | copy-start | bytes 6291460
  10.4 17.2 %copy-start.3 = (bf16[8,512,2,128]{3,2,1,0:T(2,128)(2,1)S(1)}, bf16[8,512,2,128]{3,2,1,0:T(2,128)(2,1)}, u32[]{:S(2)}) copy-start(bf16[8,512,2,128]{3,2,1,0:T(2,128)(2,1)} %param.13) | copy-start | bytes 6291460
  10.5 17.2 %copy-start.4 = (bf16[8,512,2,128]{3,2,1,0:T(2,128)(2,1)S(1)}, bf16[8,512,2,128]{3,2,1,0:T(2,128)(2,1)}, u32[]{:S(2)}) copy-start(bf16[8,512,2,128]{3,2,1,0:T(2,128)(2,1)} %param.14) | copy-start | bytes 6291460
  10.5 17.2 %copy-start.5 = (s32[16]{0:T(128)S(1)}, s32[16]{0:T(128)}, u32[]{:S(2)}) copy-start(s32[16]{0:T(128)} %length_ref.1) | copy-start | bytes 196
  10.5 1.6 %collective-permute-start.2 = (bf16[16,4096]{1,0:T(8,128)(2,1)S(1)}, bf16[16,4096]{1,0:T(8,128)(2,1)S(1)}, u32[]{:S(2)}, u32[]{:S(2)}) collective-permute-start(bf16[16,4096]{1,0:T(8,128)(2,1)S(1)} %collective-permute-done.1.chip_ref), channel_id=1, source_target_pairs={{0,1},{1,0},{2,3},{3,2},{4,5},{5,4},{6,7},{7,6},{8,9},{9,8},{10,11... | collective-permute-start | bytes 393224 | tf_op jit(solution)/shard_map/ppermute | solution.py:125
  15.6 4.6 %collective-permute-start.3 = (bf16[16,2304]{1,0:T(8,128)(2,1)S(1)}, bf16[16,2304]{1,0:T(8,128)(2,1)S(1)}, u32[]{:S(2)}, u32[]{:S(2)}) collective-permute-start(bf16[16,2304]{1,0:T(8,128)(2,1)S(1)} %get-tuple-element.18), channel_id=1, source_target_pairs={{0,4},{4,0},{8,12},{12,8},{1,5},{5,1},{9,13},{13,9},{2,6},{6,2},{1... | collective-permute-start | bytes 221192 | tf_op jit(solution)/shard_map/ppermute | solution.py:125
  17.2 9.0 %collective-permute-start.4 = (bf16[16,2304]{1,0:T(8,128)(2,1)S(1)}, bf16[16,2304]{1,0:T(8,128)(2,1)S(1)}, u32[]{:S(2)}, u32[]{:S(2)}) collective-permute-start(bf16[16,2304]{1,0:T(8,128)(2,1)S(1)} %get-tuple-element.19), channel_id=1, source_target_pairs={{0,8},{4,12},{8,0},{12,4},{1,9},{5,13},{9,1},{13,5},{2,10},{6,14},... | collective-permute-start | bytes 221192 | tf_op jit(solution)/shard_map/ppermute | solution.py:125
  19.8 6.4 %collective-permute-start.5 = (bf16[16,2304]{1,0:T(8,128)(2,1)S(1)}, bf16[16,2304]{1,0:T(8,128)(2,1)S(1)}, u32[]{:S(2)}, u32[]{:S(2)}) collective-permute-start(bf16[16,2304]{1,0:T(8,128)(2,1)S(1)} %get-tuple-element.20), channel_id=1, source_target_pairs={{0,12},{4,8},{8,4},{12,0},{1,13},{5,9},{9,5},{13,1},{2,14},{6,10},... | collective-permute-start | bytes 221192 | tf_op jit(solution)/shard_map/ppermute | solution.py:125
  26.4 1.3 %collective-permute-start.6 = (bf16[144,128]{1,0:T(8,128)(2,1)S(1)}, bf16[144,128]{1,0:T(8,128)(2,1)S(1)}, u32[]{:S(2)}, u32[]{:S(2)}) collective-permute-start(bf16[144,128]{1,0:T(8,128)(2,1)S(1)} %get-tuple-element.22), channel_id=1, source_target_pairs={{0,1},{1,0},{2,3},{3,2},{4,5},{5,4},{6,7},{7,6},{8,9},{9,8},{10,11... | collective-permute-start | bytes 110600 | tf_op jit(solution)/shard_map/ppermute | solution.py:125
  31.6 1.3 %collective-permute-start.7 = (bf16[8,2048]{1,0:T(8,128)(2,1)S(1)}, bf16[8,2048]{1,0:T(8,128)(2,1)S(1)}, u32[]{:S(2)}, u32[]{:S(2)}) collective-permute-start(bf16[8,2048]{1,0:T(8,128)(2,1)S(1)} %get-tuple-element.24), channel_id=1, source_target_pairs={{0,1},{1,0},{2,3},{3,2},{4,5},{5,4},{6,7},{7,6},{8,9},{9,8},{10,11... | collective-permute-start | bytes 98312 | tf_op jit(solution)/shard_map/ppermute | solution.py:125
  32.9 10.2 %collective-permute-start.10 = (bf16[16,2048]{1,0:T(8,128)(2,1)S(1)}, bf16[16,2048]{1,0:T(8,128)(2,1)S(1)}, u32[]{:S(2)}, u32[]{:S(2)}) collective-permute-start(bf16[16,2048]{1,0:T(8,128)(2,1)S(1)} %pad_maximum_fusion.a_ref), channel_id=1, source_target_pairs={{0,12},{4,8},{8,4},{12,0},{1,13},{5,9},{9,5},{13,1},{2,14},{6,10},... | collective-permute-start | bytes 196616 | tf_op jit(solution)/shard_map/ppermute | solution.py:125
  35.5 7.6 %collective-permute-start.9 = (bf16[16,2048]{1,0:T(8,128)(2,1)S(1)}, bf16[16,2048]{1,0:T(8,128)(2,1)S(1)}, u32[]{:S(2)}, u32[]{:S(2)}) collective-permute-start(bf16[16,2048]{1,0:T(8,128)(2,1)S(1)} %pad_maximum_fusion.a_ref), channel_id=1, source_target_pairs={{0,8},{4,12},{8,0},{12,4},{1,9},{5,13},{9,1},{13,5},{2,10},{6,14},... | collective-permute-start | bytes 196616 | tf_op jit(solution)/shard_map/ppermute | solution.py:125
  36.0 7.2 %collective-permute-start.8 = (bf16[16,2048]{1,0:T(8,128)(2,1)S(1)}, bf16[16,2048]{1,0:T(8,128)(2,1)S(1)}, u32[]{:S(2)}, u32[]{:S(2)}) collective-permute-start(bf16[16,2048]{1,0:T(8,128)(2,1)S(1)} %pad_maximum_fusion.a_ref), channel_id=1, source_target_pairs={{0,4},{4,0},{8,12},{12,8},{1,5},{5,1},{9,13},{13,9},{2,6},{6,2},{1... | collective-permute-start | bytes 196616 | tf_op jit(solution)/shard_map/ppermute | solution.py:125
  46.2 1.6 %collective-permute-start.11 = (bf16[32,4096]{1,0:T(8,128)(2,1)S(1)}, bf16[32,4096]{1,0:T(8,128)(2,1)S(1)}, u32[]{:S(2)}, u32[]{:S(2)}) collective-permute-start(bf16[32,4096]{1,0:T(8,128)(2,1)S(1)} %get-tuple-element.26), channel_id=1, source_target_pairs={{0,1},{1,0},{2,3},{3,2},{4,5},{5,4},{6,7},{7,6},{8,9},{9,8},{10,11... | collective-permute-start | bytes 786440 | tf_op jit(solution)/shard_map/ppermute | solution.py:125
  47.9 5.6 %collective-permute-start.12 = (bf16[16,4096]{1,0:T(8,128)(2,1)S(1)}, bf16[16,4096]{1,0:T(8,128)(2,1)S(1)}, u32[]{:S(2)}, u32[]{:S(2)}) collective-permute-start(bf16[16,4096]{1,0:T(8,128)(2,1)S(1)} %get-tuple-element.28), channel_id=1, source_target_pairs={{0,2},{2,0},{1,3},{3,1},{4,6},{6,4},{5,7},{7,5},{8,10},{10,8},{9,1... | collective-permute-start | bytes 393224 | tf_op jit(solution)/shard_map/ppermute | solution.py:125

commit v3 on v0

--- a/solution.py
+++ b/solution.py
@@ -1,8 +1,11 @@
+import functools
 import math
 
 import jax
 import jax.numpy as jnp
 from jax import lax
+from jax.experimental import pallas as pl
+from jax.experimental.pallas import tpu as pltpu
 from jax.sharding import PartitionSpec as P
 
 HD = 128
@@ -62,7 +65,7 @@
     return attended.astype(jnp.bfloat16).reshape(seq_count, combined_width)
 
 
-def body(tokens, q_weight, k_weight, v_weight, o_weight, cache_keys, cache_values, lengths):
+def general_body(tokens, q_weight, k_weight, v_weight, o_weight, cache_keys, cache_values, lengths):
     gathered = lax.all_gather(tokens, ("narrow", "sub"), axis=0, tiled=True)
     q_cols = q_weight.shape[1]
     kv_cols = k_weight.shape[1]
@@ -109,9 +112,404 @@
     return total.astype(jnp.bfloat16)
 
 
+VMEM_SPEC = pl.BlockSpec(memory_space=pltpu.VMEM)
+SMEM_SPEC = pl.BlockSpec(memory_space=pltpu.SMEM)
+ANY_SPEC = pl.BlockSpec(memory_space=pl.ANY)
+MIB = 2**20
+STEP = 512
+FIRST_Q, PIECE_Q = 2560, 512
+FIRST_O = 1536
+ROOM = 42
+ROOM_Q = 38
+
+
+def vmem(mib):
+    return pltpu.CompilerParams(vmem_limit_bytes=mib * MIB)
+
+
+def cost(flops, moved):
+    return pl.CostEstimate(flops=flops, bytes_accessed=moved, transcendentals=0)
+
+
+def exchange(array, axis, bit):
+    size = lax.axis_size(axis)
+    return lax.ppermute(array, axis, [(i, i ^ bit) for i in range(size)])
+
+
+def fetch_kernel(weight_ref, *refs, start, axis):
+    out_ref, mark_ref, sem = refs[-3:]
+    cut = pl.ds(start, out_ref.shape[axis])
+    source = weight_ref.at[cut] if axis == 0 else weight_ref.at[:, cut]
+    copy = pltpu.make_async_copy(source, out_ref, sem)
+    copy.start()
+    mark_ref[...] = jnp.zeros_like(mark_ref)
+    copy.wait()
+
+
+def fetch(weight, axis, start, count, *after):
+    shape = (count, weight.shape[1]) if axis == 0 else (weight.shape[0], count)
+    return pl.pallas_call(
+        functools.partial(fetch_kernel, start=start, axis=axis),
+        out_shape=[pltpu.VMEM(shape, weight.dtype), jax.ShapeDtypeStruct((8, 128), jnp.float32)],
+        in_specs=[ANY_SPEC] * (1 + len(after)),
+        out_specs=[VMEM_SPEC] * 2,
+        scratch_shapes=[pltpu.SemaphoreType.DMA],
+        compiler_params=vmem(ROOM),
+        cost_estimate=cost(0, shape[0] * shape[1] * 2),
+        name="fetch",
+    )(weight, *after)
+
+
+def split_cache(which_head, keys_ref, values_ref, out_ref, wide_rows):
+    seqs, rows, _ = keys_ref.shape
+    slots = rows // 2
+    for which, ref in enumerate((keys_ref, values_ref)):
+        for i in range(seqs):
+            slot = i % wide_rows.shape[0]
+            wide_rows[slot] = ref[i].astype(jnp.float32)
+            out_ref[which, i * slots : (i + 1) * slots, :] = wide_rows[
+                slot, pl.ds(which_head, slots, stride=2), :
+            ].astype(out_ref.dtype)
+
+
+def partner_kernel(keys_ref, values_ref, after_ref, out_ref, wide_rows):
+    del after_ref
+    split_cache(1 - lax.axis_index("sub"), keys_ref, values_ref, out_ref, wide_rows)
+
+
+def partner_cache(keys, values, after):
+    seqs, rows, _ = keys.shape
+    return pl.pallas_call(
+        partner_kernel,
+        out_shape=pltpu.VMEM((2, seqs * rows // 2, HD), keys.dtype),
+        in_specs=[VMEM_SPEC] * 2 + [ANY_SPEC],
+        out_specs=VMEM_SPEC,
+        scratch_shapes=[pltpu.VMEM((4, rows, HD), jnp.float32)],
+        compiler_params=vmem(4),
+        cost_estimate=cost(10**9, 0),
+        name="partner_cache",
+    )(keys, values, after)
+
+
+def prepare_kernel(
+    length_ref, weight_ref, keys_ref, values_ref, after_ref,
+    part_ref, own_ref, cos_ref, sin_ref, wide_rows, sem,
+):
+    del after_ref
+    copy = pltpu.make_async_copy(weight_ref.at[:, pl.ds(0, part_ref.shape[1])], part_ref, sem)
+    copy.start()
+    seqs, width = cos_ref.shape
+    lane = lax.broadcasted_iota(jnp.int32, (seqs, width), 1)
+    row = lax.broadcasted_iota(jnp.int32, (seqs, width), 0)
+    place = jnp.where(lane < width // 2, lane, lane - width // 2).astype(jnp.float32)
+    position = jnp.zeros((seqs, width), jnp.float32)
+    for i in range(seqs):
+        position = jnp.where(row == i, length_ref[i].astype(jnp.float32), position)
+    angles = position * jnp.exp(-math.log(rope_base) * (place * (2.0 / width)))
+    sine = jnp.sin(angles)
+    cos_ref[...] = jnp.cos(angles)
+    sin_ref[...] = jnp.where(lane < width // 2, -sine, sine)
+    split_cache(lax.axis_index("sub"), keys_ref, values_ref, own_ref, wide_rows)
+    copy.wait()
+
+
+def prepare(lengths, weight, columns, keys, values, after):
+    seqs, rows, _ = keys.shape
+    factors = jax.ShapeDtypeStruct((lengths.shape[0], HD), jnp.float32)
+    return pl.pallas_call(
+        prepare_kernel,
+        out_shape=[
+            pltpu.VMEM((weight.shape[0], columns), weight.dtype),
+            pltpu.VMEM((2, seqs * rows // 2, HD), keys.dtype),
+            factors,
+            factors,
+        ],
+        in_specs=[SMEM_SPEC, ANY_SPEC, VMEM_SPEC, VMEM_SPEC, ANY_SPEC],
+        out_specs=[VMEM_SPEC] * 4,
+        scratch_shapes=[
+            pltpu.VMEM((4, rows, HD), jnp.float32),
+            pltpu.SemaphoreType.DMA,
+        ],
+        compiler_params=vmem(ROOM - 8),
+        cost_estimate=cost(10**9, weight.shape[0] * columns * 2),
+        name="prepare",
+    )(lengths, weight, keys, values, after)
+
+
+def project_kernel(
+    own_ref, core_ref, chip_ref, both_ref, first_ref, k_ref, v_ref, q_ref, after_ref, *refs
+):
+    del after_ref
+    outs, (rows_scratch, rest, total, sems) = refs[:4], refs[4:]
+    narrow, sub, wide = lax.axis_index("narrow"), lax.axis_index("sub"), lax.axis_index("wide")
+    depth, columns = q_ref.shape
+    early = first_ref.shape[0]
+    head = pl.multiple_of(sub * HD, HD)
+    pieces = range(early, depth, PIECE_Q)
+    copies = [
+        pltpu.make_async_copy(
+            q_ref.at[pl.ds(start, PIECE_Q)], rest.at[pl.ds(start - early, PIECE_Q)], sems.at[j]
+        )
+        for j, start in enumerate(pieces)
+    ]
+    for copy in copies:
+        copy.start()
+    mine = (narrow * 2 + sub) ^ wide
+    rows = own_ref.shape[0]
+    for m, ref in enumerate((own_ref, core_ref, chip_ref, both_ref)):
+        place = pl.multiple_of((mine ^ m) * rows, rows)
+        rows_scratch[pl.ds(place, rows), :] = ref[...]
+
+    def part(start, block):
+        tokens = rows_scratch[:, start : start + block.shape[0]]
+        return jnp.dot(tokens, block, preferred_element_type=jnp.float32)
+
+    def store(product, start):
+        for place, out in enumerate(outs):
+            out[:, start : start + product.shape[1]] = product[
+                place * rows : (place + 1) * rows
+            ].astype(out.dtype)
+
+    cuts = [slice(start, start + STEP) for start in range(0, columns, STEP)]
+    for cut in cuts:
+        total[:, cut] = part(0, first_ref[:, cut])
+    side = [ref[:, pl.ds(head, HD)] for ref in (k_ref, v_ref)]
+    store(part(0, jnp.concatenate(side, axis=1)), columns)
+    for j, (start, copy) in enumerate(zip(pieces, copies)):
+        copy.wait()
+        for cut in cuts:
+            product = total[:, cut] + part(start, rest[j * PIECE_Q : (j + 1) * PIECE_Q, cut])
+            if start + PIECE_Q < depth:
+                total[:, cut] = product
+            else:
+                store(product, cut.start)
+
+
+def project(own, core, chip, both, first, k_weight, v_weight, q_weight, after):
+    rows, depth = own.shape
+    late = depth - first.shape[0]
+    columns = q_weight.shape[1]
+    return pl.pallas_call(
+        project_kernel,
+        out_shape=[jax.ShapeDtypeStruct((rows, columns + 2 * HD), jnp.bfloat16)] * 4,
+        in_specs=[VMEM_SPEC] * 7 + [ANY_SPEC] * 2,
+        out_specs=[VMEM_SPEC] * 4,
+        scratch_shapes=[
+            pltpu.VMEM((4 * rows, depth), jnp.bfloat16),
+            pltpu.VMEM((late, columns), jnp.bfloat16),
+            pltpu.VMEM((4 * rows, columns), jnp.float32),
+            pltpu.SemaphoreType.DMA((late // PIECE_Q,)),
+        ],
+        compiler_params=vmem(ROOM_Q),
+        cost_estimate=cost(4 * 2 * 4 * rows * depth * columns, 0),
+        name="project",
+    )(own, core, chip, both, first, k_weight, v_weight, q_weight, after)
+
+
+def attend_kernel(
+    length_ref, a_ref, b_ref, c_ref, d_ref, cos_ref, sin_ref, own_ref, other_ref, after_ref,
+    out_ref, turned, queries, scores, weights, mixed,
+):
+    del after_ref
+    sub = lax.axis_index("sub")
+    seqs, columns = a_ref.shape
+    half = seqs // 2
+    heads = (columns - 2 * HD) // HD
+    slots = own_ref.shape[1] // half
+    rows = seqs * heads
+    cos, sin = cos_ref[...], sin_ref[...]
+
+    def total(index):
+        cut = slice(index * HD, (index + 1) * HD)
+        return (a_ref[:, cut].astype(jnp.float32) + b_ref[:, cut].astype(jnp.float32)) + (
+            c_ref[:, cut].astype(jnp.float32) + d_ref[:, cut].astype(jnp.float32)
+        )
+
+    def turn(rows_in):
+        return rows_in * cos + pltpu.roll(rows_in, HD // 2, 1) * sin
+
+    for head in range(heads):
+        turned[head * seqs : (head + 1) * seqs, :] = turn(total(head))
+    new_keys = turn(total(heads)).astype(jnp.bfloat16)
+    new_values = total(heads + 1).astype(jnp.bfloat16)
+    for seq in range(seqs):
+        queries[seq * heads : (seq + 1) * heads, :] = turned[
+            pl.ds(seq, heads, stride=seqs), :
+        ].astype(jnp.bfloat16)
+    scale = 1.0 / math.sqrt(HD)
+    column = lax.broadcasted_iota(jnp.int32, (heads, slots), 1)
+    across = (((1,), (1,)), ((), ()))
+    places = [sub * half + i for i in range(half)] + [(1 - sub) * half + i for i in range(half)]
+    blocks = [(ref, i) for ref in (own_ref, other_ref) for i in range(half)]
+    for place, (ref, i) in zip(places, blocks):
+        at = pl.multiple_of(place * heads, heads)
+        product = lax.dot_general(
+            queries[pl.ds(at, heads), :],
+            ref[0, i * slots : (i + 1) * slots, :],
+            across,
+            preferred_element_type=jnp.float32,
+        )
+        scores[pl.ds(at, heads), :] = jnp.where(
+            column < length_ref[place], product * scale, -1e30
+        )
+    own_column = lax.broadcasted_iota(jnp.int32, (rows, seqs), 1)
+    own_row = lax.broadcasted_iota(jnp.int32, (rows, seqs), 0) // heads
+    diagonal = own_column == own_row
+    own_product = lax.dot_general(
+        queries[...], new_keys, across, preferred_element_type=jnp.float32
+    )
+    own_scores = jnp.sum(
+        jnp.where(diagonal, own_product, 0.0), axis=1, keepdims=True
+    ) * scale
+    own_weights = []
+    chunk = 4 * heads
+    for start in range(0, rows, chunk):
+        block = scores[start : start + chunk, :]
+        own = own_scores[start : start + chunk]
+        highest = jnp.maximum(jnp.max(block, axis=1, keepdims=True), own)
+        terms = jnp.exp(block - highest)
+        own_term = jnp.exp(own - highest)
+        inverse = 1.0 / (jnp.sum(terms, axis=1, keepdims=True) + own_term)
+        weights[start : start + chunk, :] = (terms * inverse).astype(jnp.bfloat16)
+        own_weights.append(own_term * inverse)
+    own_weights = jnp.where(diagonal, jnp.concatenate(own_weights, axis=0), 0.0)
+    scores[:, :HD] = jnp.dot(
+        own_weights.astype(jnp.bfloat16), new_values, preferred_element_type=jnp.float32
+    )
+    for place, (ref, i) in zip(places, blocks):
+        at = pl.multiple_of(place * heads, heads)
+        result = jnp.dot(
+            weights[pl.ds(at, heads), :],
+            ref[1, i * slots : (i + 1) * slots, :],
+            preferred_element_type=jnp.float32,
+        )
+        mixed[pl.ds(place, heads, stride=seqs), :] = result + scores[pl.ds(at, heads), :HD]
+    for head in range(heads):
+        out_ref[:, head * HD : (head + 1) * HD] = mixed[
+            head * seqs : (head + 1) * seqs, :
+        ].astype(out_ref.dtype)
+
+
+def attend_here(lengths, parts, cos, sin, own, other, after):
+    seqs, columns = parts[0].shape
+    heads = columns // HD - 2
+    slots = own.shape[1] * 2 // seqs
+    rows = seqs * heads
+    return pl.pallas_call(
+        attend_kernel,
+        out_shape=jax.ShapeDtypeStruct((seqs, heads * HD), jnp.bfloat16),
+        in_specs=[SMEM_SPEC] + [VMEM_SPEC] * 8 + [ANY_SPEC],
+        out_specs=VMEM_SPEC,
+        scratch_shapes=[
+            pltpu.VMEM((rows, HD), jnp.float32),
+            pltpu.VMEM((rows, HD), jnp.bfloat16),
+            pltpu.VMEM((rows, slots), jnp.float32),
+            pltpu.VMEM((rows, slots), jnp.bfloat16),
+            pltpu.VMEM((rows, HD), jnp.float32),
+        ],
+        compiler_params=vmem(8),
+        cost_estimate=cost(4 * 10**9, 0),
+        name="attend",
+    )(lengths, *parts, cos, sin, own, other, after)
+
+
+def output_kernel(
+    a_ref, b_ref, c_ref, d_ref, first_ref, second_ref, keep_ref, send_ref, rows_scratch
+):
+    narrow, sub, wide = lax.axis_index("narrow"), lax.axis_index("sub"), lax.axis_index("wide")
+    mine = (narrow * 2 + sub) ^ wide
+    rows = a_ref.shape[0]
+    for k, ref in enumerate((a_ref, b_ref, c_ref, d_ref)):
+        m = mine ^ k
+        place = pl.multiple_of(((m & 1) * 2 + (m >> 1)) * rows, rows)
+        rows_scratch[pl.ds(place, rows), :] = ref[...]
+    mixed = rows_scratch[...]
+
+    done = 0
+    for ref in (first_ref, second_ref):
+        for start in range(0, ref.shape[1], STEP):
+            product = jnp.dot(
+                mixed, ref[:, start : start + STEP], preferred_element_type=jnp.float32
+            )
+            cut = slice(done + start, done + start + STEP)
+            keep_ref[:, cut] = product[: 2 * rows]
+            send_ref[:, cut] = product[2 * rows :].astype(send_ref.dtype)
+        done += ref.shape[1]
+
+
+def output(blocks, first_part, second_part):
+    rows, depth = blocks[0].shape
+    columns = first_part.shape[1] + second_part.shape[1]
+    return pl.pallas_call(
+        output_kernel,
+        out_shape=[
+            jax.ShapeDtypeStruct((2 * rows, columns), jnp.float32),
+            jax.ShapeDtypeStruct((2 * rows, columns), jnp.bfloat16),
+        ],
+        in_specs=[VMEM_SPEC] * 6,
+        out_specs=[VMEM_SPEC] * 2,
+        scratch_shapes=[pltpu.VMEM((4 * rows, depth), jnp.bfloat16)],
+        compiler_params=vmem(6),
+        name="output",
+    )(*blocks, first_part, second_part)
+
+
+def add_kernel(keep_ref, other_ref, mine_ref, send_ref):
+    rows = mine_ref.shape[0]
+    total = keep_ref[...] + other_ref[...].astype(jnp.float32)
+    mine_ref[...] = total[:rows]
+    send_ref[...] = total[rows:].astype(send_ref.dtype)
+
+
+def add_halves(keep, other):
+    rows, columns = keep.shape[0] // 2, keep.shape[1]
+    return pl.pallas_call(
+        add_kernel,
+        out_shape=[
+            jax.ShapeDtypeStruct((rows, columns), jnp.float32),
+            jax.ShapeDtypeStruct((rows, columns), jnp.bfloat16),
+        ],
+        in_specs=[VMEM_SPEC] * 2,
+        out_specs=[VMEM_SPEC] * 2,
+        compiler_params=vmem(4),
+        name="add_halves",
+    )(keep, other)
+
+
+def direct_body(
+    tokens, q_weight, k_weight, v_weight, o_weight, cache_keys, cache_values, lengths
+):
+    seqs, slots, kv_heads, _ = cache_keys.shape
+    keys = cache_keys.reshape(seqs, slots * kv_heads, HD)
+    values = cache_values.reshape(seqs, slots * kv_heads, HD)
+    chip = exchange(tokens, "narrow", 1)
+    core = exchange(tokens, "sub", 1)
+    q_first, mark = fetch(q_weight, 0, 0, FIRST_Q)
+    chip, mark = lax.optimization_barrier((chip, mark))
+    both = exchange(chip, "sub", 1)
+    parts = project(tokens, core, chip, both, q_first, k_weight, v_weight, q_weight, mark)
+    parts = [parts[0]] + [exchange(parts[k], "wide", k) for k in (1, 2, 3)]
+    send_cache = partner_cache(keys, values, parts[0])
+    other_cache = exchange(send_cache, "sub", 1)
+    o_first, own_cache, cosine, sine = prepare(
+        lengths, o_weight, FIRST_O, keys, values, send_cache
+    )
+    mixed = attend_here(lengths, parts, cosine, sine, own_cache, other_cache, o_first)
+    o_second, _ = fetch(o_weight, 1, FIRST_O, o_weight.shape[1] - FIRST_O, mixed)
+    blocks = [mixed] + [exchange(mixed, "wide", k) for k in (1, 2, 3)]
+    keep, send = output(blocks, o_first, o_second)
+    mine, send = add_halves(keep, exchange(send, "sub", 1))
+    return (mine + exchange(send, "narrow", 1).astype(jnp.float32)).astype(jnp.bfloat16)
+
+
+def body_for(mesh):
+    sizes = tuple(mesh.shape[name] for name in ("wide", "narrow", "sub"))
+    return direct_body if sizes == (4, 2, 2) else general_body
+
+
 def solution(mesh):
     return jax.shard_map(
-        body,
+        body_for(mesh),
         mesh=mesh,
         in_specs=(
             P(("groups", "narrow", "sub"), "wide"),

time: 123 us -> 46.8 us (0.38)
  waiting for transfers between devices: 48.1 us -> 9.61 us
  blocking collectives: 26.7 us -> 0 us
  matrix products: 22.6 us -> 0 us
  Pallas kernels: 0 us -> 21.5 us
  between operations: 13.6 us -> 0.14 us
  starting transfers between devices: 3.34 us -> 14.1 us
  local copies, waits for them, and re-layouts: 4.33 us -> 0.52 us
  other arithmetic: 3.39 us -> 0.68 us
    reduce_scatter x2 -> x0, waiting for transfers between devices: 46.8 us -> none  [the longest x1 23.9 us: body(): lax.psum_scatter(partial_value, ('narrow', 'sub'), scatter_dimension=0, t...]
    all_gather x2 -> x0, blocking collectives: 22.9 us -> none  [the longest x1 14 us: body(): lax.all_gather(returned, 'wide', axis=0, tiled=True)]
    dot_general x7 -> x0, matrix products: 22.6 us -> none  [the longest x1 9.77 us: body(): jnp.dot(lax.all_gather(returned, 'wide', axis=0, tiled=True), o_weight, p...]
    pallas_call x0 -> x8, Pallas kernels: none -> 21.5 us  [the longest x2 8.57 us: fetch(): pl.pallas_call(functools.partial(fetch_kernel, start=start, axis=axis), o...]
    ppermute x0 -> x12, starting transfers between devices: none -> 14.1 us  [exchange(): return lax.ppermute(array, axis, [(i, i ^ bit) for i in range(size)])]
    ppermute x0 -> x12, waiting for transfers between devices: none -> 9.61 us  [exchange(): return lax.ppermute(array, axis, [(i, i ^ bit) for i in range(size)])]
    all_to_all x1 -> x0, blocking collectives: 3.79 us -> none  [body(): lax.all_to_all(attention, 'sub', split_axis=1, concat_axis=0, tiled=True)]
    all_to_all x1 -> x0, starting transfers between devices: 3.3 us -> none  [body(): lax.all_to_all(queries, 'sub', split_axis=0, concat_axis=1, tiled=True)]
  transfers between devices with their start and end apart: 3 -> 12, of which waited for: 3 -> 4; matrix products, arithmetic and copies ran while one was open for 0% -> 0% of each run, Pallas kernels for 0% -> 26%
where the time goes in v3:
time: 46.8 us; the launch traced here: 46.6 us
  Pallas kernels  21.5 us (46%)
  starting transfers between devices  14.1 us (30%)
  waiting for transfers between devices  9.61 us (21%)
  other arithmetic  0.68 us (1%)
  local copies, waits for them, and re-layouts  0.52 us (1%)
    ppermute x12, starting transfers between devices, exchange(): return lax.ppermute(array, axis, [(i, i ^ bit) for i in range(size)])  14.1 us
    ppermute x12, waiting for transfers between devices, exchange(): return lax.ppermute(array, axis, [(i, i ^ bit) for i in range(size)])  9.61 us
    pallas_call x2, Pallas kernels, fetch(): pl.pallas_call(functools.partial(fetch_kernel, start=start, axis=axis), o...  8.57 us
    pallas_call x1, Pallas kernels, project(): pl.pallas_call(project_kernel, out_shape=[jax.ShapeDtypeStruct((rows, col...  3.57 us
    pallas_call x1, Pallas kernels, prepare(): pl.pallas_call(prepare_kernel, out_shape=[pltpu.VMEM((weight.shape[0], co...  3.33 us
    pallas_call x1, Pallas kernels, output(): pl.pallas_call(output_kernel, out_shape=[jax.ShapeDtypeStruct((2 * rows,...  3 us
    pallas_call x1, Pallas kernels, attend_here(): pl.pallas_call(attend_kernel, out_shape=jax.ShapeDtypeStruct((seqs, heads...  2.07 us
  transfers between devices with their start and end apart: 12, of which 4 were waited for; matrix products, arithmetic and copies ran while one was open for 0% of the time, Pallas kernels for 26%

profile of v3, /device:TPU:0, one launch (start us, length us, event | category | flops | bytes accessed | tf_op | source)
XLA Modules:
  0.0 46.6 jit_solution(16825609405970349868)
XLA Ops:
  0.0 0.0 copy-start.6
  0.0 0.0 copy-start.5
  0.0 0.0 copy-start.4
  0.0 3.0 %collective-permute-start.1 = (bf16[16,4096]{1,0:T(8,128)(2,1)}, bf16[16,4096]{1,0:T(8,128)(2,1)S(1)}, u32[]{:S(2)}, u32[]{:S(2)}) collective-permute-start(bf16[16,4096]{1,0:T(8,128)(2,1)} %own_ref.1), channel_id=1, source_target_pairs={{0,2},{2,0},{1,3},{3,1},{4,6},{6,4},{5,7},{7,5},{8,10},{10,8},{9,1... | collective-permute-start | bytes 393224 | tf_op jit(solution)/shard_map/ppermute | solution.py:136
  3.0 0.0 collective-permute-start
  3.0 4.0 %fetch.2 = (bf16[2560,2048]{1,0:T(8,128)(2,1)S(1)}, f32[8,128]{1,0:T(8,128)S(1)}) custom-call(bf16[4096,2048]{1,0:T(8,128)(2,1)} %q_ref.1), custom_call_target="tpu_custom_call" | custom-call | bytes 10485760 | tf_op jit(solution)/shard_map/fetch/pallas_call | solution.py:151
  7.0 0.0 collective-permute-done.1.chip_ref
  7.0 0.6 %collective-permute-start.2 = (bf16[16,4096]{1,0:T(8,128)(2,1)S(1)}, bf16[16,4096]{1,0:T(8,128)(2,1)S(1)}, u32[]{:S(2)}, u32[]{:S(2)}) collective-permute-start(bf16[16,4096]{1,0:T(8,128)(2,1)S(1)} %collective-permute-done.1.chip_ref), channel_id=1, source_target_pairs={{0,1},{1,0},{2,3},{3,2},{4,5},{5,4},{6,7},{7,6},{8,9},{9,8},{10,11... | collective-permute-start | bytes 393224 | tf_op jit(solution)/shard_map/ppermute | solution.py:136
  7.6 0.0 collective-permute-done.core_ref
  7.6 1.0 %collective-permute-done.2.both_ref = bf16[16,4096]{1,0:T(8,128)(2,1)S(1)} collective-permute-done((bf16[16,4096]{1,0:T(8,128)(2,1)S(1)}, bf16[16,4096]{1,0:T(8,128)(2,1)S(1)}, u32[]{:S(2)}, u32[]{:S(2)}) %collective-permute-start.2) | collective-permute-done | bytes 131104 | tf_op jit(solution)/shard_map/ppermute | solution.py:136
  8.6 0.0 copy-done.6
  8.6 0.0 copy-done.5
  8.6 0.0 copy-done.4
  8.6 0.0 copy-start
  8.6 0.0 copy-start.2
  8.6 3.6 %project.1 = (bf16[16,2304]{1,0:T(8,128)(2,1)S(1)}, bf16[16,2304]{1,0:T(8,128)(2,1)S(1)}, bf16[16,2304]{1,0:T(8,128)(2,1)S(1)}, bf16[16,2304]{1,0:T(8,128)(2,1)S(1)}) custom-call(bf16[16,4096]{1,0:T(8,128)(2,1)S(1)} %copy-done.6, bf16[16,4096]{1,0:T(8,128)(2,1)S(1)} %collective-permute-done.core_ref, bf16[16,4096]{1,0:T(8,128)(2,1)S(1)} %collective-permute-done.1.chip_ref, ...), custom_call_target="tpu_custom_call" | custom-call | flops 4294967296 | tf_op jit(solution)/shard_map/project/pallas_call | solution.py:292
  12.2 0.0 copy-done
  12.2 0.5 %copy-done.2 = bf16[8,512,2,128]{3,2,1,0:T(2,128)(2,1)S(1)} copy-done((bf16[8,512,2,128]{3,2,1,0:T(2,128)(2,1)S(1)}, bf16[8,512,2,128]{3,2,1,0:T(2,128)(2,1)}, u32[]{:S(2)}) %copy-start.2) | copy-done | bytes 2097176
  12.7 0.0 copy-start.1
  12.7 0.0 copy-start.3
  12.7 0.0 copy-start.7
  12.7 0.9 %partner_cache.1.after_ref = bf16[2,4096,128]{2,1,0:T(8,128)(2,1)S(1)} custom-call(bf16[8,1024,128]{2,1,0:T(8,128)(2,1)S(1)} %bitcast.2, bf16[8,1024,128]{2,1,0:T(8,128)(2,1)S(1)} %bitcast.4, bf16[16,2304]{1,0:T(8,128)(2,1)S(1)} %get-tuple-element.26.after_ref.a_ref), custom_call_target="tpu_custom_call" | custom-call | flops 1000000000 | tf_op jit(solution)/shard_map/partner_cache/pallas_call | solution.py:182
  13.6 0.4 collective-permute-start.6
  14.0 1.6 %collective-permute-start.3 = (bf16[16,2304]{1,0:T(8,128)(2,1)S(1)}, bf16[16,2304]{1,0:T(8,128)(2,1)S(1)}, u32[]{:S(2)}, u32[]{:S(2)}) collective-permute-start(bf16[16,2304]{1,0:T(8,128)(2,1)S(1)} %get-tuple-element.27), channel_id=1, source_target_pairs={{0,4},{4,0},{8,12},{12,8},{1,5},{5,1},{9,13},{13,9},{2,6},{6,2},{1... | collective-permute-start | bytes 221192 | tf_op jit(solution)/shard_map/ppermute | solution.py:136
  15.6 2.6 %collective-permute-start.4 = (bf16[16,2304]{1,0:T(8,128)(2,1)S(1)}, bf16[16,2304]{1,0:T(8,128)(2,1)S(1)}, u32[]{:S(2)}, u32[]{:S(2)}) collective-permute-start(bf16[16,2304]{1,0:T(8,128)(2,1)S(1)} %get-tuple-element.28), channel_id=1, source_target_pairs={{0,8},{4,12},{8,0},{12,4},{1,9},{5,13},{9,1},{13,5},{2,10},{6,14},... | collective-permute-start | bytes 221192 | tf_op jit(solution)/shard_map/ppermute | solution.py:136
  18.2 0.2 collective-permute-start.5
  18.4 0.0 copy-done.1
  18.4 0.0 copy-done.3
  18.4 0.0 copy-done.7
  18.4 3.3 %prepare.1 = (bf16[2048,1536]{1,0:T(8,128)(2,1)S(1)}, bf16[2,4096,128]{2,1,0:T(8,128)(2,1)S(1)}, f32[16,128]{1,0:T(8,128)S(1)}, f32[16,128]{1,0:T(8,128)S(1)}) custom-call(s32[16]{0:T(128)S(1)} %copy-done.7, bf16[2048,4096]{1,0:T(8,128)(2,1)} %weight_ref.5, bf16[8,1024,128]{2,1,0:T(8,128)(2,1)S(1)} %bitcast.3, bf16[8,1024,128]{2,1,0:T(8,128)(2,1)S(1)} %bitcast.5, ...), custom_call_target="tpu_custom_call" | custom-call | flops 1000000000 | bytes 6291456 | tf_op jit(solution)/shard_map/prepare/pallas_call | solution.py:219
  21.8 0.0 collective-permute-done.3.b_ref
  21.8 2.7 %collective-permute-done.4.c_ref = bf16[16,2304]{1,0:T(8,128)(2,1)S(1)} collective-permute-done((bf16[16,2304]{1,0:T(8,128)(2,1)S(1)}, bf16[16,2304]{1,0:T(8,128)(2,1)S(1)}, u32[]{:S(2)}, u32[]{:S(2)}) %collective-permute-start.4) | collective-permute-done | bytes 73760 | tf_op jit(solution)/shard_map/ppermute | solution.py:136
  24.5 0.0 collective-permute-done.5.d_ref
  24.5 0.0 collective-permute-done.6.other_ref
  24.5 2.1 %attend.1.refs_0_.a_ref = bf16[16,2048]{1,0:T(8,128)(2,1)S(1)} custom-call(s32[16]{0:T(128)S(1)} %copy-done.7, bf16[16,2304]{1,0:T(8,128)(2,1)S(1)} %get-tuple-element.26.after_ref.a_ref, bf16[16,2304]{1,0:T(8,128)(2,1)S(1)} %collective-permute-done.3.b_ref, bf16[16,2304]{1,0:T(8,128)(2,1)S(1)} %collective-permute-done.4.c_ref, ...), custom_call_target="tpu_custom_call" | custom-call | flops 4000000000 | tf_op jit(solution)/shard_map/attend/pallas_call | solution.py:398
  26.6 2.6 %collective-permute-start.9 = (bf16[16,2048]{1,0:T(8,128)(2,1)S(1)}, bf16[16,2048]{1,0:T(8,128)(2,1)S(1)}, u32[]{:S(2)}, u32[]{:S(2)}) collective-permute-start(bf16[16,2048]{1,0:T(8,128)(2,1)S(1)} %attend.1.refs_0_.a_ref), channel_id=1, source_target_pairs={{0,12},{4,8},{8,4},{12,0},{1,13},{5,9},{9,5},{13,1},{2,14},{6,10},... | collective-permute-start | bytes 196616 | tf_op jit(solution)/shard_map/ppermute | solution.py:136
  29.1 0.4 collective-permute-start.8
  29.5 1.5 %collective-permute-start.7 = (bf16[16,2048]{1,0:T(8,128)(2,1)S(1)}, bf16[16,2048]{1,0:T(8,128)(2,1)S(1)}, u32[]{:S(2)}, u32[]{:S(2)}) collective-permute-start(bf16[16,2048]{1,0:T(8,128)(2,1)S(1)} %attend.1.refs_0_.a_ref), channel_id=1, source_target_pairs={{0,4},{4,0},{8,12},{12,8},{1,5},{5,1},{9,13},{13,9},{2,6},{6,2},{1... | collective-permute-start | bytes 196616 | tf_op jit(solution)/shard_map/ppermute | solution.py:136
  31.0 4.6 %fetch.3 = (bf16[2048,2560]{1,0:T(8,128)(2,1)S(1)}, f32[8,128]{1,0:T(8,128)}) custom-call(bf16[2048,4096]{1,0:T(8,128)(2,1)} %weight_ref.5, bf16[16,2048]{1,0:T(8,128)(2,1)S(1)} %attend.1.refs_0_.a_ref), custom_call_target="tpu_custom_call" | custom-call | bytes 10485760 | tf_op jit(solution)/shard_map/fetch/pallas_call | solution.py:151
  35.6 0.0 collective-permute-done.9.d_ref
  35.6 0.0 collective-permute-done.8.c_ref
  35.6 0.0 collective-permute-done.7.b_ref
  35.6 3.0 %output.1 = (f32[32,4096]{1,0:T(8,128)S(1)}, bf16[32,4096]{1,0:T(8,128)(2,1)S(1)}) custom-call(bf16[16,2048]{1,0:T(8,128)(2,1)S(1)} %attend.1.refs_0_.a_ref, bf16[16,2048]{1,0:T(8,128)(2,1)S(1)} %collective-permute-done.7.b_ref, bf16[16,2048]{1,0:T(8,128)(2,1)S(1)} %collective-permute-done.8.c_ref, bf16[16,2048]{1,0:T(8,128)(2,1)S(1)} %collective-permute-done.9.d_ref, ...), custom_call_target="tpu_custom_call" | custom-call | tf_op jit(solution)/shard_map/output/pallas_call | solution.py:443
  38.6 0.1 collective-permute-start.10
  38.7 1.5 %collective-permute-done.10.other_ref = bf16[32,4096]{1,0:T(8,128)(2,1)S(1)} collective-permute-done((bf16[32,4096]{1,0:T(8,128)(2,1)S(1)}, bf16[32,4096]{1,0:T(8,128)(2,1)S(1)}, u32[]{:S(2)}, u32[]{:S(2)}) %collective-permute-start.10) | collective-permute-done | bytes 262176 | tf_op jit(solution)/shard_map/ppermute | solution.py:136
  40.3 1.2 %collective-permute-start.11 = (bf16[16,4096]{1,0:T(8,128)(2,1)S(1)}, bf16[16,4096]{1,0:T(8,128)(2,1)S(1)}, u32[]{:S(2)}, u32[]{:S(2)}) collective-permute-start(bf16[16,4096]{1,0:T(8,128)(2,1)S(1)} %get-tuple-element.38), channel_id=1, source_target_pairs={{0,2},{2,0},{1,3},{3,1},{4,6},{6,4},{5,7},{7,5},{8,10},{10,8},{9,1... | collective-permute-start | bytes 393224 | tf_op jit(solution)/shard_map/ppermute | solution.py:136
  41.5 4.4 %collective-permute-done.11 = bf16[16,4096]{1,0:T(8,128)(2,1)S(1)} collective-permute-done((bf16[16,4096]{1,0:T(8,128)(2,1)S(1)}, bf16[16,4096]{1,0:T(8,128)(2,1)S(1)}, u32[]{:S(2)}, u32[]{:S(2)}) %collective-permute-start.11) | collective-permute-done | bytes 131104 | tf_op jit(solution)/shard_map/ppermute | solution.py:136
  45.9 0.7 %add_convert_fusion = bf16[16,4096]{1,0:T(8,128)(2,1)} fusion(f32[16,4096]{1,0:T(8,128)S(1)} %get-tuple-element.37, bf16[16,4096]{1,0:T(8,128)(2,1)S(1)} %collective-permute-done.11), kind=kLoop, calls=%fused_computation | loop fusion | flops 196608 | bytes 524288 | tf_op jit(solution)/shard_map/convert_element_type | solution.py:502
  (1 shorter events, 0.0 us)
Async XLA Ops:
  0.0 8.6 %copy-start.6 = (bf16[16,4096]{1,0:T(8,128)(2,1)S(1)}, bf16[16,4096]{1,0:T(8,128)(2,1)}, u32[]{:S(2)}) copy-start(bf16[16,4096]{1,0:T(8,128)(2,1)} %own_ref.1) | copy-start | bytes 393220
  0.0 8.6 %copy-start.5 = (bf16[4096,256]{1,0:T(8,128)(2,1)S(1)}, bf16[4096,256]{1,0:T(8,128)(2,1)}, u32[]{:S(2)}) copy-start(bf16[4096,256]{1,0:T(8,128)(2,1)} %v_ref.1) | copy-start | bytes 6291460
  0.0 8.6 %copy-start.4 = (bf16[4096,256]{1,0:T(8,128)(2,1)S(1)}, bf16[4096,256]{1,0:T(8,128)(2,1)}, u32[]{:S(2)}) copy-start(bf16[4096,256]{1,0:T(8,128)(2,1)} %k_ref.1) | copy-start | bytes 6291460
  0.0 7.0 %collective-permute-start.1 = (bf16[16,4096]{1,0:T(8,128)(2,1)}, bf16[16,4096]{1,0:T(8,128)(2,1)S(1)}, u32[]{:S(2)}, u32[]{:S(2)}) collective-permute-start(bf16[16,4096]{1,0:T(8,128)(2,1)} %own_ref.1), channel_id=1, source_target_pairs={{0,2},{2,0},{1,3},{3,1},{4,6},{6,4},{5,7},{7,5},{8,10},{10,8},{9,1... | collective-permute-start | bytes 393224 | tf_op jit(solution)/shard_map/ppermute | solution.py:136
  3.0 4.6 %collective-permute-start = (bf16[16,4096]{1,0:T(8,128)(2,1)}, bf16[16,4096]{1,0:T(8,128)(2,1)S(1)}, u32[]{:S(2)}, u32[]{:S(2)}) collective-permute-start(bf16[16,4096]{1,0:T(8,128)(2,1)} %own_ref.1), channel_id=1, source_target_pairs={{0,1},{1,0},{2,3},{3,2},{4,5},{5,4},{6,7},{7,6},{8,9},{9,8},{10,11... | collective-permute-start | bytes 393224 | tf_op jit(solution)/shard_map/ppermute | solution.py:136
  7.0 1.6 %collective-permute-start.2 = (bf16[16,4096]{1,0:T(8,128)(2,1)S(1)}, bf16[16,4096]{1,0:T(8,128)(2,1)S(1)}, u32[]{:S(2)}, u32[]{:S(2)}) collective-permute-start(bf16[16,4096]{1,0:T(8,128)(2,1)S(1)} %collective-permute-done.1.chip_ref), channel_id=1, source_target_pairs={{0,1},{1,0},{2,3},{3,2},{4,5},{5,4},{6,7},{7,6},{8,9},{9,8},{10,11... | collective-permute-start | bytes 393224 | tf_op jit(solution)/shard_map/ppermute | solution.py:136
  8.6 3.6 %copy-start = (bf16[8,512,2,128]{3,2,1,0:T(2,128)(2,1)S(1)}, bf16[8,512,2,128]{3,2,1,0:T(2,128)(2,1)}, u32[]{:S(2)}) copy-start(bf16[8,512,2,128]{3,2,1,0:T(2,128)(2,1)} %param.13) | copy-start | bytes 6291460
  8.6 4.1 %copy-start.2 = (bf16[8,512,2,128]{3,2,1,0:T(2,128)(2,1)S(1)}, bf16[8,512,2,128]{3,2,1,0:T(2,128)(2,1)}, u32[]{:S(2)}) copy-start(bf16[8,512,2,128]{3,2,1,0:T(2,128)(2,1)} %param.14) | copy-start | bytes 6291460
  12.7 5.8 %copy-start.1 = (bf16[8,512,2,128]{3,2,1,0:T(2,128)(2,1)S(1)}, bf16[8,512,2,128]{3,2,1,0:T(2,128)(2,1)}, u32[]{:S(2)}) copy-start(bf16[8,512,2,128]{3,2,1,0:T(2,128)(2,1)} %param.13) | copy-start | bytes 6291460
  12.7 5.8 %copy-start.3 = (bf16[8,512,2,128]{3,2,1,0:T(2,128)(2,1)S(1)}, bf16[8,512,2,128]{3,2,1,0:T(2,128)(2,1)}, u32[]{:S(2)}) copy-start(bf16[8,512,2,128]{3,2,1,0:T(2,128)(2,1)} %param.14) | copy-start | bytes 6291460
  12.7 5.8 %copy-start.7 = (s32[16]{0:T(128)S(1)}, s32[16]{0:T(128)}, u32[]{:S(2)}) copy-start(s32[16]{0:T(128)} %length_ref.3) | copy-start | bytes 196
  13.6 10.9 %collective-permute-start.6 = (bf16[2,4096,128]{2,1,0:T(8,128)(2,1)S(1)}, bf16[2,4096,128]{2,1,0:T(8,128)(2,1)S(1)}, u32[]{:S(2)}, u32[]{:S(2)}) collective-permute-start(bf16[2,4096,128]{2,1,0:T(8,128)(2,1)S(1)} %partner_cache.1.after_ref), channel_id=1, source_target_pairs={{0,1},{1,0},{2,3},{3,2},{4,5},{5,4},{6,7},{7,6},{8,9},{9,8},{10,11... | collective-permute-start | bytes 6291464 | tf_op jit(solution)/shard_map/ppermute | solution.py:136
  14.0 7.7 %collective-permute-start.3 = (bf16[16,2304]{1,0:T(8,128)(2,1)S(1)}, bf16[16,2304]{1,0:T(8,128)(2,1)S(1)}, u32[]{:S(2)}, u32[]{:S(2)}) collective-permute-start(bf16[16,2304]{1,0:T(8,128)(2,1)S(1)} %get-tuple-element.27), channel_id=1, source_target_pairs={{0,4},{4,0},{8,12},{12,8},{1,5},{5,1},{9,13},{13,9},{2,6},{6,2},{1... | collective-permute-start | bytes 221192 | tf_op jit(solution)/shard_map/ppermute | solution.py:136
  15.6 8.9 %collective-permute-start.4 = (bf16[16,2304]{1,0:T(8,128)(2,1)S(1)}, bf16[16,2304]{1,0:T(8,128)(2,1)S(1)}, u32[]{:S(2)}, u32[]{:S(2)}) collective-permute-start(bf16[16,2304]{1,0:T(8,128)(2,1)S(1)} %get-tuple-element.28), channel_id=1, source_target_pairs={{0,8},{4,12},{8,0},{12,4},{1,9},{5,13},{9,1},{13,5},{2,10},{6,14},... | collective-permute-start | bytes 221192 | tf_op jit(solution)/shard_map/ppermute | solution.py:136
  18.2 6.3 %collective-permute-start.5 = (bf16[16,2304]{1,0:T(8,128)(2,1)S(1)}, bf16[16,2304]{1,0:T(8,128)(2,1)S(1)}, u32[]{:S(2)}, u32[]{:S(2)}) collective-permute-start(bf16[16,2304]{1,0:T(8,128)(2,1)S(1)} %get-tuple-element.29), channel_id=1, source_target_pairs={{0,12},{4,8},{8,4},{12,0},{1,13},{5,9},{9,5},{13,1},{2,14},{6,10},... | collective-permute-start | bytes 221192 | tf_op jit(solution)/shard_map/ppermute | solution.py:136
  26.6 9.0 %collective-permute-start.9 = (bf16[16,2048]{1,0:T(8,128)(2,1)S(1)}, bf16[16,2048]{1,0:T(8,128)(2,1)S(1)}, u32[]{:S(2)}, u32[]{:S(2)}) collective-permute-start(bf16[16,2048]{1,0:T(8,128)(2,1)S(1)} %attend.1.refs_0_.a_ref), channel_id=1, source_target_pairs={{0,12},{4,8},{8,4},{12,0},{1,13},{5,9},{9,5},{13,1},{2,14},{6,10},... | collective-permute-start | bytes 196616 | tf_op jit(solution)/shard_map/ppermute | solution.py:136
  29.1 6.5 %collective-permute-start.8 = (bf16[16,2048]{1,0:T(8,128)(2,1)S(1)}, bf16[16,2048]{1,0:T(8,128)(2,1)S(1)}, u32[]{:S(2)}, u32[]{:S(2)}) collective-permute-start(bf16[16,2048]{1,0:T(8,128)(2,1)S(1)} %attend.1.refs_0_.a_ref), channel_id=1, source_target_pairs={{0,8},{4,12},{8,0},{12,4},{1,9},{5,13},{9,1},{13,5},{2,10},{6,14},... | collective-permute-start | bytes 196616 | tf_op jit(solution)/shard_map/ppermute | solution.py:136
  29.5 6.1 %collective-permute-start.7 = (bf16[16,2048]{1,0:T(8,128)(2,1)S(1)}, bf16[16,2048]{1,0:T(8,128)(2,1)S(1)}, u32[]{:S(2)}, u32[]{:S(2)}) collective-permute-start(bf16[16,2048]{1,0:T(8,128)(2,1)S(1)} %attend.1.refs_0_.a_ref), channel_id=1, source_target_pairs={{0,4},{4,0},{8,12},{12,8},{1,5},{5,1},{9,13},{13,9},{2,6},{6,2},{1... | collective-permute-start | bytes 196616 | tf_op jit(solution)/shard_map/ppermute | solution.py:136
  38.6 1.6 %collective-permute-start.10 = (bf16[32,4096]{1,0:T(8,128)(2,1)S(1)}, bf16[32,4096]{1,0:T(8,128)(2,1)S(1)}, u32[]{:S(2)}, u32[]{:S(2)}) collective-permute-start(bf16[32,4096]{1,0:T(8,128)(2,1)S(1)} %get-tuple-element.36), channel_id=1, source_target_pairs={{0,1},{1,0},{2,3},{3,2},{4,5},{5,4},{6,7},{7,6},{8,9},{9,8},{10,11... | collective-permute-start | bytes 786440 | tf_op jit(solution)/shard_map/ppermute | solution.py:136
  40.3 5.6 %collective-permute-start.11 = (bf16[16,4096]{1,0:T(8,128)(2,1)S(1)}, bf16[16,4096]{1,0:T(8,128)(2,1)S(1)}, u32[]{:S(2)}, u32[]{:S(2)}) collective-permute-start(bf16[16,4096]{1,0:T(8,128)(2,1)S(1)} %get-tuple-element.38), channel_id=1, source_target_pairs={{0,2},{2,0},{1,3},{3,1},{4,6},{6,4},{5,7},{7,5},{8,10},{10,8},{9,1... | collective-permute-start | bytes 393224 | tf_op jit(solution)/shard_map/ppermute | solution.py:136

commit v4 on v3

--- a/solution.py
+++ b/solution.py
@@ -118,9 +118,11 @@
 MIB = 2**20
 STEP = 512
 FIRST_Q, PIECE_Q = 2560, 512
-FIRST_O = 1536
+FIRST_O, SECOND_O, PIECE_O = 768, 768, 512
 ROOM = 42
 ROOM_Q = 38
+ROOM_O = 38
+ORDER = (0, 3, 2, 1)
 
 
 def vmem(mib):
@@ -136,20 +138,18 @@
     return lax.ppermute(array, axis, [(i, i ^ bit) for i in range(size)])
 
 
-def fetch_kernel(weight_ref, *refs, start, axis):
+def fetch_kernel(weight_ref, *refs, start):
     out_ref, mark_ref, sem = refs[-3:]
-    cut = pl.ds(start, out_ref.shape[axis])
-    source = weight_ref.at[cut] if axis == 0 else weight_ref.at[:, cut]
-    copy = pltpu.make_async_copy(source, out_ref, sem)
+    copy = pltpu.make_async_copy(weight_ref.at[pl.ds(start, out_ref.shape[0])], out_ref, sem)
     copy.start()
     mark_ref[...] = jnp.zeros_like(mark_ref)
     copy.wait()
 
 
-def fetch(weight, axis, start, count, *after):
-    shape = (count, weight.shape[1]) if axis == 0 else (weight.shape[0], count)
-    return pl.pallas_call(
-        functools.partial(fetch_kernel, start=start, axis=axis),
+def fetch(weight, start, count, *after):
+    shape = (count, weight.shape[1])
+    return pl.pallas_call(
+        functools.partial(fetch_kernel, start=start),
         out_shape=[pltpu.VMEM(shape, weight.dtype), jax.ShapeDtypeStruct((8, 128), jnp.float32)],
         in_specs=[ANY_SPEC] * (1 + len(after)),
         out_specs=[VMEM_SPEC] * 2,
@@ -196,7 +196,7 @@
     part_ref, own_ref, cos_ref, sin_ref, wide_rows, sem,
 ):
     del after_ref
-    copy = pltpu.make_async_copy(weight_ref.at[:, pl.ds(0, part_ref.shape[1])], part_ref, sem)
+    copy = pltpu.make_async_copy(weight_ref.at[pl.ds(0, part_ref.shape[0])], part_ref, sem)
     copy.start()
     seqs, width = cos_ref.shape
     lane = lax.broadcasted_iota(jnp.int32, (seqs, width), 1)
@@ -213,13 +213,13 @@
     copy.wait()
 
 
-def prepare(lengths, weight, columns, keys, values, after):
+def prepare(lengths, weight, count, keys, values, after):
     seqs, rows, _ = keys.shape
     factors = jax.ShapeDtypeStruct((lengths.shape[0], HD), jnp.float32)
     return pl.pallas_call(
         prepare_kernel,
         out_shape=[
-            pltpu.VMEM((weight.shape[0], columns), weight.dtype),
+            pltpu.VMEM((count, weight.shape[1]), weight.dtype),
             pltpu.VMEM((2, seqs * rows // 2, HD), keys.dtype),
             factors,
             factors,
@@ -231,7 +231,7 @@
             pltpu.SemaphoreType.DMA,
         ],
         compiler_params=vmem(ROOM - 8),
-        cost_estimate=cost(10**9, weight.shape[0] * columns * 2),
+        cost_estimate=cost(10**11, count * weight.shape[1] * 2),
         name="prepare",
     )(lengths, weight, keys, values, after)
 
@@ -265,7 +265,7 @@
         return jnp.dot(tokens, block, preferred_element_type=jnp.float32)
 
     def store(product, start):
-        for place, out in enumerate(outs):
+        for place, out in zip(ORDER, outs):
             out[:, start : start + product.shape[1]] = product[
                 place * rows : (place + 1) * rows
             ].astype(out.dtype)
@@ -414,44 +414,70 @@
 
 
 def output_kernel(
-    a_ref, b_ref, c_ref, d_ref, first_ref, second_ref, keep_ref, send_ref, rows_scratch
+    a_ref, b_ref, c_ref, d_ref, first_ref, second_ref, weight_ref,
+    keep_ref, send_ref, rows_scratch, rest, total, sems,
 ):
     narrow, sub, wide = lax.axis_index("narrow"), lax.axis_index("sub"), lax.axis_index("wide")
+    depth, columns = weight_ref.shape
+    early = first_ref.shape[0]
+    ready = early + second_ref.shape[0]
+    pieces = range(ready, depth, PIECE_O)
+    copies = [
+        pltpu.make_async_copy(
+            weight_ref.at[pl.ds(start, PIECE_O)],
+            rest.at[pl.ds(start - ready, PIECE_O)],
+            sems.at[j],
+        )
+        for j, start in enumerate(pieces)
+    ]
+    for copy in copies:
+        copy.start()
     mine = (narrow * 2 + sub) ^ wide
     rows = a_ref.shape[0]
     for k, ref in enumerate((a_ref, b_ref, c_ref, d_ref)):
         m = mine ^ k
         place = pl.multiple_of(((m & 1) * 2 + (m >> 1)) * rows, rows)
         rows_scratch[pl.ds(place, rows), :] = ref[...]
-    mixed = rows_scratch[...]
-
-    done = 0
-    for ref in (first_ref, second_ref):
-        for start in range(0, ref.shape[1], STEP):
-            product = jnp.dot(
-                mixed, ref[:, start : start + STEP], preferred_element_type=jnp.float32
-            )
-            cut = slice(done + start, done + start + STEP)
-            keep_ref[:, cut] = product[: 2 * rows]
-            send_ref[:, cut] = product[2 * rows :].astype(send_ref.dtype)
-        done += ref.shape[1]
-
-
-def output(blocks, first_part, second_part):
-    rows, depth = blocks[0].shape
-    columns = first_part.shape[1] + second_part.shape[1]
+
+    def part(start, block):
+        mixed = rows_scratch[:, start : start + block.shape[0]]
+        return jnp.dot(mixed, block, preferred_element_type=jnp.float32)
+
+    cuts = [slice(start, start + STEP) for start in range(0, columns, STEP)]
+    for cut in cuts:
+        total[:, cut] = part(0, first_ref[:, cut]) + part(early, second_ref[:, cut])
+    for j, (start, copy) in enumerate(zip(pieces, copies)):
+        copy.wait()
+        for cut in cuts:
+            product = total[:, cut] + part(start, rest[j * PIECE_O : (j + 1) * PIECE_O, cut])
+            if start + PIECE_O < depth:
+                total[:, cut] = product
+            else:
+                keep_ref[:, cut] = product[: 2 * rows]
+                send_ref[:, cut] = product[2 * rows :].astype(send_ref.dtype)
+
+
+def output(blocks, first_part, second_part, weight):
+    rows = blocks[0].shape[0]
+    depth, columns = weight.shape
+    late = depth - first_part.shape[0] - second_part.shape[0]
     return pl.pallas_call(
         output_kernel,
         out_shape=[
             jax.ShapeDtypeStruct((2 * rows, columns), jnp.float32),
             jax.ShapeDtypeStruct((2 * rows, columns), jnp.bfloat16),
         ],
-        in_specs=[VMEM_SPEC] * 6,
+        in_specs=[VMEM_SPEC] * 6 + [ANY_SPEC],
         out_specs=[VMEM_SPEC] * 2,
-        scratch_shapes=[pltpu.VMEM((4 * rows, depth), jnp.bfloat16)],
-        compiler_params=vmem(6),
+        scratch_shapes=[
+            pltpu.VMEM((4 * rows, depth), jnp.bfloat16),
+            pltpu.VMEM((late, columns), jnp.bfloat16),
+            pltpu.VMEM((4 * rows, columns), jnp.float32),
+            pltpu.SemaphoreType.DMA((late // PIECE_O,)),
+        ],
+        compiler_params=vmem(ROOM_O),
         name="output",
-    )(*blocks, first_part, second_part)
+    )(*blocks, first_part, second_part, weight)
 
 
 def add_kernel(keep_ref, other_ref, mine_ref, send_ref):
@@ -484,20 +510,20 @@
     values = cache_values.reshape(seqs, slots * kv_heads, HD)
     chip = exchange(tokens, "narrow", 1)
     core = exchange(tokens, "sub", 1)
-    q_first, mark = fetch(q_weight, 0, 0, FIRST_Q)
+    q_first, mark = fetch(q_weight, 0, FIRST_Q)
     chip, mark = lax.optimization_barrier((chip, mark))
     both = exchange(chip, "sub", 1)
     parts = project(tokens, core, chip, both, q_first, k_weight, v_weight, q_weight, mark)
-    parts = [parts[0]] + [exchange(parts[k], "wide", k) for k in (1, 2, 3)]
+    parts = [parts[0]] + [exchange(part, "wide", k) for k, part in zip(ORDER[1:], parts[1:])]
     send_cache = partner_cache(keys, values, parts[0])
     other_cache = exchange(send_cache, "sub", 1)
     o_first, own_cache, cosine, sine = prepare(
         lengths, o_weight, FIRST_O, keys, values, send_cache
     )
     mixed = attend_here(lengths, parts, cosine, sine, own_cache, other_cache, o_first)
-    o_second, _ = fetch(o_weight, 1, FIRST_O, o_weight.shape[1] - FIRST_O, mixed)
+    o_second, _ = fetch(o_weight, FIRST_O, SECOND_O, mixed)
     blocks = [mixed] + [exchange(mixed, "wide", k) for k in (1, 2, 3)]
-    keep, send = output(blocks, o_first, o_second)
+    keep, send = output(blocks, o_first, o_second, o_weight)
     mine, send = add_halves(keep, exchange(send, "sub", 1))
     return (mine + exchange(send, "narrow", 1).astype(jnp.float32)).astype(jnp.bfloat16)
 

time: 46.8 us -> 44.9 us (0.959)
  Pallas kernels: 21.5 us -> 20.4 us
  waiting for transfers between devices: 9.61 us -> 8.95 us
    pallas_call x3, Pallas kernels: 11.9 us -> 10.7 us  [the longest x2 7.37 us: fetch(): pl.pallas_call(functools.partial(fetch_kernel, start=start), out_shape=[p...]
    ppermute x12, waiting for transfers between devices: 9.61 us -> 8.95 us  [exchange(): return lax.ppermute(array, axis, [(i, i ^ bit) for i in range(size)])]
  transfers between devices with their start and end apart: 12 -> 12, of which waited for: 4 -> 5; matrix products, arithmetic and copies ran while one was open for 0% -> 0% of each run, Pallas kernels for 26% -> 26%
where the time goes in v4:
time: 44.9 us; the launch traced here: 44.6 us
  Pallas kernels  20.4 us (45%)
  starting transfers between devices  13.8 us (31%)
  waiting for transfers between devices  8.95 us (20%)
  other arithmetic  0.68 us (2%)
  local copies, waits for them, and re-layouts  0.6 us (1%)
    ppermute x12, starting transfers between devices, exchange(): return lax.ppermute(array, axis, [(i, i ^ bit) for i in range(size)])  13.8 us
    ppermute x12, waiting for transfers between devices, exchange(): return lax.ppermute(array, axis, [(i, i ^ bit) for i in range(size)])  8.95 us
    pallas_call x2, Pallas kernels, fetch(): pl.pallas_call(functools.partial(fetch_kernel, start=start), out_shape=[p...  7.37 us
    pallas_call x1, Pallas kernels, project(): pl.pallas_call(project_kernel, out_shape=[jax.ShapeDtypeStruct((rows, col...  3.57 us
    pallas_call x1, Pallas kernels, prepare(): pl.pallas_call(prepare_kernel, out_shape=[pltpu.VMEM((count, weight.shape...  3.33 us
    pallas_call x1, Pallas kernels, output(): pl.pallas_call(output_kernel, out_shape=[jax.ShapeDtypeStruct((2 * rows,...  3.07 us
    pallas_call x1, Pallas kernels, attend_here(): pl.pallas_call(attend_kernel, out_shape=jax.ShapeDtypeStruct((seqs, heads...  2.07 us
    pallas_call x1, Pallas kernels, partner_cache(): pl.pallas_call(partner_kernel, out_shape=pltpu.VMEM((2, seqs * rows // 2,...  0.92 us
  transfers between devices with their start and end apart: 12, of which 5 were waited for; matrix products, arithmetic and copies ran while one was open for 0% of the time, Pallas kernels for 26%

profile of v4, /device:TPU:0, one launch (start us, length us, event | category | flops | bytes accessed | tf_op | source)
XLA Modules:
  0.0 44.6 jit_solution(1142952369867810640)
XLA Ops:
  0.0 0.0 copy-start.5
  0.0 0.0 copy-start.1
  0.0 0.0 copy-start
  0.0 3.0 %collective-permute-start.1 = (bf16[16,4096]{1,0:T(8,128)(2,1)}, bf16[16,4096]{1,0:T(8,128)(2,1)S(1)}, u32[]{:S(2)}, u32[]{:S(2)}) collective-permute-start(bf16[16,4096]{1,0:T(8,128)(2,1)} %own_ref.1), channel_id=1, source_target_pairs={{0,2},{2,0},{1,3},{3,1},{4,6},{6,4},{5,7},{7,5},{8,10},{10,8},{9,1... | collective-permute-start | bytes 393224 | tf_op jit(solution)/shard_map/ppermute | solution.py:138
  3.0 0.0 collective-permute-start
  3.0 4.0 %fetch.2 = (bf16[2560,2048]{1,0:T(8,128)(2,1)S(1)}, f32[8,128]{1,0:T(8,128)S(1)}) custom-call(bf16[4096,2048]{1,0:T(8,128)(2,1)} %q_ref.1), custom_call_target="tpu_custom_call" | custom-call | bytes 10485760 | tf_op jit(solution)/shard_map/fetch/pallas_call | solution.py:151
  7.0 0.0 collective-permute-done.1.chip_ref
  7.0 0.6 %collective-permute-start.2 = (bf16[16,4096]{1,0:T(8,128)(2,1)S(1)}, bf16[16,4096]{1,0:T(8,128)(2,1)S(1)}, u32[]{:S(2)}, u32[]{:S(2)}) collective-permute-start(bf16[16,4096]{1,0:T(8,128)(2,1)S(1)} %collective-permute-done.1.chip_ref), channel_id=1, source_target_pairs={{0,1},{1,0},{2,3},{3,2},{4,5},{5,4},{6,7},{7,6},{8,9},{9,8},{10,11... | collective-permute-start | bytes 393224 | tf_op jit(solution)/shard_map/ppermute | solution.py:138
  7.6 0.0 collective-permute-done.core_ref
  7.6 1.0 %collective-permute-done.2.both_ref = bf16[16,4096]{1,0:T(8,128)(2,1)S(1)} collective-permute-done((bf16[16,4096]{1,0:T(8,128)(2,1)S(1)}, bf16[16,4096]{1,0:T(8,128)(2,1)S(1)}, u32[]{:S(2)}, u32[]{:S(2)}) %collective-permute-start.2) | collective-permute-done | bytes 131104 | tf_op jit(solution)/shard_map/ppermute | solution.py:138
  8.6 0.0 copy-done.5
  8.6 0.0 copy-done.1
  8.6 0.0 copy-done
  8.6 0.0 copy-start.2
  8.6 0.0 copy-start.3
  8.6 3.6 %project.1 = (bf16[16,2304]{1,0:T(8,128)(2,1)S(1)}, bf16[16,2304]{1,0:T(8,128)(2,1)S(1)}, bf16[16,2304]{1,0:T(8,128)(2,1)S(1)}, bf16[16,2304]{1,0:T(8,128)(2,1)S(1)}) custom-call(bf16[16,4096]{1,0:T(8,128)(2,1)S(1)} %copy-done.5, bf16[16,4096]{1,0:T(8,128)(2,1)S(1)} %collective-permute-done.core_ref, bf16[16,4096]{1,0:T(8,128)(2,1)S(1)} %collective-permute-done.1.chip_ref, ...), custom_call_target="tpu_custom_call" | custom-call | flops 4294967296 | tf_op jit(solution)/shard_map/project/pallas_call | solution.py:292
  12.2 3.7 %collective-permute-start.3 = (bf16[16,2304]{1,0:T(8,128)(2,1)S(1)}, bf16[16,2304]{1,0:T(8,128)(2,1)S(1)}, u32[]{:S(2)}, u32[]{:S(2)}) collective-permute-start(bf16[16,2304]{1,0:T(8,128)(2,1)S(1)} %get-tuple-element.27), channel_id=1, source_target_pairs={{0,12},{4,8},{8,4},{12,0},{1,13},{5,9},{9,5},{13,1},{2,14},{6,10},... | collective-permute-start | bytes 221192 | tf_op jit(solution)/shard_map/ppermute | solution.py:138
  15.9 0.0 collective-permute-start.4
  15.9 0.8 %collective-permute-start.5 = (bf16[16,2304]{1,0:T(8,128)(2,1)S(1)}, bf16[16,2304]{1,0:T(8,128)(2,1)S(1)}, u32[]{:S(2)}, u32[]{:S(2)}) collective-permute-start(bf16[16,2304]{1,0:T(8,128)(2,1)S(1)} %get-tuple-element.29), channel_id=1, source_target_pairs={{0,4},{4,0},{8,12},{12,8},{1,5},{5,1},{9,13},{13,9},{2,6},{6,2},{1... | collective-permute-start | bytes 221192 | tf_op jit(solution)/shard_map/ppermute | solution.py:138
  16.7 0.0 copy-done.2
  16.7 0.0 copy-done.3
  16.7 0.0 copy-start.4
  16.7 0.0 copy-start.6
  16.7 0.9 %partner_cache.1.after_ref = bf16[2,4096,128]{2,1,0:T(8,128)(2,1)S(1)} custom-call(bf16[8,1024,128]{2,1,0:T(8,128)(2,1)S(1)} %bitcast.2, bf16[8,1024,128]{2,1,0:T(8,128)(2,1)S(1)} %bitcast.4, bf16[16,2304]{1,0:T(8,128)(2,1)S(1)} %get-tuple-element.26.after_ref.a_ref), custom_call_target="tpu_custom_call" | custom-call | flops 1000000000 | tf_op jit(solution)/shard_map/partner_cache/pallas_call | solution.py:182
  17.6 0.1 collective-permute-start.6
  17.7 0.6 %copy-done.4 = bf16[8,512,2,128]{3,2,1,0:T(2,128)(2,1)S(1)} copy-done((bf16[8,512,2,128]{3,2,1,0:T(2,128)(2,1)S(1)}, bf16[8,512,2,128]{3,2,1,0:T(2,128)(2,1)}, u32[]{:S(2)}) %copy-start.4) | copy-done | bytes 2097176
  18.3 0.0 copy-done.6
  18.3 3.3 %prepare.1 = (bf16[768,4096]{1,0:T(8,128)(2,1)S(1)}, bf16[2,4096,128]{2,1,0:T(8,128)(2,1)S(1)}, f32[16,128]{1,0:T(8,128)S(1)}, f32[16,128]{1,0:T(8,128)S(1)}) custom-call(s32[16]{0:T(128)S(1)} %copy-done.6, bf16[2048,4096]{1,0:T(8,128)(2,1)} %weight_ref.7, bf16[8,1024,128]{2,1,0:T(8,128)(2,1)S(1)} %bitcast.3, bf16[8,1024,128]{2,1,0:T(8,128)(2,1)S(1)} %bitcast.5, ...), custom_call_target="tpu_custom_call" | custom-call | flops 99999997952 | bytes 6291456 | tf_op jit(solution)/shard_map/prepare/pallas_call | solution.py:219
  21.6 0.0 collective-permute-done.3.b_ref
  21.6 0.9 %collective-permute-done.4.c_ref = bf16[16,2304]{1,0:T(8,128)(2,1)S(1)} collective-permute-done((bf16[16,2304]{1,0:T(8,128)(2,1)S(1)}, bf16[16,2304]{1,0:T(8,128)(2,1)S(1)}, u32[]{:S(2)}, u32[]{:S(2)}) %collective-permute-start.4) | collective-permute-done | bytes 73760 | tf_op jit(solution)/shard_map/ppermute | solution.py:138
  22.5 0.0 collective-permute-done.5.d_ref
  22.5 0.0 collective-permute-done.6.other_ref
  22.6 2.1 %attend.1.refs_0_.a_ref = bf16[16,2048]{1,0:T(8,128)(2,1)S(1)} custom-call(s32[16]{0:T(128)S(1)} %copy-done.6, bf16[16,2304]{1,0:T(8,128)(2,1)S(1)} %get-tuple-element.26.after_ref.a_ref, bf16[16,2304]{1,0:T(8,128)(2,1)S(1)} %collective-permute-done.3.b_ref, bf16[16,2304]{1,0:T(8,128)(2,1)S(1)} %collective-permute-done.4.c_ref, ...), custom_call_target="tpu_custom_call" | custom-call | flops 4000000000 | tf_op jit(solution)/shard_map/attend/pallas_call | solution.py:398
  24.6 2.9 %collective-permute-start.9 = (bf16[16,2048]{1,0:T(8,128)(2,1)S(1)}, bf16[16,2048]{1,0:T(8,128)(2,1)S(1)}, u32[]{:S(2)}, u32[]{:S(2)}) collective-permute-start(bf16[16,2048]{1,0:T(8,128)(2,1)S(1)} %attend.1.refs_0_.a_ref), channel_id=1, source_target_pairs={{0,12},{4,8},{8,4},{12,0},{1,13},{5,9},{9,5},{13,1},{2,14},{6,10},... | collective-permute-start | bytes 196616 | tf_op jit(solution)/shard_map/ppermute | solution.py:138
  27.6 0.0 collective-permute-start.8
  27.6 1.5 %collective-permute-start.7 = (bf16[16,2048]{1,0:T(8,128)(2,1)S(1)}, bf16[16,2048]{1,0:T(8,128)(2,1)S(1)}, u32[]{:S(2)}, u32[]{:S(2)}) collective-permute-start(bf16[16,2048]{1,0:T(8,128)(2,1)S(1)} %attend.1.refs_0_.a_ref), channel_id=1, source_target_pairs={{0,4},{4,0},{8,12},{12,8},{1,5},{5,1},{9,13},{13,9},{2,6},{6,2},{1... | collective-permute-start | bytes 196616 | tf_op jit(solution)/shard_map/ppermute | solution.py:138
  29.1 3.4 %fetch.3 = (bf16[768,4096]{1,0:T(8,128)(2,1)S(1)}, f32[8,128]{1,0:T(8,128)}) custom-call(bf16[2048,4096]{1,0:T(8,128)(2,1)} %weight_ref.7, bf16[16,2048]{1,0:T(8,128)(2,1)S(1)} %attend.1.refs_0_.a_ref), custom_call_target="tpu_custom_call" | custom-call | bytes 6291456 | tf_op jit(solution)/shard_map/fetch/pallas_call | solution.py:151
  32.5 0.0 collective-permute-done.9.d_ref
  32.5 1.1 %collective-permute-done.8.c_ref = bf16[16,2048]{1,0:T(8,128)(2,1)S(1)} collective-permute-done((bf16[16,2048]{1,0:T(8,128)(2,1)S(1)}, bf16[16,2048]{1,0:T(8,128)(2,1)S(1)}, u32[]{:S(2)}, u32[]{:S(2)}) %collective-permute-start.8) | collective-permute-done | bytes 65568 | tf_op jit(solution)/shard_map/ppermute | solution.py:138
  33.5 0.0 collective-permute-done.7.b_ref
  33.6 3.1 %output.1 = (f32[32,4096]{1,0:T(8,128)S(1)}, bf16[32,4096]{1,0:T(8,128)(2,1)S(1)}) custom-call(bf16[16,2048]{1,0:T(8,128)(2,1)S(1)} %attend.1.refs_0_.a_ref, bf16[16,2048]{1,0:T(8,128)(2,1)S(1)} %collective-permute-done.7.b_ref, bf16[16,2048]{1,0:T(8,128)(2,1)S(1)} %collective-permute-done.8.c_ref, bf16[16,2048]{1,0:T(8,128)(2,1)S(1)} %collective-permute-done.9.d_ref, ...), custom_call_target="tpu_custom_call" | custom-call | tf_op jit(solution)/shard_map/output/pallas_call | solution.py:464
  36.6 0.1 collective-permute-start.10
  36.7 1.5 %collective-permute-done.10.other_ref = bf16[32,4096]{1,0:T(8,128)(2,1)S(1)} collective-permute-done((bf16[32,4096]{1,0:T(8,128)(2,1)S(1)}, bf16[32,4096]{1,0:T(8,128)(2,1)S(1)}, u32[]{:S(2)}, u32[]{:S(2)}) %collective-permute-start.10) | collective-permute-done | bytes 262176 | tf_op jit(solution)/shard_map/ppermute | solution.py:138
  38.3 1.2 %collective-permute-start.11 = (bf16[16,4096]{1,0:T(8,128)(2,1)S(1)}, bf16[16,4096]{1,0:T(8,128)(2,1)S(1)}, u32[]{:S(2)}, u32[]{:S(2)}) collective-permute-start(bf16[16,4096]{1,0:T(8,128)(2,1)S(1)} %get-tuple-element.38), channel_id=1, source_target_pairs={{0,2},{2,0},{1,3},{3,1},{4,6},{6,4},{5,7},{7,5},{8,10},{10,8},{9,1... | collective-permute-start | bytes 393224 | tf_op jit(solution)/shard_map/ppermute | solution.py:138
  39.5 4.4 %collective-permute-done.11 = bf16[16,4096]{1,0:T(8,128)(2,1)S(1)} collective-permute-done((bf16[16,4096]{1,0:T(8,128)(2,1)S(1)}, bf16[16,4096]{1,0:T(8,128)(2,1)S(1)}, u32[]{:S(2)}, u32[]{:S(2)}) %collective-permute-start.11) | collective-permute-done | bytes 131104 | tf_op jit(solution)/shard_map/ppermute | solution.py:138
  43.9 0.7 %add_convert_fusion = bf16[16,4096]{1,0:T(8,128)(2,1)} fusion(f32[16,4096]{1,0:T(8,128)S(1)} %get-tuple-element.37, bf16[16,4096]{1,0:T(8,128)(2,1)S(1)} %collective-permute-done.11), kind=kLoop, calls=%fused_computation | loop fusion | flops 196608 | bytes 524288 | tf_op jit(solution)/shard_map/convert_element_type | solution.py:528
  (1 shorter events, 0.0 us)
Async XLA Ops:
  0.0 8.6 %copy-start.5 = (bf16[16,4096]{1,0:T(8,128)(2,1)S(1)}, bf16[16,4096]{1,0:T(8,128)(2,1)}, u32[]{:S(2)}) copy-start(bf16[16,4096]{1,0:T(8,128)(2,1)} %own_ref.1) | copy-start | bytes 393220
  0.0 8.6 %copy-start.1 = (bf16[4096,256]{1,0:T(8,128)(2,1)S(1)}, bf16[4096,256]{1,0:T(8,128)(2,1)}, u32[]{:S(2)}) copy-start(bf16[4096,256]{1,0:T(8,128)(2,1)} %v_ref.1) | copy-start | bytes 6291460
  0.0 8.6 %copy-start = (bf16[4096,256]{1,0:T(8,128)(2,1)S(1)}, bf16[4096,256]{1,0:T(8,128)(2,1)}, u32[]{:S(2)}) copy-start(bf16[4096,256]{1,0:T(8,128)(2,1)} %k_ref.1) | copy-start | bytes 6291460
  0.0 7.0 %collective-permute-start.1 = (bf16[16,4096]{1,0:T(8,128)(2,1)}, bf16[16,4096]{1,0:T(8,128)(2,1)S(1)}, u32[]{:S(2)}, u32[]{:S(2)}) collective-permute-start(bf16[16,4096]{1,0:T(8,128)(2,1)} %own_ref.1), channel_id=1, source_target_pairs={{0,2},{2,0},{1,3},{3,1},{4,6},{6,4},{5,7},{7,5},{8,10},{10,8},{9,1... | collective-permute-start | bytes 393224 | tf_op jit(solution)/shard_map/ppermute | solution.py:138
  3.0 4.6 %collective-permute-start = (bf16[16,4096]{1,0:T(8,128)(2,1)}, bf16[16,4096]{1,0:T(8,128)(2,1)S(1)}, u32[]{:S(2)}, u32[]{:S(2)}) collective-permute-start(bf16[16,4096]{1,0:T(8,128)(2,1)} %own_ref.1), channel_id=1, source_target_pairs={{0,1},{1,0},{2,3},{3,2},{4,5},{5,4},{6,7},{7,6},{8,9},{9,8},{10,11... | collective-permute-start | bytes 393224 | tf_op jit(solution)/shard_map/ppermute | solution.py:138
  7.0 1.6 %collective-permute-start.2 = (bf16[16,4096]{1,0:T(8,128)(2,1)S(1)}, bf16[16,4096]{1,0:T(8,128)(2,1)S(1)}, u32[]{:S(2)}, u32[]{:S(2)}) collective-permute-start(bf16[16,4096]{1,0:T(8,128)(2,1)S(1)} %collective-permute-done.1.chip_ref), channel_id=1, source_target_pairs={{0,1},{1,0},{2,3},{3,2},{4,5},{5,4},{6,7},{7,6},{8,9},{9,8},{10,11... | collective-permute-start | bytes 393224 | tf_op jit(solution)/shard_map/ppermute | solution.py:138
  8.6 8.1 %copy-start.2 = (bf16[8,512,2,128]{3,2,1,0:T(2,128)(2,1)S(1)}, bf16[8,512,2,128]{3,2,1,0:T(2,128)(2,1)}, u32[]{:S(2)}) copy-start(bf16[8,512,2,128]{3,2,1,0:T(2,128)(2,1)} %param.13) | copy-start | bytes 6291460
  8.6 8.1 %copy-start.3 = (bf16[8,512,2,128]{3,2,1,0:T(2,128)(2,1)S(1)}, bf16[8,512,2,128]{3,2,1,0:T(2,128)(2,1)}, u32[]{:S(2)}) copy-start(bf16[8,512,2,128]{3,2,1,0:T(2,128)(2,1)} %param.14) | copy-start | bytes 6291460
  12.2 9.4 %collective-permute-start.3 = (bf16[16,2304]{1,0:T(8,128)(2,1)S(1)}, bf16[16,2304]{1,0:T(8,128)(2,1)S(1)}, u32[]{:S(2)}, u32[]{:S(2)}) collective-permute-start(bf16[16,2304]{1,0:T(8,128)(2,1)S(1)} %get-tuple-element.27), channel_id=1, source_target_pairs={{0,12},{4,8},{8,4},{12,0},{1,13},{5,9},{9,5},{13,1},{2,14},{6,10},... | collective-permute-start | bytes 221192 | tf_op jit(solution)/shard_map/ppermute | solution.py:138
  15.9 6.7 %collective-permute-start.4 = (bf16[16,2304]{1,0:T(8,128)(2,1)S(1)}, bf16[16,2304]{1,0:T(8,128)(2,1)S(1)}, u32[]{:S(2)}, u32[]{:S(2)}) collective-permute-start(bf16[16,2304]{1,0:T(8,128)(2,1)S(1)} %get-tuple-element.28), channel_id=1, source_target_pairs={{0,8},{4,12},{8,0},{12,4},{1,9},{5,13},{9,1},{13,5},{2,10},{6,14},... | collective-permute-start | bytes 221192 | tf_op jit(solution)/shard_map/ppermute | solution.py:138
  15.9 6.7 %collective-permute-start.5 = (bf16[16,2304]{1,0:T(8,128)(2,1)S(1)}, bf16[16,2304]{1,0:T(8,128)(2,1)S(1)}, u32[]{:S(2)}, u32[]{:S(2)}) collective-permute-start(bf16[16,2304]{1,0:T(8,128)(2,1)S(1)} %get-tuple-element.29), channel_id=1, source_target_pairs={{0,4},{4,0},{8,12},{12,8},{1,5},{5,1},{9,13},{13,9},{2,6},{6,2},{1... | collective-permute-start | bytes 221192 | tf_op jit(solution)/shard_map/ppermute | solution.py:138
  16.7 1.6 %copy-start.4 = (bf16[8,512,2,128]{3,2,1,0:T(2,128)(2,1)S(1)}, bf16[8,512,2,128]{3,2,1,0:T(2,128)(2,1)}, u32[]{:S(2)}) copy-start(bf16[8,512,2,128]{3,2,1,0:T(2,128)(2,1)} %param.14) | copy-start | bytes 6291460
  16.7 1.6 %copy-start.6 = (s32[16]{0:T(128)S(1)}, s32[16]{0:T(128)}, u32[]{:S(2)}) copy-start(s32[16]{0:T(128)} %length_ref.3) | copy-start | bytes 196
  17.6 5.0 %collective-permute-start.6 = (bf16[2,4096,128]{2,1,0:T(8,128)(2,1)S(1)}, bf16[2,4096,128]{2,1,0:T(8,128)(2,1)S(1)}, u32[]{:S(2)}, u32[]{:S(2)}) collective-permute-start(bf16[2,4096,128]{2,1,0:T(8,128)(2,1)S(1)} %partner_cache.1.after_ref), channel_id=1, source_target_pairs={{0,1},{1,0},{2,3},{3,2},{4,5},{5,4},{6,7},{7,6},{8,9},{9,8},{10,11... | collective-permute-start | bytes 6291464 | tf_op jit(solution)/shard_map/ppermute | solution.py:138
  24.6 7.8 %collective-permute-start.9 = (bf16[16,2048]{1,0:T(8,128)(2,1)S(1)}, bf16[16,2048]{1,0:T(8,128)(2,1)S(1)}, u32[]{:S(2)}, u32[]{:S(2)}) collective-permute-start(bf16[16,2048]{1,0:T(8,128)(2,1)S(1)} %attend.1.refs_0_.a_ref), channel_id=1, source_target_pairs={{0,12},{4,8},{8,4},{12,0},{1,13},{5,9},{9,5},{13,1},{2,14},{6,10},... | collective-permute-start | bytes 196616 | tf_op jit(solution)/shard_map/ppermute | solution.py:138
  27.6 6.0 %collective-permute-start.8 = (bf16[16,2048]{1,0:T(8,128)(2,1)S(1)}, bf16[16,2048]{1,0:T(8,128)(2,1)S(1)}, u32[]{:S(2)}, u32[]{:S(2)}) collective-permute-start(bf16[16,2048]{1,0:T(8,128)(2,1)S(1)} %attend.1.refs_0_.a_ref), channel_id=1, source_target_pairs={{0,8},{4,12},{8,0},{12,4},{1,9},{5,13},{9,1},{13,5},{2,10},{6,14},... | collective-permute-start | bytes 196616 | tf_op jit(solution)/shard_map/ppermute | solution.py:138
  27.6 6.0 %collective-permute-start.7 = (bf16[16,2048]{1,0:T(8,128)(2,1)S(1)}, bf16[16,2048]{1,0:T(8,128)(2,1)S(1)}, u32[]{:S(2)}, u32[]{:S(2)}) collective-permute-start(bf16[16,2048]{1,0:T(8,128)(2,1)S(1)} %attend.1.refs_0_.a_ref), channel_id=1, source_target_pairs={{0,4},{4,0},{8,12},{12,8},{1,5},{5,1},{9,13},{13,9},{2,6},{6,2},{1... | collective-permute-start | bytes 196616 | tf_op jit(solution)/shard_map/ppermute | solution.py:138
  36.6 1.6 %collective-permute-start.10 = (bf16[32,4096]{1,0:T(8,128)(2,1)S(1)}, bf16[32,4096]{1,0:T(8,128)(2,1)S(1)}, u32[]{:S(2)}, u32[]{:S(2)}) collective-permute-start(bf16[32,4096]{1,0:T(8,128)(2,1)S(1)} %get-tuple-element.36), channel_id=1, source_target_pairs={{0,1},{1,0},{2,3},{3,2},{4,5},{5,4},{6,7},{7,6},{8,9},{9,8},{10,11... | collective-permute-start | bytes 786440 | tf_op jit(solution)/shard_map/ppermute | solution.py:138
  38.3 5.6 %collective-permute-start.11 = (bf16[16,4096]{1,0:T(8,128)(2,1)S(1)}, bf16[16,4096]{1,0:T(8,128)(2,1)S(1)}, u32[]{:S(2)}, u32[]{:S(2)}) collective-permute-start(bf16[16,4096]{1,0:T(8,128)(2,1)S(1)} %get-tuple-element.38), channel_id=1, source_target_pairs={{0,2},{2,0},{1,3},{3,1},{4,6},{6,4},{5,7},{7,5},{8,10},{10,8},{9,1... | collective-permute-start | bytes 393224 | tf_op jit(solution)/shard_map/ppermute | solution.py:138

commit v5 on v3

--- a/solution.py
+++ b/solution.py
@@ -118,9 +118,11 @@
 MIB = 2**20
 STEP = 512
 FIRST_Q, PIECE_Q = 2560, 512
-FIRST_O = 1536
+FIRST_O, SECOND_O = 1024, 256
 ROOM = 42
 ROOM_Q = 38
+ROOM_O = 36
+ORDER = (0, 3, 2, 1)
 
 
 def vmem(mib):
@@ -136,25 +138,23 @@
     return lax.ppermute(array, axis, [(i, i ^ bit) for i in range(size)])
 
 
-def fetch_kernel(weight_ref, *refs, start, axis):
+def fetch_kernel(weight_ref, *refs, start):
     out_ref, mark_ref, sem = refs[-3:]
-    cut = pl.ds(start, out_ref.shape[axis])
-    source = weight_ref.at[cut] if axis == 0 else weight_ref.at[:, cut]
-    copy = pltpu.make_async_copy(source, out_ref, sem)
+    copy = pltpu.make_async_copy(weight_ref.at[pl.ds(start, out_ref.shape[0])], out_ref, sem)
     copy.start()
     mark_ref[...] = jnp.zeros_like(mark_ref)
     copy.wait()
 
 
-def fetch(weight, axis, start, count, *after):
-    shape = (count, weight.shape[1]) if axis == 0 else (weight.shape[0], count)
-    return pl.pallas_call(
-        functools.partial(fetch_kernel, start=start, axis=axis),
+def fetch(weight, start, count, room, *after):
+    shape = (count, weight.shape[1])
+    return pl.pallas_call(
+        functools.partial(fetch_kernel, start=start),
         out_shape=[pltpu.VMEM(shape, weight.dtype), jax.ShapeDtypeStruct((8, 128), jnp.float32)],
         in_specs=[ANY_SPEC] * (1 + len(after)),
         out_specs=[VMEM_SPEC] * 2,
         scratch_shapes=[pltpu.SemaphoreType.DMA],
-        compiler_params=vmem(ROOM),
+        compiler_params=vmem(room),
         cost_estimate=cost(0, shape[0] * shape[1] * 2),
         name="fetch",
     )(weight, *after)
@@ -166,7 +166,7 @@
     for which, ref in enumerate((keys_ref, values_ref)):
         for i in range(seqs):
             slot = i % wide_rows.shape[0]
-            wide_rows[slot] = ref[i].astype(jnp.float32)
+            wide_rows[slot, :rows, :] = ref[i].astype(jnp.float32)
             out_ref[which, i * slots : (i + 1) * slots, :] = wide_rows[
                 slot, pl.ds(which_head, slots, stride=2), :
             ].astype(out_ref.dtype)
@@ -184,7 +184,7 @@
         out_shape=pltpu.VMEM((2, seqs * rows // 2, HD), keys.dtype),
         in_specs=[VMEM_SPEC] * 2 + [ANY_SPEC],
         out_specs=VMEM_SPEC,
-        scratch_shapes=[pltpu.VMEM((4, rows, HD), jnp.float32)],
+        scratch_shapes=[pltpu.VMEM((4, rows + 8, HD), jnp.float32)],
         compiler_params=vmem(4),
         cost_estimate=cost(10**9, 0),
         name="partner_cache",
@@ -196,7 +196,7 @@
     part_ref, own_ref, cos_ref, sin_ref, wide_rows, sem,
 ):
     del after_ref
-    copy = pltpu.make_async_copy(weight_ref.at[:, pl.ds(0, part_ref.shape[1])], part_ref, sem)
+    copy = pltpu.make_async_copy(weight_ref.at[pl.ds(0, part_ref.shape[0])], part_ref, sem)
     copy.start()
     seqs, width = cos_ref.shape
     lane = lax.broadcasted_iota(jnp.int32, (seqs, width), 1)
@@ -213,13 +213,13 @@
     copy.wait()
 
 
-def prepare(lengths, weight, columns, keys, values, after):
+def prepare(lengths, weight, count, keys, values, after):
     seqs, rows, _ = keys.shape
     factors = jax.ShapeDtypeStruct((lengths.shape[0], HD), jnp.float32)
     return pl.pallas_call(
         prepare_kernel,
         out_shape=[
-            pltpu.VMEM((weight.shape[0], columns), weight.dtype),
+            pltpu.VMEM((count, weight.shape[1]), weight.dtype),
             pltpu.VMEM((2, seqs * rows // 2, HD), keys.dtype),
             factors,
             factors,
@@ -227,11 +227,11 @@
         in_specs=[SMEM_SPEC, ANY_SPEC, VMEM_SPEC, VMEM_SPEC, ANY_SPEC],
         out_specs=[VMEM_SPEC] * 4,
         scratch_shapes=[
-            pltpu.VMEM((4, rows, HD), jnp.float32),
+            pltpu.VMEM((4, rows + 8, HD), jnp.float32),
             pltpu.SemaphoreType.DMA,
         ],
         compiler_params=vmem(ROOM - 8),
-        cost_estimate=cost(10**9, weight.shape[0] * columns * 2),
+        cost_estimate=cost(10**11, count * weight.shape[1] * 2),
         name="prepare",
     )(lengths, weight, keys, values, after)
 
@@ -260,21 +260,27 @@
         place = pl.multiple_of((mine ^ m) * rows, rows)
         rows_scratch[pl.ds(place, rows), :] = ref[...]
 
+    rows_scratch[4 * rows :, :] = jnp.zeros((4 * rows, depth), rows_scratch.dtype)
+
     def part(start, block):
         tokens = rows_scratch[:, start : start + block.shape[0]]
-        return jnp.dot(tokens, block, preferred_element_type=jnp.float32)
+        return jnp.dot(tokens, block, preferred_element_type=jnp.float32)[: 4 * rows]
 
     def store(product, start):
-        for place, out in enumerate(outs):
+        for place, out in zip(ORDER, outs):
             out[:, start : start + product.shape[1]] = product[
                 place * rows : (place + 1) * rows
             ].astype(out.dtype)
 
     cuts = [slice(start, start + STEP) for start in range(0, columns, STEP)]
-    for cut in cuts:
-        total[:, cut] = part(0, first_ref[:, cut])
-    side = [ref[:, pl.ds(head, HD)] for ref in (k_ref, v_ref)]
-    store(part(0, jnp.concatenate(side, axis=1)), columns)
+
+    @pl.when(sub < 2)
+    def _():
+        for cut in cuts:
+            total[:, cut] = part(0, first_ref[:, cut])
+        side = [ref[:, pl.ds(head, HD)] for ref in (k_ref, v_ref)]
+        store(part(0, jnp.concatenate(side, axis=1)), columns)
+
     for j, (start, copy) in enumerate(zip(pieces, copies)):
         copy.wait()
         for cut in cuts:
@@ -295,7 +301,7 @@
         in_specs=[VMEM_SPEC] * 7 + [ANY_SPEC] * 2,
         out_specs=[VMEM_SPEC] * 4,
         scratch_shapes=[
-            pltpu.VMEM((4 * rows, depth), jnp.bfloat16),
+            pltpu.VMEM((8 * rows, depth), jnp.bfloat16),
             pltpu.VMEM((late, columns), jnp.bfloat16),
             pltpu.VMEM((4 * rows, columns), jnp.float32),
             pltpu.SemaphoreType.DMA((late // PIECE_Q,)),
@@ -308,10 +314,29 @@
 
 def attend_kernel(
     length_ref, a_ref, b_ref, c_ref, d_ref, cos_ref, sin_ref, own_ref, other_ref, after_ref,
+    weight_ref, out_ref, part_ref, turned, queries, scores, weights, mixed, sem,
+):
+    del after_ref
+    copy = pltpu.make_async_copy(
+        weight_ref.at[pl.ds(FIRST_O, part_ref.shape[0])], part_ref, sem
+    )
+    copy.start()
+    sub = lax.axis_index("sub")
+
+    @pl.when(sub < 2)
+    def _():
+        attend_block(
+            sub, length_ref, a_ref, b_ref, c_ref, d_ref, cos_ref, sin_ref, own_ref, other_ref,
+            out_ref, turned, queries, scores, weights, mixed,
+        )
+
+    copy.wait()
+
+
+def attend_block(
+    sub, length_ref, a_ref, b_ref, c_ref, d_ref, cos_ref, sin_ref, own_ref, other_ref,
     out_ref, turned, queries, scores, weights, mixed,
 ):
-    del after_ref
-    sub = lax.axis_index("sub")
     seqs, columns = a_ref.shape
     half = seqs // 2
     heads = (columns - 2 * HD) // HD
@@ -390,31 +415,35 @@
         ].astype(out_ref.dtype)
 
 
-def attend_here(lengths, parts, cos, sin, own, other, after):
+def attend_here(lengths, parts, cos, sin, own, other, after, weight):
     seqs, columns = parts[0].shape
     heads = columns // HD - 2
     slots = own.shape[1] * 2 // seqs
     rows = seqs * heads
     return pl.pallas_call(
         attend_kernel,
-        out_shape=jax.ShapeDtypeStruct((seqs, heads * HD), jnp.bfloat16),
-        in_specs=[SMEM_SPEC] + [VMEM_SPEC] * 8 + [ANY_SPEC],
-        out_specs=VMEM_SPEC,
+        out_shape=[
+            jax.ShapeDtypeStruct((seqs, heads * HD), jnp.bfloat16),
+            pltpu.VMEM((SECOND_O, weight.shape[1]), weight.dtype),
+        ],
+        in_specs=[SMEM_SPEC] + [VMEM_SPEC] * 8 + [ANY_SPEC] * 2,
+        out_specs=[VMEM_SPEC] * 2,
         scratch_shapes=[
             pltpu.VMEM((rows, HD), jnp.float32),
             pltpu.VMEM((rows, HD), jnp.bfloat16),
             pltpu.VMEM((rows, slots), jnp.float32),
             pltpu.VMEM((rows, slots), jnp.bfloat16),
-            pltpu.VMEM((rows, HD), jnp.float32),
-        ],
-        compiler_params=vmem(8),
+            pltpu.VMEM((rows + heads, HD), jnp.float32),
+            pltpu.SemaphoreType.DMA,
+        ],
+        compiler_params=vmem(ROOM_Q),
         cost_estimate=cost(4 * 10**9, 0),
         name="attend",
-    )(lengths, *parts, cos, sin, own, other, after)
+    )(lengths, *parts, cos, sin, own, other, after, weight)
 
 
 def output_kernel(
-    a_ref, b_ref, c_ref, d_ref, first_ref, second_ref, keep_ref, send_ref, rows_scratch
+    a_ref, b_ref, c_ref, d_ref, first_ref, second_ref, third_ref, keep_ref, send_ref, rows_scratch
 ):
     narrow, sub, wide = lax.axis_index("narrow"), lax.axis_index("sub"), lax.axis_index("wide")
     mine = (narrow * 2 + sub) ^ wide
@@ -423,35 +452,33 @@
         m = mine ^ k
         place = pl.multiple_of(((m & 1) * 2 + (m >> 1)) * rows, rows)
         rows_scratch[pl.ds(place, rows), :] = ref[...]
-    mixed = rows_scratch[...]
-
-    done = 0
-    for ref in (first_ref, second_ref):
-        for start in range(0, ref.shape[1], STEP):
-            product = jnp.dot(
-                mixed, ref[:, start : start + STEP], preferred_element_type=jnp.float32
-            )
-            cut = slice(done + start, done + start + STEP)
-            keep_ref[:, cut] = product[: 2 * rows]
-            send_ref[:, cut] = product[2 * rows :].astype(send_ref.dtype)
-        done += ref.shape[1]
-
-
-def output(blocks, first_part, second_part):
+    rows_scratch[4 * rows :, :] = jnp.zeros_like(rows_scratch[4 * rows :, :])
+    for start in range(0, first_ref.shape[1], STEP):
+        cut = slice(start, start + STEP)
+        product, done = 0.0, 0
+        for ref in (first_ref, second_ref, third_ref):
+            mixed = rows_scratch[:, done : done + ref.shape[0]]
+            product = product + jnp.dot(mixed, ref[:, cut], preferred_element_type=jnp.float32)
+            done += ref.shape[0]
+        keep_ref[:, cut] = product[: 2 * rows]
+        send_ref[:, cut] = product[2 * rows : 4 * rows].astype(send_ref.dtype)
+
+
+def output(blocks, weights):
     rows, depth = blocks[0].shape
-    columns = first_part.shape[1] + second_part.shape[1]
+    columns = weights[0].shape[1]
     return pl.pallas_call(
         output_kernel,
         out_shape=[
             jax.ShapeDtypeStruct((2 * rows, columns), jnp.float32),
             jax.ShapeDtypeStruct((2 * rows, columns), jnp.bfloat16),
         ],
-        in_specs=[VMEM_SPEC] * 6,
+        in_specs=[VMEM_SPEC] * 7,
         out_specs=[VMEM_SPEC] * 2,
-        scratch_shapes=[pltpu.VMEM((4 * rows, depth), jnp.bfloat16)],
-        compiler_params=vmem(6),
+        scratch_shapes=[pltpu.VMEM((8 * rows, depth), jnp.bfloat16)],
+        compiler_params=vmem(8),
         name="output",
-    )(*blocks, first_part, second_part)
+    )(*blocks, *weights)
 
 
 def add_kernel(keep_ref, other_ref, mine_ref, send_ref):
@@ -484,20 +511,23 @@
     values = cache_values.reshape(seqs, slots * kv_heads, HD)
     chip = exchange(tokens, "narrow", 1)
     core = exchange(tokens, "sub", 1)
-    q_first, mark = fetch(q_weight, 0, 0, FIRST_Q)
+    q_first, mark = fetch(q_weight, 0, FIRST_Q, ROOM)
     chip, mark = lax.optimization_barrier((chip, mark))
     both = exchange(chip, "sub", 1)
     parts = project(tokens, core, chip, both, q_first, k_weight, v_weight, q_weight, mark)
-    parts = [parts[0]] + [exchange(parts[k], "wide", k) for k in (1, 2, 3)]
+    parts = [parts[0]] + [exchange(part, "wide", k) for k, part in zip(ORDER[1:], parts[1:])]
     send_cache = partner_cache(keys, values, parts[0])
     other_cache = exchange(send_cache, "sub", 1)
     o_first, own_cache, cosine, sine = prepare(
         lengths, o_weight, FIRST_O, keys, values, send_cache
     )
-    mixed = attend_here(lengths, parts, cosine, sine, own_cache, other_cache, o_first)
-    o_second, _ = fetch(o_weight, 1, FIRST_O, o_weight.shape[1] - FIRST_O, mixed)
+    mixed, o_second = attend_here(
+        lengths, parts, cosine, sine, own_cache, other_cache, o_first, o_weight
+    )
+    start = FIRST_O + SECOND_O
+    o_third, _ = fetch(o_weight, start, o_weight.shape[0] - start, ROOM_O, mixed)
     blocks = [mixed] + [exchange(mixed, "wide", k) for k in (1, 2, 3)]
-    keep, send = output(blocks, o_first, o_second)
+    keep, send = output(blocks, (o_first, o_second, o_third))
     mine, send = add_halves(keep, exchange(send, "sub", 1))
     return (mine + exchange(send, "narrow", 1).astype(jnp.float32)).astype(jnp.bfloat16)
 

time: 46.8 us -> 44.3 us (0.947)
  waiting for transfers between devices: 9.61 us -> 8.38 us
  Pallas kernels: 21.5 us -> 20.3 us
    ppermute x12, waiting for transfers between devices: 9.61 us -> 8.38 us  [exchange(): return lax.ppermute(array, axis, [(i, i ^ bit) for i in range(size)])]
    pallas_call x1, Pallas kernels: 3 us -> 2.39 us  [output(): pl.pallas_call(output_kernel, out_shape=[jax.ShapeDtypeStruct((2 * rows,...]
    pallas_call x4, Pallas kernels: 14 us -> 13.4 us  [the longest x2 7.37 us: fetch(): pl.pallas_call(functools.partial(fetch_kernel, start=start), out_shape=[p...]
  transfers between devices with their start and end apart: 12 -> 12, of which waited for: 4 -> 5; matrix products, arithmetic and copies ran while one was open for 0% -> 0% of each run, Pallas kernels for 26% -> 28%
where the time goes in v5:
time: 44.3 us; the launch traced here: 44 us
  Pallas kernels  20.3 us (46%)
  starting transfers between devices  13.9 us (31%)
  waiting for transfers between devices  8.38 us (19%)
  other arithmetic  0.68 us (2%)
  local copies, waits for them, and re-layouts  0.6 us (1%)
    ppermute x12, starting transfers between devices, exchange(): return lax.ppermute(array, axis, [(i, i ^ bit) for i in range(size)])  13.9 us
    ppermute x12, waiting for transfers between devices, exchange(): return lax.ppermute(array, axis, [(i, i ^ bit) for i in range(size)])  8.38 us
    pallas_call x2, Pallas kernels, fetch(): pl.pallas_call(functools.partial(fetch_kernel, start=start), out_shape=[p...  7.37 us
    pallas_call x1, Pallas kernels, prepare(): pl.pallas_call(prepare_kernel, out_shape=[pltpu.VMEM((count, weight.shape...  3.93 us
    pallas_call x1, Pallas kernels, project(): pl.pallas_call(project_kernel, out_shape=[jax.ShapeDtypeStruct((rows, col...  3.49 us
    pallas_call x1, Pallas kernels, output(): pl.pallas_call(output_kernel, out_shape=[jax.ShapeDtypeStruct((2 * rows,...  2.39 us
    pallas_call x1, Pallas kernels, attend_here(): pl.pallas_call(attend_kernel, out_shape=[jax.ShapeDtypeStruct((seqs, head...  2.14 us
    pallas_call x1, Pallas kernels, partner_cache(): pl.pallas_call(partner_kernel, out_shape=pltpu.VMEM((2, seqs * rows // 2,...  0.92 us
  transfers between devices with their start and end apart: 12, of which 5 were waited for; matrix products, arithmetic and copies ran while one was open for 0% of the time, Pallas kernels for 28%

profile of v5, /device:TPU:0, one launch (start us, length us, event | category | flops | bytes accessed | tf_op | source)
XLA Modules:
  0.0 44.0 jit_solution(16461330026315971045)
XLA Ops:
  0.0 0.0 copy-start.5
  0.0 0.0 copy-start.1
  0.0 0.0 copy-start
  0.0 3.0 %collective-permute-start.1 = (bf16[16,4096]{1,0:T(8,128)(2,1)}, bf16[16,4096]{1,0:T(8,128)(2,1)S(1)}, u32[]{:S(2)}, u32[]{:S(2)}) collective-permute-start(bf16[16,4096]{1,0:T(8,128)(2,1)} %own_ref.1), channel_id=1, source_target_pairs={{0,2},{2,0},{1,3},{3,1},{4,6},{6,4},{5,7},{7,5},{8,10},{10,8},{9,1... | collective-permute-start | bytes 393224 | tf_op jit(solution)/shard_map/ppermute | solution.py:138
  3.0 0.0 collective-permute-start
  3.0 4.0 %fetch.2 = (bf16[2560,2048]{1,0:T(8,128)(2,1)S(1)}, f32[8,128]{1,0:T(8,128)S(1)}) custom-call(bf16[4096,2048]{1,0:T(8,128)(2,1)} %q_ref.1), custom_call_target="tpu_custom_call" | custom-call | bytes 10485760 | tf_op jit(solution)/shard_map/fetch/pallas_call | solution.py:151
  7.0 0.0 collective-permute-done.1.chip_ref
  7.0 0.6 %collective-permute-start.2 = (bf16[16,4096]{1,0:T(8,128)(2,1)S(1)}, bf16[16,4096]{1,0:T(8,128)(2,1)S(1)}, u32[]{:S(2)}, u32[]{:S(2)}) collective-permute-start(bf16[16,4096]{1,0:T(8,128)(2,1)S(1)} %collective-permute-done.1.chip_ref), channel_id=1, source_target_pairs={{0,1},{1,0},{2,3},{3,2},{4,5},{5,4},{6,7},{7,6},{8,9},{9,8},{10,11... | collective-permute-start | bytes 393224 | tf_op jit(solution)/shard_map/ppermute | solution.py:138
  7.6 0.0 collective-permute-done.core_ref
  7.6 1.0 %collective-permute-done.2.both_ref = bf16[16,4096]{1,0:T(8,128)(2,1)S(1)} collective-permute-done((bf16[16,4096]{1,0:T(8,128)(2,1)S(1)}, bf16[16,4096]{1,0:T(8,128)(2,1)S(1)}, u32[]{:S(2)}, u32[]{:S(2)}) %collective-permute-start.2) | collective-permute-done | bytes 131104 | tf_op jit(solution)/shard_map/ppermute | solution.py:138
  8.6 0.0 copy-done.5
  8.6 0.0 copy-done.1
  8.6 0.0 copy-done
  8.6 0.0 copy-start.2
  8.6 0.0 copy-start.3
  8.6 3.5 %project.1 = (bf16[16,2304]{1,0:T(8,128)(2,1)S(1)}, bf16[16,2304]{1,0:T(8,128)(2,1)S(1)}, bf16[16,2304]{1,0:T(8,128)(2,1)S(1)}, bf16[16,2304]{1,0:T(8,128)(2,1)S(1)}) custom-call(bf16[16,4096]{1,0:T(8,128)(2,1)S(1)} %copy-done.5, bf16[16,4096]{1,0:T(8,128)(2,1)S(1)} %collective-permute-done.core_ref, bf16[16,4096]{1,0:T(8,128)(2,1)S(1)} %collective-permute-done.1.chip_ref, ...), custom_call_target="tpu_custom_call" | custom-call | flops 4294967296 | tf_op jit(solution)/shard_map/project/pallas_call | solution.py:298
  12.1 3.7 %collective-permute-start.3 = (bf16[16,2304]{1,0:T(8,128)(2,1)S(1)}, bf16[16,2304]{1,0:T(8,128)(2,1)S(1)}, u32[]{:S(2)}, u32[]{:S(2)}) collective-permute-start(bf16[16,2304]{1,0:T(8,128)(2,1)S(1)} %get-tuple-element.29), channel_id=1, source_target_pairs={{0,12},{4,8},{8,4},{12,0},{1,13},{5,9},{9,5},{13,1},{2,14},{6,10},... | collective-permute-start | bytes 221192 | tf_op jit(solution)/shard_map/ppermute | solution.py:138
  15.8 0.0 collective-permute-start.4
  15.8 0.8 %collective-permute-start.5 = (bf16[16,2304]{1,0:T(8,128)(2,1)S(1)}, bf16[16,2304]{1,0:T(8,128)(2,1)S(1)}, u32[]{:S(2)}, u32[]{:S(2)}) collective-permute-start(bf16[16,2304]{1,0:T(8,128)(2,1)S(1)} %get-tuple-element.31), channel_id=1, source_target_pairs={{0,4},{4,0},{8,12},{12,8},{1,5},{5,1},{9,13},{13,9},{2,6},{6,2},{1... | collective-permute-start | bytes 221192 | tf_op jit(solution)/shard_map/ppermute | solution.py:138
  16.6 0.0 copy-done.2
  16.6 0.0 copy-done.3
  16.6 0.0 copy-start.4
  16.6 0.0 copy-start.6
  16.6 0.9 %partner_cache.1.after_ref = bf16[2,4096,128]{2,1,0:T(8,128)(2,1)S(1)} custom-call(bf16[8,1024,128]{2,1,0:T(8,128)(2,1)S(1)} %bitcast.2, bf16[8,1024,128]{2,1,0:T(8,128)(2,1)S(1)} %bitcast.4, bf16[16,2304]{1,0:T(8,128)(2,1)S(1)} %get-tuple-element.28.after_ref.a_ref), custom_call_target="tpu_custom_call" | custom-call | flops 1000000000 | tf_op jit(solution)/shard_map/partner_cache/pallas_call | solution.py:182
  17.5 0.1 collective-permute-start.6
  17.6 0.6 %copy-done.4 = bf16[8,512,2,128]{3,2,1,0:T(2,128)(2,1)S(1)} copy-done((bf16[8,512,2,128]{3,2,1,0:T(2,128)(2,1)S(1)}, bf16[8,512,2,128]{3,2,1,0:T(2,128)(2,1)}, u32[]{:S(2)}) %copy-start.4) | copy-done | bytes 2097176
  18.2 0.0 copy-done.6
  18.2 3.9 %prepare.1 = (bf16[1024,4096]{1,0:T(8,128)(2,1)S(1)}, bf16[2,4096,128]{2,1,0:T(8,128)(2,1)S(1)}, f32[16,128]{1,0:T(8,128)S(1)}, f32[16,128]{1,0:T(8,128)S(1)}) custom-call(s32[16]{0:T(128)S(1)} %copy-done.6, bf16[2048,4096]{1,0:T(8,128)(2,1)} %weight_ref.7, bf16[8,1024,128]{2,1,0:T(8,128)(2,1)S(1)} %bitcast.3, bf16[8,1024,128]{2,1,0:T(8,128)(2,1)S(1)} %bitcast.5, ...), custom_call_target="tpu_custom_call" | custom-call | flops 99999997952 | bytes 8388608 | tf_op jit(solution)/shard_map/prepare/pallas_call | solution.py:219
  22.1 0.0 collective-permute-done.3.b_ref
  22.1 0.3 collective-permute-done.4.c_ref
  22.5 0.0 collective-permute-done.5.d_ref
  22.5 0.0 collective-permute-done.6.other_ref
  22.5 2.1 %attend.1 = (bf16[16,2048]{1,0:T(8,128)(2,1)S(1)}, bf16[256,4096]{1,0:T(8,128)(2,1)S(1)}) custom-call(s32[16]{0:T(128)S(1)} %copy-done.6, bf16[16,2304]{1,0:T(8,128)(2,1)S(1)} %get-tuple-element.28.after_ref.a_ref, bf16[16,2304]{1,0:T(8,128)(2,1)S(1)} %collective-permute-done.3.b_ref, bf16[16,2304]{1,0:T(8,128)(2,1)S(1)} %collective-permute-done.4.c_ref, ...), custom_call_target="tpu_custom_call" | custom-call | flops 4000000000 | tf_op jit(solution)/shard_map/attend/pallas_call | solution.py:423
  24.6 3.3 %collective-permute-start.9 = (bf16[16,2048]{1,0:T(8,128)(2,1)S(1)}, bf16[16,2048]{1,0:T(8,128)(2,1)S(1)}, u32[]{:S(2)}, u32[]{:S(2)}) collective-permute-start(bf16[16,2048]{1,0:T(8,128)(2,1)S(1)} %get-tuple-element.36.refs_0_.a_ref), channel_id=1, source_target_pairs={{0,12},{4,8},{8,4},{12,0},{1,13},{5,9},{9,5},{13,1},{2,14},{6,10},... | collective-permute-start | bytes 196616 | tf_op jit(solution)/shard_map/ppermute | solution.py:138
  28.0 0.0 collective-permute-start.8
  28.0 1.1 %collective-permute-start.7 = (bf16[16,2048]{1,0:T(8,128)(2,1)S(1)}, bf16[16,2048]{1,0:T(8,128)(2,1)S(1)}, u32[]{:S(2)}, u32[]{:S(2)}) collective-permute-start(bf16[16,2048]{1,0:T(8,128)(2,1)S(1)} %get-tuple-element.36.refs_0_.a_ref), channel_id=1, source_target_pairs={{0,4},{4,0},{8,12},{12,8},{1,5},{5,1},{9,13},{13,9},{2,6},{6,2},{1... | collective-permute-start | bytes 196616 | tf_op jit(solution)/shard_map/ppermute | solution.py:138
  29.1 3.4 %fetch.3 = (bf16[768,4096]{1,0:T(8,128)(2,1)S(1)}, f32[8,128]{1,0:T(8,128)}) custom-call(bf16[2048,4096]{1,0:T(8,128)(2,1)} %weight_ref.7, bf16[16,2048]{1,0:T(8,128)(2,1)S(1)} %get-tuple-element.36.refs_0_.a_ref), custom_call_target="tpu_custom_call" | custom-call | bytes 6291456 | tf_op jit(solution)/shard_map/fetch/pallas_call | solution.py:151
  32.5 0.0 collective-permute-done.9.d_ref
  32.5 1.2 %collective-permute-done.8.c_ref = bf16[16,2048]{1,0:T(8,128)(2,1)S(1)} collective-permute-done((bf16[16,2048]{1,0:T(8,128)(2,1)S(1)}, bf16[16,2048]{1,0:T(8,128)(2,1)S(1)}, u32[]{:S(2)}, u32[]{:S(2)}) %collective-permute-start.8) | collective-permute-done | bytes 65568 | tf_op jit(solution)/shard_map/ppermute | solution.py:138
  33.7 0.0 collective-permute-done.7.b_ref
  33.7 2.4 %output.1 = (f32[32,4096]{1,0:T(8,128)S(1)}, bf16[32,4096]{1,0:T(8,128)(2,1)S(1)}) custom-call(bf16[16,2048]{1,0:T(8,128)(2,1)S(1)} %get-tuple-element.36.refs_0_.a_ref, bf16[16,2048]{1,0:T(8,128)(2,1)S(1)} %collective-permute-done.7.b_ref, bf16[16,2048]{1,0:T(8,128)(2,1)S(1)} %collective-permute-done.8.c_ref, ...), custom_call_target="tpu_custom_call" | custom-call | tf_op jit(solution)/shard_map/output/pallas_call | solution.py:470
  36.1 0.1 collective-permute-start.10
  36.1 1.5 %collective-permute-done.10.other_ref = bf16[32,4096]{1,0:T(8,128)(2,1)S(1)} collective-permute-done((bf16[32,4096]{1,0:T(8,128)(2,1)S(1)}, bf16[32,4096]{1,0:T(8,128)(2,1)S(1)}, u32[]{:S(2)}, u32[]{:S(2)}) %collective-permute-start.10) | collective-permute-done | bytes 262176 | tf_op jit(solution)/shard_map/ppermute | solution.py:138
  37.7 1.3 %collective-permute-start.11 = (bf16[16,4096]{1,0:T(8,128)(2,1)S(1)}, bf16[16,4096]{1,0:T(8,128)(2,1)S(1)}, u32[]{:S(2)}, u32[]{:S(2)}) collective-permute-start(bf16[16,4096]{1,0:T(8,128)(2,1)S(1)} %get-tuple-element.42), channel_id=1, source_target_pairs={{0,2},{2,0},{1,3},{3,1},{4,6},{6,4},{5,7},{7,5},{8,10},{10,8},{9,1... | collective-permute-start | bytes 393224 | tf_op jit(solution)/shard_map/ppermute | solution.py:138
  39.0 4.3 %collective-permute-done.11 = bf16[16,4096]{1,0:T(8,128)(2,1)S(1)} collective-permute-done((bf16[16,4096]{1,0:T(8,128)(2,1)S(1)}, bf16[16,4096]{1,0:T(8,128)(2,1)S(1)}, u32[]{:S(2)}, u32[]{:S(2)}) %collective-permute-start.11) | collective-permute-done | bytes 131104 | tf_op jit(solution)/shard_map/ppermute | solution.py:138
  43.3 0.7 %add_convert_fusion = bf16[16,4096]{1,0:T(8,128)(2,1)} fusion(f32[16,4096]{1,0:T(8,128)S(1)} %get-tuple-element.41, bf16[16,4096]{1,0:T(8,128)(2,1)S(1)} %collective-permute-done.11), kind=kLoop, calls=%fused_computation | loop fusion | flops 196608 | bytes 524288 | tf_op jit(solution)/shard_map/convert_element_type | solution.py:532
  (1 shorter events, 0.0 us)
Async XLA Ops:
  0.0 8.6 %copy-start.5 = (bf16[16,4096]{1,0:T(8,128)(2,1)S(1)}, bf16[16,4096]{1,0:T(8,128)(2,1)}, u32[]{:S(2)}) copy-start(bf16[16,4096]{1,0:T(8,128)(2,1)} %own_ref.1) | copy-start | bytes 393220
  0.0 8.6 %copy-start.1 = (bf16[4096,256]{1,0:T(8,128)(2,1)S(1)}, bf16[4096,256]{1,0:T(8,128)(2,1)}, u32[]{:S(2)}) copy-start(bf16[4096,256]{1,0:T(8,128)(2,1)} %v_ref.1) | copy-start | bytes 6291460
  0.0 8.6 %copy-start = (bf16[4096,256]{1,0:T(8,128)(2,1)S(1)}, bf16[4096,256]{1,0:T(8,128)(2,1)}, u32[]{:S(2)}) copy-start(bf16[4096,256]{1,0:T(8,128)(2,1)} %k_ref.1) | copy-start | bytes 6291460
  0.0 7.0 %collective-permute-start.1 = (bf16[16,4096]{1,0:T(8,128)(2,1)}, bf16[16,4096]{1,0:T(8,128)(2,1)S(1)}, u32[]{:S(2)}, u32[]{:S(2)}) collective-permute-start(bf16[16,4096]{1,0:T(8,128)(2,1)} %own_ref.1), channel_id=1, source_target_pairs={{0,2},{2,0},{1,3},{3,1},{4,6},{6,4},{5,7},{7,5},{8,10},{10,8},{9,1... | collective-permute-start | bytes 393224 | tf_op jit(solution)/shard_map/ppermute | solution.py:138
  3.0 4.6 %collective-permute-start = (bf16[16,4096]{1,0:T(8,128)(2,1)}, bf16[16,4096]{1,0:T(8,128)(2,1)S(1)}, u32[]{:S(2)}, u32[]{:S(2)}) collective-permute-start(bf16[16,4096]{1,0:T(8,128)(2,1)} %own_ref.1), channel_id=1, source_target_pairs={{0,1},{1,0},{2,3},{3,2},{4,5},{5,4},{6,7},{7,6},{8,9},{9,8},{10,11... | collective-permute-start | bytes 393224 | tf_op jit(solution)/shard_map/ppermute | solution.py:138
  7.0 1.6 %collective-permute-start.2 = (bf16[16,4096]{1,0:T(8,128)(2,1)S(1)}, bf16[16,4096]{1,0:T(8,128)(2,1)S(1)}, u32[]{:S(2)}, u32[]{:S(2)}) collective-permute-start(bf16[16,4096]{1,0:T(8,128)(2,1)S(1)} %collective-permute-done.1.chip_ref), channel_id=1, source_target_pairs={{0,1},{1,0},{2,3},{3,2},{4,5},{5,4},{6,7},{7,6},{8,9},{9,8},{10,11... | collective-permute-start | bytes 393224 | tf_op jit(solution)/shard_map/ppermute | solution.py:138
  8.6 8.0 %copy-start.2 = (bf16[8,512,2,128]{3,2,1,0:T(2,128)(2,1)S(1)}, bf16[8,512,2,128]{3,2,1,0:T(2,128)(2,1)}, u32[]{:S(2)}) copy-start(bf16[8,512,2,128]{3,2,1,0:T(2,128)(2,1)} %param.13) | copy-start | bytes 6291460
  8.6 8.0 %copy-start.3 = (bf16[8,512,2,128]{3,2,1,0:T(2,128)(2,1)S(1)}, bf16[8,512,2,128]{3,2,1,0:T(2,128)(2,1)}, u32[]{:S(2)}) copy-start(bf16[8,512,2,128]{3,2,1,0:T(2,128)(2,1)} %param.14) | copy-start | bytes 6291460
  12.1 10.0 %collective-permute-start.3 = (bf16[16,2304]{1,0:T(8,128)(2,1)S(1)}, bf16[16,2304]{1,0:T(8,128)(2,1)S(1)}, u32[]{:S(2)}, u32[]{:S(2)}) collective-permute-start(bf16[16,2304]{1,0:T(8,128)(2,1)S(1)} %get-tuple-element.29), channel_id=1, source_target_pairs={{0,12},{4,8},{8,4},{12,0},{1,13},{5,9},{9,5},{13,1},{2,14},{6,10},... | collective-permute-start | bytes 221192 | tf_op jit(solution)/shard_map/ppermute | solution.py:138
  15.8 6.7 %collective-permute-start.4 = (bf16[16,2304]{1,0:T(8,128)(2,1)S(1)}, bf16[16,2304]{1,0:T(8,128)(2,1)S(1)}, u32[]{:S(2)}, u32[]{:S(2)}) collective-permute-start(bf16[16,2304]{1,0:T(8,128)(2,1)S(1)} %get-tuple-element.30), channel_id=1, source_target_pairs={{0,8},{4,12},{8,0},{12,4},{1,9},{5,13},{9,1},{13,5},{2,10},{6,14},... | collective-permute-start | bytes 221192 | tf_op jit(solution)/shard_map/ppermute | solution.py:138
  15.8 6.7 %collective-permute-start.5 = (bf16[16,2304]{1,0:T(8,128)(2,1)S(1)}, bf16[16,2304]{1,0:T(8,128)(2,1)S(1)}, u32[]{:S(2)}, u32[]{:S(2)}) collective-permute-start(bf16[16,2304]{1,0:T(8,128)(2,1)S(1)} %get-tuple-element.31), channel_id=1, source_target_pairs={{0,4},{4,0},{8,12},{12,8},{1,5},{5,1},{9,13},{13,9},{2,6},{6,2},{1... | collective-permute-start | bytes 221192 | tf_op jit(solution)/shard_map/ppermute | solution.py:138
  16.6 1.6 %copy-start.4 = (bf16[8,512,2,128]{3,2,1,0:T(2,128)(2,1)S(1)}, bf16[8,512,2,128]{3,2,1,0:T(2,128)(2,1)}, u32[]{:S(2)}) copy-start(bf16[8,512,2,128]{3,2,1,0:T(2,128)(2,1)} %param.14) | copy-start | bytes 6291460
  16.6 1.6 %copy-start.6 = (s32[16]{0:T(128)S(1)}, s32[16]{0:T(128)}, u32[]{:S(2)}) copy-start(s32[16]{0:T(128)} %length_ref.3) | copy-start | bytes 196
  17.5 5.0 %collective-permute-start.6 = (bf16[2,4096,128]{2,1,0:T(8,128)(2,1)S(1)}, bf16[2,4096,128]{2,1,0:T(8,128)(2,1)S(1)}, u32[]{:S(2)}, u32[]{:S(2)}) collective-permute-start(bf16[2,4096,128]{2,1,0:T(8,128)(2,1)S(1)} %partner_cache.1.after_ref), channel_id=1, source_target_pairs={{0,1},{1,0},{2,3},{3,2},{4,5},{5,4},{6,7},{7,6},{8,9},{9,8},{10,11... | collective-permute-start | bytes 6291464 | tf_op jit(solution)/shard_map/ppermute | solution.py:138
  24.6 7.8 %collective-permute-start.9 = (bf16[16,2048]{1,0:T(8,128)(2,1)S(1)}, bf16[16,2048]{1,0:T(8,128)(2,1)S(1)}, u32[]{:S(2)}, u32[]{:S(2)}) collective-permute-start(bf16[16,2048]{1,0:T(8,128)(2,1)S(1)} %get-tuple-element.36.refs_0_.a_ref), channel_id=1, source_target_pairs={{0,12},{4,8},{8,4},{12,0},{1,13},{5,9},{9,5},{13,1},{2,14},{6,10},... | collective-permute-start | bytes 196616 | tf_op jit(solution)/shard_map/ppermute | solution.py:138
  28.0 5.7 %collective-permute-start.8 = (bf16[16,2048]{1,0:T(8,128)(2,1)S(1)}, bf16[16,2048]{1,0:T(8,128)(2,1)S(1)}, u32[]{:S(2)}, u32[]{:S(2)}) collective-permute-start(bf16[16,2048]{1,0:T(8,128)(2,1)S(1)} %get-tuple-element.36.refs_0_.a_ref), channel_id=1, source_target_pairs={{0,8},{4,12},{8,0},{12,4},{1,9},{5,13},{9,1},{13,5},{2,10},{6,14},... | collective-permute-start | bytes 196616 | tf_op jit(solution)/shard_map/ppermute | solution.py:138
  28.0 5.7 %collective-permute-start.7 = (bf16[16,2048]{1,0:T(8,128)(2,1)S(1)}, bf16[16,2048]{1,0:T(8,128)(2,1)S(1)}, u32[]{:S(2)}, u32[]{:S(2)}) collective-permute-start(bf16[16,2048]{1,0:T(8,128)(2,1)S(1)} %get-tuple-element.36.refs_0_.a_ref), channel_id=1, source_target_pairs={{0,4},{4,0},{8,12},{12,8},{1,5},{5,1},{9,13},{13,9},{2,6},{6,2},{1... | collective-permute-start | bytes 196616 | tf_op jit(solution)/shard_map/ppermute | solution.py:138
  36.1 1.6 %collective-permute-start.10 = (bf16[32,4096]{1,0:T(8,128)(2,1)S(1)}, bf16[32,4096]{1,0:T(8,128)(2,1)S(1)}, u32[]{:S(2)}, u32[]{:S(2)}) collective-permute-start(bf16[32,4096]{1,0:T(8,128)(2,1)S(1)} %get-tuple-element.40), channel_id=1, source_target_pairs={{0,1},{1,0},{2,3},{3,2},{4,5},{5,4},{6,7},{7,6},{8,9},{9,8},{10,11... | collective-permute-start | bytes 786440 | tf_op jit(solution)/shard_map/ppermute | solution.py:138
  37.7 5.6 %collective-permute-start.11 = (bf16[16,4096]{1,0:T(8,128)(2,1)S(1)}, bf16[16,4096]{1,0:T(8,128)(2,1)S(1)}, u32[]{:S(2)}, u32[]{:S(2)}) collective-permute-start(bf16[16,4096]{1,0:T(8,128)(2,1)S(1)} %get-tuple-element.42), channel_id=1, source_target_pairs={{0,2},{2,0},{1,3},{3,1},{4,6},{6,4},{5,7},{7,5},{8,10},{10,8},{9,1... | collective-permute-start | bytes 393224 | tf_op jit(solution)/shard_map/ppermute | solution.py:138

commit v6 on v5

--- a/solution.py
+++ b/solution.py
@@ -118,7 +118,7 @@
 MIB = 2**20
 STEP = 512
 FIRST_Q, PIECE_Q = 2560, 512
-FIRST_O, SECOND_O = 1024, 256
+FIRST_O, SECOND_O = 768, 256
 ROOM = 42
 ROOM_Q = 38
 ROOM_O = 36
@@ -515,9 +515,12 @@
     chip, mark = lax.optimization_barrier((chip, mark))
     both = exchange(chip, "sub", 1)
     parts = project(tokens, core, chip, both, q_first, k_weight, v_weight, q_weight, mark)
-    parts = [parts[0]] + [exchange(part, "wide", k) for k, part in zip(ORDER[1:], parts[1:])]
     send_cache = partner_cache(keys, values, parts[0])
+    last, send_cache = lax.optimization_barrier((parts[-1], send_cache))
     other_cache = exchange(send_cache, "sub", 1)
+    parts = [parts[0]] + [
+        exchange(part, "wide", k) for k, part in zip(ORDER[1:], [*parts[1:-1], last])
+    ]
     o_first, own_cache, cosine, sine = prepare(
         lengths, o_weight, FIRST_O, keys, values, send_cache
     )

time: 44.3 us -> 44.1 us (level)
  local copies, waits for them, and re-layouts: 0.6 us -> 0.03 us
  waiting for transfers between devices: 8.38 us -> 8.87 us
    pallas_call x2, Pallas kernels: 7.37 us -> 7.97 us  [fetch(): pl.pallas_call(functools.partial(fetch_kernel, start=start), out_shape=[p...]
    pallas_call x1, Pallas kernels: 3.93 us -> 3.34 us  [prepare(): pl.pallas_call(prepare_kernel, out_shape=[pltpu.VMEM((count, weight.shape...]
    unnamed x14, local copies, waits for them, and re-layouts: 0.6 us -> 0.03 us
    ppermute x12, waiting for transfers between devices: 8.38 us -> 8.87 us  [exchange(): return lax.ppermute(array, axis, [(i, i ^ bit) for i in range(size)])]
  transfers between devices with their start and end apart: 12 -> 12, of which waited for: 5 -> 6; matrix products, arithmetic and copies ran while one was open for 0% -> 0% of each run, Pallas kernels for 28% -> 28%
where the time goes in v6:
time: 44.1 us; the launch traced here: 43.9 us
  Pallas kernels  20.3 us (46%)
  starting transfers between devices  13.9 us (32%)
  waiting for transfers between devices  8.87 us (20%)
  other arithmetic  0.68 us (2%)
    ppermute x12, starting transfers between devices, exchange(): return lax.ppermute(array, axis, [(i, i ^ bit) for i in range(size)])  13.9 us
    ppermute x12, waiting for transfers between devices, exchange(): return lax.ppermute(array, axis, [(i, i ^ bit) for i in range(size)])  8.87 us
    pallas_call x2, Pallas kernels, fetch(): pl.pallas_call(functools.partial(fetch_kernel, start=start), out_shape=[p...  7.97 us
    pallas_call x1, Pallas kernels, project(): pl.pallas_call(project_kernel, out_shape=[jax.ShapeDtypeStruct((rows, col...  3.49 us
    pallas_call x1, Pallas kernels, prepare(): pl.pallas_call(prepare_kernel, out_shape=[pltpu.VMEM((count, weight.shape...  3.34 us
    pallas_call x1, Pallas kernels, output(): pl.pallas_call(output_kernel, out_shape=[jax.ShapeDtypeStruct((2 * rows,...  2.38 us
    pallas_call x1, Pallas kernels, attend_here(): pl.pallas_call(attend_kernel, out_shape=[jax.ShapeDtypeStruct((seqs, head...  2.14 us
    pallas_call x1, Pallas kernels, partner_cache(): pl.pallas_call(partner_kernel, out_shape=pltpu.VMEM((2, seqs * rows // 2,...  0.92 us
  transfers between devices with their start and end apart: 12, of which 6 were waited for; matrix products, arithmetic and copies ran while one was open for 0% of the time, Pallas kernels for 28%

profile of v6, /device:TPU:0, one launch (start us, length us, event | category | flops | bytes accessed | tf_op | source)
XLA Modules:
  0.0 43.9 jit_solution(3176520525266120601)
XLA Ops:
  0.0 0.0 copy-start.5
  0.0 0.0 copy-start.1
  0.0 0.0 copy-start
  0.0 3.0 %collective-permute-start.1 = (bf16[16,4096]{1,0:T(8,128)(2,1)}, bf16[16,4096]{1,0:T(8,128)(2,1)S(1)}, u32[]{:S(2)}, u32[]{:S(2)}) collective-permute-start(bf16[16,4096]{1,0:T(8,128)(2,1)} %own_ref.1), channel_id=1, source_target_pairs={{0,2},{2,0},{1,3},{3,1},{4,6},{6,4},{5,7},{7,5},{8,10},{10,8},{9,1... | collective-permute-start | bytes 393224 | tf_op jit(solution)/shard_map/ppermute | solution.py:138
  3.0 0.0 collective-permute-start
  3.0 4.0 %fetch.2 = (bf16[2560,2048]{1,0:T(8,128)(2,1)S(1)}, f32[8,128]{1,0:T(8,128)S(1)}) custom-call(bf16[4096,2048]{1,0:T(8,128)(2,1)} %q_ref.1), custom_call_target="tpu_custom_call" | custom-call | bytes 10485760 | tf_op jit(solution)/shard_map/fetch/pallas_call | solution.py:151
  7.0 0.0 collective-permute-done.1.chip_ref
  7.0 0.6 %collective-permute-start.2 = (bf16[16,4096]{1,0:T(8,128)(2,1)S(1)}, bf16[16,4096]{1,0:T(8,128)(2,1)S(1)}, u32[]{:S(2)}, u32[]{:S(2)}) collective-permute-start(bf16[16,4096]{1,0:T(8,128)(2,1)S(1)} %collective-permute-done.1.chip_ref), channel_id=1, source_target_pairs={{0,1},{1,0},{2,3},{3,2},{4,5},{5,4},{6,7},{7,6},{8,9},{9,8},{10,11... | collective-permute-start | bytes 393224 | tf_op jit(solution)/shard_map/ppermute | solution.py:138
  7.6 0.0 collective-permute-done.core_ref
  7.6 1.0 %collective-permute-done.2.both_ref = bf16[16,4096]{1,0:T(8,128)(2,1)S(1)} collective-permute-done((bf16[16,4096]{1,0:T(8,128)(2,1)S(1)}, bf16[16,4096]{1,0:T(8,128)(2,1)S(1)}, u32[]{:S(2)}, u32[]{:S(2)}) %collective-permute-start.2) | collective-permute-done | bytes 131104 | tf_op jit(solution)/shard_map/ppermute | solution.py:138
  8.6 0.0 copy-done.5
  8.6 0.0 copy-done.1
  8.6 0.0 copy-done
  8.6 0.0 copy-start.2
  8.6 0.0 copy-start.3
  8.6 3.5 %project.1 = (bf16[16,2304]{1,0:T(8,128)(2,1)S(1)}, bf16[16,2304]{1,0:T(8,128)(2,1)S(1)}, bf16[16,2304]{1,0:T(8,128)(2,1)S(1)}, bf16[16,2304]{1,0:T(8,128)(2,1)S(1)}) custom-call(bf16[16,4096]{1,0:T(8,128)(2,1)S(1)} %copy-done.5, bf16[16,4096]{1,0:T(8,128)(2,1)S(1)} %collective-permute-done.core_ref, bf16[16,4096]{1,0:T(8,128)(2,1)S(1)} %collective-permute-done.1.chip_ref, ...), custom_call_target="tpu_custom_call" | custom-call | flops 4294967296 | tf_op jit(solution)/shard_map/project/pallas_call | solution.py:298
  12.1 3.7 %collective-permute-start.3 = (bf16[16,2304]{1,0:T(8,128)(2,1)S(1)}, bf16[16,2304]{1,0:T(8,128)(2,1)S(1)}, u32[]{:S(2)}, u32[]{:S(2)}) collective-permute-start(bf16[16,2304]{1,0:T(8,128)(2,1)S(1)} %get-tuple-element.31), channel_id=1, source_target_pairs={{0,12},{4,8},{8,4},{12,0},{1,13},{5,9},{9,5},{13,1},{2,14},{6,10},... | collective-permute-start | bytes 221192 | tf_op jit(solution)/shard_map/ppermute | solution.py:138
  15.8 0.0 collective-permute-start.4
  15.8 0.0 copy-done.2
  15.8 0.0 copy-done.3
  15.8 0.0 copy-start.4
  15.8 0.0 copy-start.6
  15.8 0.9 %partner_cache.1.after_ref = bf16[2,4096,128]{2,1,0:T(8,128)(2,1)S(1)} custom-call(bf16[8,1024,128]{2,1,0:T(8,128)(2,1)S(1)} %bitcast.2, bf16[8,1024,128]{2,1,0:T(8,128)(2,1)S(1)} %bitcast.4, bf16[16,2304]{1,0:T(8,128)(2,1)S(1)} %get-tuple-element.30.after_ref.a_ref), custom_call_target="tpu_custom_call" | custom-call | flops 1000000000 | tf_op jit(solution)/shard_map/partner_cache/pallas_call | solution.py:182
  16.7 0.8 %collective-permute-start.5 = (bf16[16,2304]{1,0:T(8,128)(2,1)S(1)}, bf16[16,2304]{1,0:T(8,128)(2,1)S(1)}, u32[]{:S(2)}, u32[]{:S(2)}) collective-permute-start(bf16[16,2304]{1,0:T(8,128)(2,1)S(1)} %get-tuple-element.34), channel_id=1, source_target_pairs={{0,4},{4,0},{8,12},{12,8},{1,5},{5,1},{9,13},{13,9},{2,6},{6,2},{1... | collective-permute-start | bytes 221192 | tf_op jit(solution)/shard_map/ppermute | solution.py:138
  17.6 0.0 collective-permute-start.6
  17.6 0.0 copy-done.4
  17.6 0.0 copy-done.6
  17.6 3.3 %prepare.1 = (bf16[768,4096]{1,0:T(8,128)(2,1)S(1)}, bf16[2,4096,128]{2,1,0:T(8,128)(2,1)S(1)}, f32[16,128]{1,0:T(8,128)S(1)}, f32[16,128]{1,0:T(8,128)S(1)}) custom-call(s32[16]{0:T(128)S(1)} %copy-done.6, bf16[2048,4096]{1,0:T(8,128)(2,1)} %weight_ref.7, bf16[8,1024,128]{2,1,0:T(8,128)(2,1)S(1)} %bitcast.3, bf16[8,1024,128]{2,1,0:T(8,128)(2,1)S(1)} %bitcast.5, ...), custom_call_target="tpu_custom_call" | custom-call | flops 99999997952 | bytes 6291456 | tf_op jit(solution)/shard_map/prepare/pallas_call | solution.py:219
  20.9 0.0 collective-permute-done.3.b_ref
  20.9 1.6 %collective-permute-done.4.c_ref = bf16[16,2304]{1,0:T(8,128)(2,1)S(1)} collective-permute-done((bf16[16,2304]{1,0:T(8,128)(2,1)S(1)}, bf16[16,2304]{1,0:T(8,128)(2,1)S(1)}, u32[]{:S(2)}, u32[]{:S(2)}) %collective-permute-start.4) | collective-permute-done | bytes 73760 | tf_op jit(solution)/shard_map/ppermute | solution.py:138
  22.6 0.1 collective-permute-done.5.d_ref
  22.7 0.0 collective-permute-done.6.other_ref
  22.7 2.1 %attend.1 = (bf16[16,2048]{1,0:T(8,128)(2,1)S(1)}, bf16[256,4096]{1,0:T(8,128)(2,1)S(1)}) custom-call(s32[16]{0:T(128)S(1)} %copy-done.6, bf16[16,2304]{1,0:T(8,128)(2,1)S(1)} %get-tuple-element.30.after_ref.a_ref, bf16[16,2304]{1,0:T(8,128)(2,1)S(1)} %collective-permute-done.3.b_ref, bf16[16,2304]{1,0:T(8,128)(2,1)S(1)} %collective-permute-done.4.c_ref, ...), custom_call_target="tpu_custom_call" | custom-call | flops 4000000000 | tf_op jit(solution)/shard_map/attend/pallas_call | solution.py:423
  24.9 2.7 %collective-permute-start.9 = (bf16[16,2048]{1,0:T(8,128)(2,1)S(1)}, bf16[16,2048]{1,0:T(8,128)(2,1)S(1)}, u32[]{:S(2)}, u32[]{:S(2)}) collective-permute-start(bf16[16,2048]{1,0:T(8,128)(2,1)S(1)} %get-tuple-element.40.refs_0_.a_ref), channel_id=1, source_target_pairs={{0,12},{4,8},{8,4},{12,0},{1,13},{5,9},{9,5},{13,1},{2,14},{6,10},... | collective-permute-start | bytes 196616 | tf_op jit(solution)/shard_map/ppermute | solution.py:138
  27.6 0.0 collective-permute-start.8
  27.6 1.8 %collective-permute-start.7 = (bf16[16,2048]{1,0:T(8,128)(2,1)S(1)}, bf16[16,2048]{1,0:T(8,128)(2,1)S(1)}, u32[]{:S(2)}, u32[]{:S(2)}) collective-permute-start(bf16[16,2048]{1,0:T(8,128)(2,1)S(1)} %get-tuple-element.40.refs_0_.a_ref), channel_id=1, source_target_pairs={{0,4},{4,0},{8,12},{12,8},{1,5},{5,1},{9,13},{13,9},{2,6},{6,2},{1... | collective-permute-start | bytes 196616 | tf_op jit(solution)/shard_map/ppermute | solution.py:138
  29.3 4.0 %fetch.3 = (bf16[1024,4096]{1,0:T(8,128)(2,1)S(1)}, f32[8,128]{1,0:T(8,128)}) custom-call(bf16[2048,4096]{1,0:T(8,128)(2,1)} %weight_ref.7, bf16[16,2048]{1,0:T(8,128)(2,1)S(1)} %get-tuple-element.40.refs_0_.a_ref), custom_call_target="tpu_custom_call" | custom-call | bytes 8388608 | tf_op jit(solution)/shard_map/fetch/pallas_call | solution.py:151
  33.3 0.0 collective-permute-done.9.d_ref
  33.3 0.2 collective-permute-done.8.c_ref
  33.6 0.0 collective-permute-done.7.b_ref
  33.6 2.4 %output.1 = (f32[32,4096]{1,0:T(8,128)S(1)}, bf16[32,4096]{1,0:T(8,128)(2,1)S(1)}) custom-call(bf16[16,2048]{1,0:T(8,128)(2,1)S(1)} %get-tuple-element.40.refs_0_.a_ref, bf16[16,2048]{1,0:T(8,128)(2,1)S(1)} %collective-permute-done.7.b_ref, bf16[16,2048]{1,0:T(8,128)(2,1)S(1)} %collective-permute-done.8.c_ref, ...), custom_call_target="tpu_custom_call" | custom-call | tf_op jit(solution)/shard_map/output/pallas_call | solution.py:470
  35.9 0.1 collective-permute-start.10
  36.0 1.5 %collective-permute-done.10.other_ref = bf16[32,4096]{1,0:T(8,128)(2,1)S(1)} collective-permute-done((bf16[32,4096]{1,0:T(8,128)(2,1)S(1)}, bf16[32,4096]{1,0:T(8,128)(2,1)S(1)}, u32[]{:S(2)}, u32[]{:S(2)}) %collective-permute-start.10) | collective-permute-done | bytes 262176 | tf_op jit(solution)/shard_map/ppermute | solution.py:138
  37.6 1.3 %collective-permute-start.11 = (bf16[16,4096]{1,0:T(8,128)(2,1)S(1)}, bf16[16,4096]{1,0:T(8,128)(2,1)S(1)}, u32[]{:S(2)}, u32[]{:S(2)}) collective-permute-start(bf16[16,4096]{1,0:T(8,128)(2,1)S(1)} %get-tuple-element.46), channel_id=1, source_target_pairs={{0,2},{2,0},{1,3},{3,1},{4,6},{6,4},{5,7},{7,5},{8,10},{10,8},{9,1... | collective-permute-start | bytes 393224 | tf_op jit(solution)/shard_map/ppermute | solution.py:138
  38.9 4.3 %collective-permute-done.11 = bf16[16,4096]{1,0:T(8,128)(2,1)S(1)} collective-permute-done((bf16[16,4096]{1,0:T(8,128)(2,1)S(1)}, bf16[16,4096]{1,0:T(8,128)(2,1)S(1)}, u32[]{:S(2)}, u32[]{:S(2)}) %collective-permute-start.11) | collective-permute-done | bytes 131104 | tf_op jit(solution)/shard_map/ppermute | solution.py:138
  43.2 0.7 %add_convert_fusion = bf16[16,4096]{1,0:T(8,128)(2,1)} fusion(f32[16,4096]{1,0:T(8,128)S(1)} %get-tuple-element.45, bf16[16,4096]{1,0:T(8,128)(2,1)S(1)} %collective-permute-done.11), kind=kLoop, calls=%fused_computation | loop fusion | flops 196608 | bytes 524288 | tf_op jit(solution)/shard_map/convert_element_type | solution.py:535
  (1 shorter events, 0.0 us)
Async XLA Ops:
  0.0 8.6 %copy-start.5 = (bf16[16,4096]{1,0:T(8,128)(2,1)S(1)}, bf16[16,4096]{1,0:T(8,128)(2,1)}, u32[]{:S(2)}) copy-start(bf16[16,4096]{1,0:T(8,128)(2,1)} %own_ref.1) | copy-start | bytes 393220
  0.0 8.6 %copy-start.1 = (bf16[4096,256]{1,0:T(8,128)(2,1)S(1)}, bf16[4096,256]{1,0:T(8,128)(2,1)}, u32[]{:S(2)}) copy-start(bf16[4096,256]{1,0:T(8,128)(2,1)} %v_ref.1) | copy-start | bytes 6291460
  0.0 8.6 %copy-start = (bf16[4096,256]{1,0:T(8,128)(2,1)S(1)}, bf16[4096,256]{1,0:T(8,128)(2,1)}, u32[]{:S(2)}) copy-start(bf16[4096,256]{1,0:T(8,128)(2,1)} %k_ref.1) | copy-start | bytes 6291460
  0.0 7.0 %collective-permute-start.1 = (bf16[16,4096]{1,0:T(8,128)(2,1)}, bf16[16,4096]{1,0:T(8,128)(2,1)S(1)}, u32[]{:S(2)}, u32[]{:S(2)}) collective-permute-start(bf16[16,4096]{1,0:T(8,128)(2,1)} %own_ref.1), channel_id=1, source_target_pairs={{0,2},{2,0},{1,3},{3,1},{4,6},{6,4},{5,7},{7,5},{8,10},{10,8},{9,1... | collective-permute-start | bytes 393224 | tf_op jit(solution)/shard_map/ppermute | solution.py:138
  3.0 4.6 %collective-permute-start = (bf16[16,4096]{1,0:T(8,128)(2,1)}, bf16[16,4096]{1,0:T(8,128)(2,1)S(1)}, u32[]{:S(2)}, u32[]{:S(2)}) collective-permute-start(bf16[16,4096]{1,0:T(8,128)(2,1)} %own_ref.1), channel_id=1, source_target_pairs={{0,1},{1,0},{2,3},{3,2},{4,5},{5,4},{6,7},{7,6},{8,9},{9,8},{10,11... | collective-permute-start | bytes 393224 | tf_op jit(solution)/shard_map/ppermute | solution.py:138
  7.0 1.6 %collective-permute-start.2 = (bf16[16,4096]{1,0:T(8,128)(2,1)S(1)}, bf16[16,4096]{1,0:T(8,128)(2,1)S(1)}, u32[]{:S(2)}, u32[]{:S(2)}) collective-permute-start(bf16[16,4096]{1,0:T(8,128)(2,1)S(1)} %collective-permute-done.1.chip_ref), channel_id=1, source_target_pairs={{0,1},{1,0},{2,3},{3,2},{4,5},{5,4},{6,7},{7,6},{8,9},{9,8},{10,11... | collective-permute-start | bytes 393224 | tf_op jit(solution)/shard_map/ppermute | solution.py:138
  8.6 7.2 %copy-start.2 = (bf16[8,512,2,128]{3,2,1,0:T(2,128)(2,1)S(1)}, bf16[8,512,2,128]{3,2,1,0:T(2,128)(2,1)}, u32[]{:S(2)}) copy-start(bf16[8,512,2,128]{3,2,1,0:T(2,128)(2,1)} %param.13) | copy-start | bytes 6291460
  8.6 7.2 %copy-start.3 = (bf16[8,512,2,128]{3,2,1,0:T(2,128)(2,1)S(1)}, bf16[8,512,2,128]{3,2,1,0:T(2,128)(2,1)}, u32[]{:S(2)}) copy-start(bf16[8,512,2,128]{3,2,1,0:T(2,128)(2,1)} %param.14) | copy-start | bytes 6291460
  12.1 8.8 %collective-permute-start.3 = (bf16[16,2304]{1,0:T(8,128)(2,1)S(1)}, bf16[16,2304]{1,0:T(8,128)(2,1)S(1)}, u32[]{:S(2)}, u32[]{:S(2)}) collective-permute-start(bf16[16,2304]{1,0:T(8,128)(2,1)S(1)} %get-tuple-element.31), channel_id=1, source_target_pairs={{0,12},{4,8},{8,4},{12,0},{1,13},{5,9},{9,5},{13,1},{2,14},{6,10},... | collective-permute-start | bytes 221192 | tf_op jit(solution)/shard_map/ppermute | solution.py:138
  15.8 6.8 %collective-permute-start.4 = (bf16[16,2304]{1,0:T(8,128)(2,1)S(1)}, bf16[16,2304]{1,0:T(8,128)(2,1)S(1)}, u32[]{:S(2)}, u32[]{:S(2)}) collective-permute-start(bf16[16,2304]{1,0:T(8,128)(2,1)S(1)} %get-tuple-element.32), channel_id=1, source_target_pairs={{0,8},{4,12},{8,0},{12,4},{1,9},{5,13},{9,1},{13,5},{2,10},{6,14},... | collective-permute-start | bytes 221192 | tf_op jit(solution)/shard_map/ppermute | solution.py:138
  15.8 1.8 %copy-start.4 = (bf16[8,512,2,128]{3,2,1,0:T(2,128)(2,1)S(1)}, bf16[8,512,2,128]{3,2,1,0:T(2,128)(2,1)}, u32[]{:S(2)}) copy-start(bf16[8,512,2,128]{3,2,1,0:T(2,128)(2,1)} %param.14) | copy-start | bytes 6291460
  15.8 1.8 %copy-start.6 = (s32[16]{0:T(128)S(1)}, s32[16]{0:T(128)}, u32[]{:S(2)}) copy-start(s32[16]{0:T(128)} %length_ref.3) | copy-start | bytes 196
  16.7 6.0 %collective-permute-start.5 = (bf16[16,2304]{1,0:T(8,128)(2,1)S(1)}, bf16[16,2304]{1,0:T(8,128)(2,1)S(1)}, u32[]{:S(2)}, u32[]{:S(2)}) collective-permute-start(bf16[16,2304]{1,0:T(8,128)(2,1)S(1)} %get-tuple-element.34), channel_id=1, source_target_pairs={{0,4},{4,0},{8,12},{12,8},{1,5},{5,1},{9,13},{13,9},{2,6},{6,2},{1... | collective-permute-start | bytes 221192 | tf_op jit(solution)/shard_map/ppermute | solution.py:138
  17.6 5.1 %collective-permute-start.6 = (bf16[2,4096,128]{2,1,0:T(8,128)(2,1)S(1)}, bf16[2,4096,128]{2,1,0:T(8,128)(2,1)S(1)}, u32[]{:S(2)}, u32[]{:S(2)}) collective-permute-start(bf16[2,4096,128]{2,1,0:T(8,128)(2,1)S(1)} %partner_cache.1.after_ref), channel_id=1, source_target_pairs={{0,1},{1,0},{2,3},{3,2},{4,5},{5,4},{6,7},{7,6},{8,9},{9,8},{10,11... | collective-permute-start | bytes 6291464 | tf_op jit(solution)/shard_map/ppermute | solution.py:138
  24.9 8.4 %collective-permute-start.9 = (bf16[16,2048]{1,0:T(8,128)(2,1)S(1)}, bf16[16,2048]{1,0:T(8,128)(2,1)S(1)}, u32[]{:S(2)}, u32[]{:S(2)}) collective-permute-start(bf16[16,2048]{1,0:T(8,128)(2,1)S(1)} %get-tuple-element.40.refs_0_.a_ref), channel_id=1, source_target_pairs={{0,12},{4,8},{8,4},{12,0},{1,13},{5,9},{9,5},{13,1},{2,14},{6,10},... | collective-permute-start | bytes 196616 | tf_op jit(solution)/shard_map/ppermute | solution.py:138
  27.6 6.0 %collective-permute-start.8 = (bf16[16,2048]{1,0:T(8,128)(2,1)S(1)}, bf16[16,2048]{1,0:T(8,128)(2,1)S(1)}, u32[]{:S(2)}, u32[]{:S(2)}) collective-permute-start(bf16[16,2048]{1,0:T(8,128)(2,1)S(1)} %get-tuple-element.40.refs_0_.a_ref), channel_id=1, source_target_pairs={{0,8},{4,12},{8,0},{12,4},{1,9},{5,13},{9,1},{13,5},{2,10},{6,14},... | collective-permute-start | bytes 196616 | tf_op jit(solution)/shard_map/ppermute | solution.py:138
  27.6 6.0 %collective-permute-start.7 = (bf16[16,2048]{1,0:T(8,128)(2,1)S(1)}, bf16[16,2048]{1,0:T(8,128)(2,1)S(1)}, u32[]{:S(2)}, u32[]{:S(2)}) collective-permute-start(bf16[16,2048]{1,0:T(8,128)(2,1)S(1)} %get-tuple-element.40.refs_0_.a_ref), channel_id=1, source_target_pairs={{0,4},{4,0},{8,12},{12,8},{1,5},{5,1},{9,13},{13,9},{2,6},{6,2},{1... | collective-permute-start | bytes 196616 | tf_op jit(solution)/shard_map/ppermute | solution.py:138
  35.9 1.6 %collective-permute-start.10 = (bf16[32,4096]{1,0:T(8,128)(2,1)S(1)}, bf16[32,4096]{1,0:T(8,128)(2,1)S(1)}, u32[]{:S(2)}, u32[]{:S(2)}) collective-permute-start(bf16[32,4096]{1,0:T(8,128)(2,1)S(1)} %get-tuple-element.44), channel_id=1, source_target_pairs={{0,1},{1,0},{2,3},{3,2},{4,5},{5,4},{6,7},{7,6},{8,9},{9,8},{10,11... | collective-permute-start | bytes 786440 | tf_op jit(solution)/shard_map/ppermute | solution.py:138
  37.6 5.6 %collective-permute-start.11 = (bf16[16,4096]{1,0:T(8,128)(2,1)S(1)}, bf16[16,4096]{1,0:T(8,128)(2,1)S(1)}, u32[]{:S(2)}, u32[]{:S(2)}) collective-permute-start(bf16[16,4096]{1,0:T(8,128)(2,1)S(1)} %get-tuple-element.46), channel_id=1, source_target_pairs={{0,2},{2,0},{1,3},{3,1},{4,6},{6,4},{5,7},{7,5},{8,10},{10,8},{9,1... | collective-permute-start | bytes 393224 | tf_op jit(solution)/shard_map/ppermute | solution.py:138
